TPU v7x, 32 devices: a whole 2x2x4 slice. The times are simulated.
32 devices in a mesh: ctx: 8 (over z, y), tp: 4 (over x, core).
Axes of the slice: x: 2, y: 2, z: 4, core: 2. Of those that a mesh axis runs over, the one named last changes fastest.
Arguments:
- hidden: bfloat16 [2, 2, 384, 2048], P(None, None, 'ctx'), may hold values from -6 to 6
- cotangent: bfloat16 [2, 2, 384, 2048], P(None, None, 'ctx'), may hold values from -6 to 6
- lengths: int32 [2], replicated, may hold values from 192 to 768, as said below
- norm_gains: bfloat16 [2, 2, 2048], P(None, None, 'ctx'), may hold values from 0.5 to 1.5
- mix_weight: bfloat16 [2, 2048, 7168], P(None, 'ctx', 'tp'), may hold values from -0.125 to 0.125
- share_weight: bfloat16 [2, 2048, 1072], P(None, 'ctx'), may hold values from -0.125 to 0.125
- chan_params: float32 [2, 6, 3072], P(None, None, 'tp'), may hold values from -1.5 to 1.5
- shared_conv: float32 [2, 5, 512], replicated, may hold values from -1.5 to 1.5
- head_params: float32 [2, 3, 48], P(None, None, 'tp'), may hold values from -15 to 3
- out_weight: bfloat16 [2, 4096, 2048], P(None, 'tp', 'ctx'), may hold values from -0.15625 to 0.15625
- up_weight: bfloat16 [2, 2048, 8192], P(None, 'ctx', 'tp'), may hold values from -0.125 to 0.125
- down_weight: bfloat16 [2, 4096, 2048], P(None, 'tp', 'ctx'), may hold values from -0.1875 to 0.1875
Outputs:
- activations: float32 [2, 2, 384, 2048], P(None, None, 'ctx')
- input_grad: float32 [2, 2, 384, 2048], P(None, None, 'ctx')
- grad_norm_gains: float32 [2, 2, 2048], P(None, None, 'ctx')
- grad_mix_weight: float32 [2, 2048, 7168], P(None, 'ctx', 'tp')
- grad_share_weight: float32 [2, 2048, 1072], P(None, 'ctx')
- grad_chan_params: float32 [2, 6, 3072], P(None, None, 'tp')
- grad_shared_conv: float32 [2, 5, 512], replicated
- grad_head_params: float32 [2, 3, 48], P(None, None, 'tp')
- grad_out_weight: float32 [2, 4096, 2048], P(None, 'tp', 'ctx')
- grad_up_weight: float32 [2, 2048, 8192], P(None, 'ctx', 'tp')
- grad_down_weight: float32 [2, 4096, 2048], P(None, 'tp', 'ctx')
Inputs may be any that keep to these rules, and one draw needn't show every extreme that they name: `lengths`: in every draw one slot has length 768.
All inputs are finite; a program needn't handle non-finite values.
Results may differ from a plain program's by a relative error of at most 0.03.
Values may be sent and summed in bfloat16 or wider, within the bound.
No kernel may reach another device: no remote copies, remote signals or barrier semaphores. Data moves between devices by JAX's collectives and lax.ppermute only.
A program may use at most 448 MiB of HBM per device.

v0:
```python
import jax
import jax.numpy as jnp
from jax import lax
from jax.sharding import PartitionSpec as P

D = 2048
MH = 48
P_SIZE = 64
N = 256
CONV = 4
AH = 8
KVH = 2
HD = 128
FF = 4096
LAYERS = 2


eps_norm = 1e-05
rope_base = 100000000000.0
highest = lax.Precision.HIGHEST


def shortened(x):
    return jax.tree.map(lambda a: a.astype(jnp.bfloat16) if a.dtype == jnp.float32 else a, x)


def shifted(block, axis, distance):
    devices = range(lax.axis_size(axis))
    route = [(i - distance, i) for i in devices if i - distance in devices]
    return lax.ppermute(block, axis, route)


def extended(x, sides, width):
    for axis, dim in sides:
        peers, length = (lax.axis_size(axis), x.shape[dim])
        up = [(i, (i + 1) % peers) for i in range(peers - 1)]
        down = [(j, i) for i, j in up]
        last = lax.slice_in_dim(x, length - width, length, axis=dim)
        leading = lax.slice_in_dim(x, 0, width, axis=dim)
        before = lax.ppermute(last, axis, up)
        after = lax.ppermute(leading, axis, down)
        x = jnp.concatenate([before, x, after], axis=dim)
    return x


def matmul(left_op, right_op):
    return jnp.dot(left_op, right_op, preferred_element_type=jnp.float32)


def matmul_tn(left_op, right_op):
    return lax.dot_general(
        left_op, right_op, (((0,), (0,)), ((), ())), preferred_element_type=jnp.float32
    )


def matmul_nt(left_op, right_op):
    return lax.dot_general(
        left_op, right_op, (((1,), (1,)), ((), ())), preferred_element_type=jnp.float32
    )


def silu_grad(inputs):
    sigmoid = jax.nn.sigmoid(inputs)
    return sigmoid * (1.0 + inputs * (1.0 - sigmoid))


def rotate(values, positions):
    half_dim = HD // 2
    inverse = jnp.exp(-jnp.log(rope_base) * (2.0 * jnp.arange(half_dim, dtype=jnp.float32) / HD))
    angles = positions.astype(jnp.float32)[..., None] * inverse
    cosine = jnp.cos(angles)
    sine_vals = jnp.sin(angles)
    front_half = values[..., :half_dim]
    back_half = values[..., half_dim:]
    return jnp.concatenate(
        [front_half * cosine - back_half * sine_vals, back_half * cosine + front_half * sine_vals],
        axis=-1,
    )


def norm_piece(stream, gain_row):
    factor = lax.rsqrt(jnp.mean(stream * stream, axis=-1, keepdims=True) + eps_norm)
    return stream * factor * gain_row


def input_piece(pre_conv, prev_rows, conv_taps, conv_bias, dt_raw, params):
    block_len = pre_conv.shape[2]
    heads_local = params.shape[1]
    width_ssm = heads_local * P_SIZE
    block_count = pre_conv.shape[0] * 2
    joined = jnp.concatenate([prev_rows, pre_conv], axis=2)
    running = conv_bias + conv_taps[0] * joined[:, :, 0:block_len]
    for offset in range(1, CONV):
        running = running + conv_taps[offset] * joined[:, :, offset : offset + block_len]
    activation = jax.nn.silu(running)
    x_conv = activation[..., :width_ssm].reshape(block_count, block_len, heads_local, P_SIZE)
    b_conv = activation[..., width_ssm : width_ssm + N].reshape(block_count, block_len, N)
    c_conv = activation[..., width_ssm + N :].reshape(block_count, block_len, N)
    step_size = jax.nn.softplus(dt_raw + params[1]).reshape(block_count, block_len, heads_local)
    decay_rate = -jnp.exp(params[0])
    return (x_conv, b_conv, c_conv, step_size, decay_rate, params[2])


def state_piece(x_conv, b_conv, step_size, decay_rate):
    cumulative = jnp.cumsum(step_size * decay_rate, axis=1)
    total_log = cumulative[:, -1]
    weight = jnp.exp(total_log[:, None, :] - cumulative) * step_size
    states = jnp.einsum("bsn,bshp->bhpn", b_conv, x_conv * weight[..., None], precision=highest)
    return (jnp.exp(total_log), states)


def output_piece(x_conv, b_conv, c_conv, step_size, decay_rate, skip_gain, entering):
    block_len = x_conv.shape[1]
    cumulative = jnp.cumsum(step_size * decay_rate, axis=1)
    segment = cumulative[:, :, None, :] - cumulative[:, None, :, :]
    lower_mask = (jnp.arange(block_len)[:, None] >= jnp.arange(block_len)[None, :])[
        None, :, :, None
    ]
    decay_mat = jnp.where(lower_mask, jnp.exp(jnp.where(lower_mask, segment, 0.0)), 0.0)
    inner_bc = jnp.einsum("btn,bsn->bts", c_conv, b_conv, precision=highest)
    mixing = decay_mat * inner_bc[..., None] * step_size[:, None, :, :]
    local_part = jnp.einsum("btsh,bshp->bthp", mixing, x_conv, precision=highest)
    carried = (
        jnp.einsum("btn,bhpn->bthp", c_conv, entering, precision=highest)
        * jnp.exp(cumulative)[..., None]
    )
    return local_part + carried + skip_gain[:, None] * x_conv


def combine(earlier, later_part):
    return (earlier[0] * later_part[0], later_part[0][..., None, None] * earlier[1] + later_part[1])


def combine_pair(earlier, later_part):
    return (combine(later_part[0], earlier[0]), combine(earlier[1], later_part[1]))


def chain_up(parts, step):
    return jax.tree.map(
        lambda part, own: part.astype(own.dtype), shifted(shortened(parts), "ctx", step), parts
    )


def chain_down(parts, step):
    return jax.tree.map(
        lambda part, own: part.astype(own.dtype), shifted(shortened(parts), "ctx", -step), parts
    )


def exclusive_prefix(parts, identity, combine_fn, mover, position, count):
    moved = mover(parts, 1)
    running = jax.tree.map(lambda got, ident: jnp.where(position >= 1, got, ident), moved, identity)
    step = 1
    while step < count:
        got = mover(running, step)
        joined = combine_fn(got, running)
        running = jax.tree.map(
            lambda new_val, old_val: jnp.where(position >= step, new_val, old_val), joined, running
        )
        step = step * 2
    return running


def two_chains(first_part, second_part, ctx_index, ctx_count):
    identity = (jnp.ones_like(first_part[0]), jnp.zeros_like(first_part[1]))
    entry_first = exclusive_prefix(first_part, identity, combine, chain_up, ctx_index, ctx_count)
    rest_first, before_second = exclusive_prefix(
        (first_part, second_part),
        (identity, identity),
        combine_pair,
        chain_down,
        ctx_count - 1 - ctx_index,
        ctx_count,
    )
    total_first = combine(combine(entry_first, first_part), rest_first)
    entry_second = combine(total_first, before_second)
    return (entry_first[1], entry_second[1])


def block_rims(rim_values):
    return extended(rim_values, (("ctx", 0),), 1)


def layer_weights(bundle, layer_idx):
    return tuple((member[layer_idx] for member in bundle))


def local(
    hidden,
    cotangent,
    lengths,
    norm_gains,
    mix_weight,
    share_weight,
    chan_params,
    shared_conv,
    head_params,
    out_weight,
    up_weight,
    down_weight,
):
    ctx_count = lax.axis_size("ctx")
    tp_count = lax.axis_size("tp")
    ctx_index = lax.axis_index("ctx")
    tp_index = lax.axis_index("tp")
    at_last = ctx_index == ctx_count - 1
    slot_count = hidden.shape[0]
    block_len = hidden.shape[2]
    row_count = slot_count * 2 * block_len
    seq_len = 2 * ctx_count * block_len
    heads_local = MH // tp_count
    width_ssm = heads_local * P_SIZE
    qheads_local = AH // tp_count
    ff_local = FF // tp_count
    conv_width = width_ssm + 2 * N
    kv_cols = 2 * N
    dt_cols = 2 * N + 2 * KVH * HD
    share_cols = share_weight.shape[2]
    kv_head = tp_index * qheads_local // (AH // KVH)
    score_scale = HD ** (-0.5)
    cut_row = block_len - (CONV - 1)
    half_index = jnp.arange(2)
    own_blocks = jnp.where(half_index == 0, ctx_index, 2 * ctx_count - 1 - ctx_index)
    query_pos = own_blocks[:, None] * block_len + jnp.arange(block_len)[None, :]
    ctx_ids = jnp.arange(ctx_count)
    key_blocks = jnp.where(
        half_index[None, :] == 0, ctx_ids[:, None], 2 * ctx_count - 1 - ctx_ids[:, None]
    )
    key_pos = (key_blocks[:, :, None] * block_len + jnp.arange(block_len)[None, None, :]).reshape(
        -1
    )
    valid_rows = (
        (query_pos[None] < lengths[:, None, None]).astype(jnp.float32).reshape(row_count, 1)
    )
    row_pos = jnp.broadcast_to(query_pos[None], (slot_count, 2, block_len)).reshape(row_count)
    causal = key_pos[None, :] <= query_pos.reshape(-1)[:, None]

    def state_chains(first_part, second_part):
        return two_chains(first_part, second_part, ctx_index, ctx_count)

    def attend(inputs):
        queries, keyval = inputs
        key_rows = keyval[:, :HD]
        value_rows = keyval[:, HD:]
        scores = (
            jnp.einsum("qhd,kd->hqk", queries, key_rows, preferred_element_type=jnp.float32)
            * score_scale
        )
        scores = jnp.where(causal[None], scores, -1e30)
        row_peak = jnp.max(scores, axis=-1, keepdims=True)
        exp_scores = jnp.exp(scores - row_peak)
        row_total = jnp.sum(exp_scores, axis=-1, keepdims=True)
        probability = (exp_scores / row_total).astype(jnp.bfloat16)
        attended = jnp.einsum(
            "hqk,kd->qhd", probability, value_rows, preferred_element_type=jnp.float32
        )
        return (attended, row_peak + jnp.log(row_total))

    def attend_back(inputs):
        queries, keyval, logsum, grad_out = inputs
        key_rows = keyval[:, :HD]
        value_rows = keyval[:, HD:]
        scores = (
            jnp.einsum("qhd,kd->hqk", queries, key_rows, preferred_element_type=jnp.float32)
            * score_scale
        )
        scores = jnp.where(causal[None], scores, -1e30)
        probability = jnp.exp(scores - logsum)
        probs_low = probability.astype(jnp.bfloat16)
        grad_probs = jnp.einsum(
            "qhd,kd->hqk", grad_out, value_rows, preferred_element_type=jnp.float32
        )
        inner_sum = jnp.sum(probability * grad_probs, axis=-1, keepdims=True)
        grad_scores = (probability * (grad_probs - inner_sum)).astype(jnp.bfloat16)
        grad_q = (
            jnp.einsum("hqk,kd->qhd", grad_scores, key_rows, preferred_element_type=jnp.float32)
            * score_scale
        )
        grad_k = (
            jnp.einsum("hqk,qhd->kd", grad_scores, queries, preferred_element_type=jnp.float32)
            * score_scale
        )
        grad_v = jnp.einsum("hqk,qhd->kd", probs_low, grad_out, preferred_element_type=jnp.float32)
        return (grad_q, jnp.concatenate([grad_k, grad_v], axis=-1))

    stream = hidden.reshape(row_count, D).astype(jnp.float32)
    all_weights = (
        lax.all_gather(norm_gains, "ctx", axis=2, tiled=True),
        lax.all_gather(mix_weight, "ctx", axis=1, tiled=True),
        lax.all_gather(share_weight, "ctx", axis=1, tiled=True),
        lax.all_gather(out_weight, "ctx", axis=2, tiled=True),
        lax.all_gather(up_weight, "ctx", axis=1, tiled=True),
        lax.all_gather(down_weight, "ctx", axis=2, tiled=True),
    )
    kept_records = []
    for layer_idx in range(LAYERS):
        forward_weights = layer_weights(all_weights, layer_idx)
        (
            forward_gain_rows,
            forward_mix_full,
            forward_share_full,
            forward_out_full,
            forward_up_full,
            forward_down_full,
        ) = forward_weights
        normed_f, norm_one_back = jax.vjp(
            norm_piece, stream, forward_gain_rows[0].astype(jnp.float32)
        )
        normed_one = normed_f.astype(jnp.bfloat16)
        mixed = matmul(normed_one, forward_mix_full)
        shared = matmul(normed_one, forward_share_full)
        forward_gate_z = mixed[:, :width_ssm]
        q_pre = mixed[:, 2 * width_ssm :].reshape(row_count, qheads_local, HD)
        key_pre = lax.dynamic_slice_in_dim(shared, kv_cols + kv_head * HD, HD, 1)
        value_pre = lax.dynamic_slice_in_dim(shared, kv_cols + KVH * HD + kv_head * HD, HD, 1)
        dt_raw = lax.dynamic_slice_in_dim(shared, dt_cols + tp_index * heads_local, heads_local, 1)
        pre_conv = jnp.concatenate(
            [mixed[:, width_ssm : 2 * width_ssm], shared[:, :kv_cols]], axis=1
        ).reshape(slot_count, 2, block_len, conv_width)
        tails = pre_conv[:, :, cut_row:]
        rim_values = block_rims(jnp.stack([tails[:, 1], tails[:, 0]]))
        prev_rows = jnp.stack(
            [rim_values[0], jnp.where(at_last, tails[:, 0], rim_values[3])], axis=1
        )
        conv_taps = jnp.concatenate(
            [chan_params[layer_idx, :CONV], shared_conv[layer_idx, :CONV]], axis=1
        )
        conv_bias = jnp.concatenate([chan_params[layer_idx, CONV], shared_conv[layer_idx, CONV]])
        ssm_inputs, inputs_back = jax.vjp(
            input_piece, pre_conv, prev_rows, conv_taps, conv_bias, dt_raw, head_params[layer_idx]
        )
        x_conv, b_conv, c_conv, step_size, decay_rate, skip_gain = ssm_inputs
        summary, state_back = jax.vjp(state_piece, x_conv, b_conv, step_size, decay_rate)
        forward_decays_h = summary[0].reshape(slot_count, 2, heads_local)
        states_h = summary[1].reshape(slot_count, 2, heads_local, P_SIZE, N)
        enter_first, enter_second = state_chains(
            (forward_decays_h[:, 0], states_h[:, 0]), (forward_decays_h[:, 1], states_h[:, 1])
        )
        entering = jnp.stack([enter_first, enter_second], axis=1).reshape(
            slot_count * 2, heads_local, P_SIZE, N
        )
        ssm_y, output_back = jax.vjp(
            output_piece, x_conv, b_conv, c_conv, step_size, decay_rate, skip_gain, entering
        )
        ssm_flat = ssm_y.reshape(row_count, width_ssm)
        forward_gated = ssm_flat * jax.nn.silu(forward_gate_z)
        chan_gain = chan_params[layer_idx, CONV + 1]
        gated_low = (forward_gated * chan_gain).astype(jnp.bfloat16)
        squares = jnp.sum(forward_gated * forward_gated, axis=-1, keepdims=True)
        q_slots = (
            rotate(q_pre, row_pos[:, None])
            .astype(jnp.bfloat16)
            .reshape(slot_count, 2 * block_len, qheads_local, HD)
        )
        forward_key_rows = rotate(key_pre, row_pos).astype(jnp.bfloat16)
        forward_keyval = jnp.concatenate(
            [forward_key_rows, value_pre.astype(jnp.bfloat16)], axis=1
        ).reshape(slot_count, 1, 2, block_len, 2 * HD)
        gathered = lax.all_gather(forward_keyval, "ctx", axis=1, tiled=True).reshape(
            slot_count, seq_len, 2 * HD
        )
        forward_attended, forward_logsum = lax.map(attend, (q_slots, gathered))
        att_low = forward_attended.reshape(row_count, qheads_local * HD).astype(jnp.bfloat16)
        sum_ssm, sum_att, sum_squares = lax.psum(
            (
                matmul(gated_low, forward_out_full[:width_ssm]),
                matmul(att_low, forward_out_full[width_ssm:]),
                squares,
            ),
            "tp",
        )
        forward_gated_scale = lax.rsqrt(sum_squares / (MH * P_SIZE) + eps_norm)
        middle = stream + (forward_gated_scale * sum_ssm + sum_att)
        normed_two_f, norm_two_back = jax.vjp(
            norm_piece, middle, forward_gain_rows[1].astype(jnp.float32)
        )
        normed_two = normed_two_f.astype(jnp.bfloat16)
        gate_up = matmul(normed_two, forward_up_full)
        forward_gate_vals = gate_up[:, :ff_local]
        up_vals = gate_up[:, ff_local:]
        activation = (jax.nn.silu(forward_gate_vals) * up_vals).astype(jnp.bfloat16)
        ffn_out = lax.psum(matmul(activation, forward_down_full).astype(jnp.bfloat16), "tp").astype(
            jnp.float32
        )
        result = (middle + ffn_out) * valid_rows
        forward_records = dict(
            normed_one=normed_one,
            norm_one_back=norm_one_back,
            gate_z=forward_gate_z,
            inputs_back=inputs_back,
            state_back=state_back,
            output_back=output_back,
            decays_h=forward_decays_h,
            entering=entering,
            ssm_flat=ssm_flat,
            gated=forward_gated,
            gated_low=gated_low,
            chan_gain=chan_gain,
            q_slots=q_slots,
            gathered=gathered,
            logsum=forward_logsum,
            att_low=att_low,
            sum_ssm=sum_ssm,
            gated_scale=forward_gated_scale,
            norm_two_back=norm_two_back,
            normed_two=normed_two,
            gate_vals=forward_gate_vals,
            up_vals=up_vals,
            activation=activation,
        )
        stream = result
        kept_records.append(forward_records)
    activations = stream.reshape(hidden.shape)
    grad_stream = cotangent.reshape(row_count, D).astype(jnp.float32)
    big_list = [None] * LAYERS
    chan_list = [None] * LAYERS
    conv_list = [None] * LAYERS
    head_list = [None] * LAYERS
    for layer_idx in reversed(range(LAYERS)):
        grad_in = grad_stream
        backward_records = kept_records[layer_idx]
        gain_rows, mix_full, share_full, out_full, up_full, down_full = layer_weights(
            all_weights, layer_idx
        )
        grad_masked = grad_in * valid_rows
        grad_ffn = grad_masked.astype(jnp.bfloat16)
        grad_activation = matmul_nt(grad_ffn, down_full)
        grad_down = matmul_tn(backward_records["activation"], grad_ffn)
        gate_vals = backward_records["gate_vals"]
        grad_gate = grad_activation * backward_records["up_vals"] * silu_grad(gate_vals)
        grad_upper = grad_activation * jax.nn.silu(gate_vals)
        grad_gate_up = jnp.concatenate([grad_gate, grad_upper], axis=1).astype(jnp.bfloat16)
        grad_upw = matmul_tn(backward_records["normed_two"], grad_gate_up)
        grad_normed_two = lax.psum(
            matmul_nt(grad_gate_up, up_full).astype(jnp.bfloat16), "tp"
        ).astype(jnp.float32)
        grad_middle_norm, grad_gain_two = backward_records["norm_two_back"](grad_normed_two)
        grad_middle = grad_masked + grad_middle_norm
        grad_branch = grad_middle.astype(jnp.bfloat16)
        branch_f32 = grad_branch.astype(jnp.float32)
        gated_scale = backward_records["gated_scale"]
        grad_scale = jnp.sum(branch_f32 * backward_records["sum_ssm"], axis=-1, keepdims=True)
        grad_squares = grad_scale * -0.5 * gated_scale * gated_scale * gated_scale / (MH * P_SIZE)
        grad_outw_ssm = lax.dot_general(
            backward_records["gated_low"].astype(jnp.float32),
            gated_scale * branch_f32,
            (((0,), (0,)), ((), ())),
            precision=highest,
            preferred_element_type=jnp.float32,
        )
        grad_outw_att = matmul_tn(backward_records["att_low"], grad_branch)
        grad_gated_low = gated_scale * matmul_nt(grad_branch, out_full[:width_ssm])
        grad_att = matmul_nt(grad_branch, out_full[width_ssm:]).astype(jnp.bfloat16)
        gated = backward_records["gated"]
        grad_gated = grad_gated_low * backward_records["chan_gain"] + 2.0 * grad_squares * gated
        grad_chan_gain = jnp.sum(grad_gated_low * gated, axis=0)
        gate_z = backward_records["gate_z"]
        grad_ssm_y = grad_gated * jax.nn.silu(gate_z)
        grad_z = grad_gated * backward_records["ssm_flat"] * silu_grad(gate_z)
        grad_att_slots = grad_att.reshape(slot_count, 2 * block_len, qheads_local, HD)
        grads_q, grads_kv = lax.map(
            attend_back,
            (
                backward_records["q_slots"],
                backward_records["gathered"],
                backward_records["logsum"],
                grad_att_slots,
            ),
        )
        grad_kv_own = (
            lax.psum_scatter(
                grads_kv.reshape(slot_count, ctx_count, 2, block_len, 2 * HD).astype(jnp.bfloat16),
                "ctx",
                scatter_dimension=1,
                tiled=True,
            )
            .astype(jnp.float32)
            .reshape(row_count, 2 * HD)
        )
        grad_keys = rotate(grad_kv_own[:, :HD], -row_pos)
        grad_values = grad_kv_own[:, HD:]
        grad_queries = rotate(
            grads_q.reshape(row_count, qheads_local, HD), -row_pos[:, None]
        ).reshape(row_count, qheads_local * HD)
        grad_y = grad_ssm_y.reshape(slot_count * 2, block_len, heads_local, P_SIZE)
        out_grads = backward_records["output_back"](grad_y)
        enter_parts = out_grads[6].reshape(slot_count, 2, heads_local, P_SIZE, N)
        decays_h = backward_records["decays_h"]
        end_second, end_first = state_chains(
            (decays_h[:, 1], enter_parts[:, 1]), (decays_h[:, 0], enter_parts[:, 0])
        )
        grad_end = jnp.stack([end_first, end_second], axis=1).reshape(
            slot_count * 2, heads_local, P_SIZE, N
        )
        grad_decay = jnp.sum(grad_end * backward_records["entering"], axis=(2, 3))
        state_grads = backward_records["state_back"]((grad_decay, grad_end))
        input_grads = backward_records["inputs_back"](
            (
                out_grads[0] + state_grads[0],
                out_grads[1] + state_grads[1],
                out_grads[2],
                out_grads[3] + state_grads[2],
                out_grads[4] + state_grads[3],
                out_grads[5],
            )
        )
        grad_pre, grad_prev, grad_taps, grad_bias, grad_dt, grad_params = input_grads
        back_rims = block_rims(jnp.stack([grad_prev[:, 0], grad_prev[:, 1]]))
        tail_grad = jnp.stack(
            [jnp.where(at_last, grad_prev[:, 1], back_rims[3]), back_rims[0]], axis=1
        )
        grad_pre = jnp.concatenate(
            [grad_pre[:, :, :cut_row], grad_pre[:, :, cut_row:] + tail_grad], axis=2
        ).reshape(row_count, conv_width)
        grad_mix = jnp.concatenate([grad_z, grad_pre[:, :width_ssm], grad_queries], axis=1).astype(
            jnp.bfloat16
        )
        grad_share = jnp.concatenate(
            [grad_pre[:, width_ssm:], jnp.zeros((row_count, share_cols - kv_cols), jnp.float32)],
            axis=1,
        )
        grad_share = lax.dynamic_update_slice_in_dim(
            grad_share, grad_keys, kv_cols + kv_head * HD, 1
        )
        grad_share = lax.dynamic_update_slice_in_dim(
            grad_share, grad_values, kv_cols + KVH * HD + kv_head * HD, 1
        )
        grad_share = lax.dynamic_update_slice_in_dim(
            grad_share, grad_dt, dt_cols + tp_index * heads_local, 1
        )
        grad_normed_part = lax.psum(
            matmul_nt(grad_mix, mix_full).astype(jnp.bfloat16), "tp"
        ).astype(jnp.float32)
        grad_share_all = lax.psum(grad_share.astype(jnp.bfloat16), "tp")
        grad_normed_one = grad_normed_part + matmul_nt(grad_share_all, share_full)
        grad_mixw = matmul_tn(backward_records["normed_one"], grad_mix)
        grad_sharew = matmul_tn(backward_records["normed_one"], grad_share_all)
        grad_stream_norm, grad_gain_one = backward_records["norm_one_back"](grad_normed_one)
        backward_grad_stream = grad_middle + grad_stream_norm
        big_grads = (
            jnp.stack([grad_gain_one, grad_gain_two]),
            grad_mixw,
            grad_sharew,
            jnp.concatenate([grad_outw_ssm, grad_outw_att], axis=0),
            grad_upw,
            grad_down,
        )
        chan_grad = jnp.concatenate(
            [grad_taps[:, :width_ssm], grad_bias[None, :width_ssm], grad_chan_gain[None]], axis=0
        )
        conv_grad = jnp.concatenate([grad_taps[:, width_ssm:], grad_bias[None, width_ssm:]], axis=0)
        grad_stream, big_grads, chan_grad, conv_grad, head_grad = (
            backward_grad_stream,
            big_grads,
            chan_grad,
            conv_grad,
            grad_params,
        )
        chan_list[layer_idx] = chan_grad
        conv_list[layer_idx] = conv_grad
        head_list[layer_idx] = head_grad
        big_list[layer_idx] = big_grads
    input_grad = grad_stream.reshape(hidden.shape)
    stacked_gain = jnp.stack([big_list[idx_layer][0] for idx_layer in range(LAYERS)])
    stacked_mix = jnp.stack([big_list[idx_layer][1] for idx_layer in range(LAYERS)])
    stacked_share = jnp.stack([big_list[idx_layer][2] for idx_layer in range(LAYERS)])
    stacked_out = jnp.stack([big_list[idx_layer][3] for idx_layer in range(LAYERS)])
    stacked_up = jnp.stack([big_list[idx_layer][4] for idx_layer in range(LAYERS)])
    stacked_down = jnp.stack([big_list[idx_layer][5] for idx_layer in range(LAYERS)])
    stacked_gain, stacked_mix, stacked_share, stacked_out, stacked_up, stacked_down = (
        lax.psum_scatter(
            stacked_gain.astype(jnp.bfloat16), "ctx", scatter_dimension=2, tiled=True
        ).astype(jnp.float32),
        lax.psum_scatter(
            stacked_mix.astype(jnp.bfloat16), "ctx", scatter_dimension=1, tiled=True
        ).astype(jnp.float32),
        lax.psum_scatter(
            stacked_share.astype(jnp.bfloat16), "ctx", scatter_dimension=1, tiled=True
        ).astype(jnp.float32),
        lax.psum_scatter(
            stacked_out.astype(jnp.bfloat16), "ctx", scatter_dimension=2, tiled=True
        ).astype(jnp.float32),
        lax.psum_scatter(
            stacked_up.astype(jnp.bfloat16), "ctx", scatter_dimension=1, tiled=True
        ).astype(jnp.float32),
        lax.psum_scatter(
            stacked_down.astype(jnp.bfloat16), "ctx", scatter_dimension=2, tiled=True
        ).astype(jnp.float32),
    )
    chan_full = lax.dynamic_update_slice_in_dim(
        jnp.zeros((LAYERS, CONV + 2, MH * P_SIZE), jnp.float32),
        jnp.stack(chan_list),
        tp_index * width_ssm,
        2,
    )
    head_full = lax.dynamic_update_slice_in_dim(
        jnp.zeros((LAYERS, 3, MH), jnp.float32), jnp.stack(head_list), tp_index * heads_local, 2
    )
    chan_sum, head_sum, conv_sum = lax.psum(
        (chan_full, head_full, jnp.stack(conv_list)), ("ctx", "tp")
    )
    grad_chan = lax.dynamic_slice_in_dim(chan_sum, tp_index * width_ssm, width_ssm, 2)
    grad_heads = lax.dynamic_slice_in_dim(head_sum, tp_index * heads_local, heads_local, 2)
    return (
        activations,
        input_grad,
        stacked_gain,
        stacked_mix,
        stacked_share,
        grad_chan,
        conv_sum,
        grad_heads,
        stacked_out,
        stacked_up,
        stacked_down,
    )


def solution(mesh):
    return jax.shard_map(
        local,
        mesh=mesh,
        in_specs=(
            P(None, None, "ctx", None),
            P(None, None, "ctx", None),
            P(),
            P(None, None, "ctx"),
            P(None, "ctx", "tp"),
            P(None, "ctx", None),
            P(None, None, "tp"),
            P(),
            P(None, None, "tp"),
            P(None, "tp", "ctx"),
            P(None, "ctx", "tp"),
            P(None, "tp", "ctx"),
        ),
        out_specs=(
            P(None, None, "ctx", None),
            P(None, None, "ctx", None),
            P(None, None, "ctx"),
            P(None, "ctx", "tp"),
            P(None, "ctx", None),
            P(None, None, "tp"),
            P(),
            P(None, None, "tp"),
            P(None, "tp", "ctx"),
            P(None, "ctx", "tp"),
            P(None, "tp", "ctx"),
        ),
        check_vma=False,
    )
```

profile of v0, /device:TPU:0, one launch (start us, length us, event | category | flops | bytes accessed | tf_op | source)
XLA Modules:
  0.0 3531.1 jit_solution(11207907805421278376)
XLA Ops:
  38.9 104.3 %all-gather.8.cloned.1.call-done = bf16[2,2048,1072]{1,2,0:T(8,128)(2,1)} async-done(((bf16[2,256,1072]{1,2,0:T(8,128)(2,1)}), bf16[2,2048,1072]{1,2,0:T(8,128)(2,1)}) %all-gather.8.cloned.1.call-update) | async-done | bytes 8781840 | tf_op jit(solution)/shard_map/all_gather | solution.py:290
  158.5 36.9 %all_gather.28 = bf16[2,8,2,48,256]{4,3,2,0,1:T(8,128)(2,1)S(1)} all-gather(bf16[2,1,2,48,256]{4,3,2,0,1:T(8,128)(2,1)S(1)} %bitcast.880), channel_id=1, replica_groups=mesh['ctx'=8,'tp'=4] {'ctx'}, dimensions={1}, use_global_device_ids=true | all-gather | bytes 884736 | tf_op jit(solution)/shard_map/all_gather | solution.py:359
  218.8 134.1 %all-gather.6.cloned.1.call-done = bf16[2,2048,1792]{2,1,0:T(8,128)(2,1)} async-done(((bf16[2,256,1792]{2,1,0:T(8,128)(2,1)}), bf16[2,2048,1792]{2,1,0:T(8,128)(2,1)}) %all-gather.6.cloned.1.call-update) | async-done | bytes 14680080 | tf_op jit(solution)/shard_map/all_gather | solution.py:289
  446.3 30.2 collective-permute-done.6
  517.4 39.5 %collective-permute-start.8 = (bf16[2,12,64,256]{3,2,1,0:T(8,128)(2,1)}, bf16[2,12,64,256]{3,2,1,0:T(8,128)(2,1)}, u32[]{:S(2)}, u32[]{:S(2)}) collective-permute-start(bf16[2,12,64,256]{3,2,1,0:T(8,128)(2,1)} %fusion.358), channel_id=1, source_target_pairs={{0,16},{4,20},{8,24},{12,28},{1,17},{5,21},{9,25},{13,29},{2,18},{... | collective-permute-start | bytes 2359304 | tf_op jit(solution)/shard_map/ppermute | solution.py:30
  582.9 40.9 %collective-permute-done.20 = bf16[2,12,64,256]{3,2,1,0:T(8,128)(2,1)} collective-permute-done((bf16[2,12,64,256]{3,2,1,0:T(8,128)(2,1)}, bf16[2,12,64,256]{3,2,1,0:T(8,128)(2,1)}, u32[]{:S(2)}, u32[]{:S(2)}) %collective-permute-start.20) | collective-permute-done | bytes 786464 | tf_op jit(solution)/shard_map/ppermute | solution.py:30
  670.7 57.2 %all-reduce.64.cloned.1.call-done = (f32[192,2048]{1,0:T(8,128)}, f32[192,2048]{1,0:T(8,128)}) async-done(((f32[192,2048]{1,0:T(8,128)}, f32[192,2048]{1,0:T(8,128)}), (f32[192,2048]{1,0:T(8,128)}, f32[192,2048]{1,0:T(8,128)})) %all-reduce.64.cloned.1.call-update) | async-done | bytes 3145744 | tf_op jit(solution)/shard_map/psum | solution.py:364
  730.5 227.2 %all-gather.12.cloned.1.call-done = bf16[2,2048,2048]{2,1,0:T(8,128)(2,1)} async-done(((bf16[2,256,2048]{2,1,0:T(8,128)(2,1)}), bf16[2,2048,2048]{2,1,0:T(8,128)(2,1)}) %all-gather.12.cloned.1.call-update) | async-done | bytes 16777232 | tf_op jit(solution)/shard_map/all_gather | solution.py:292
  964.5 118.7 %all-gather.14.cloned.1.call-done = bf16[2,1024,2048]{2,1,0:T(8,128)(2,1)} async-done(((bf16[2,1024,256]{2,1,0:T(8,128)(2,1)}), bf16[2,1024,2048]{2,1,0:T(8,128)(2,1)}) %all-gather.14.cloned.1.call-update) | async-done | bytes 8388624 | tf_op jit(solution)/shard_map/all_gather | solution.py:293
  1090.7 29.6 all-reduce.50.cloned.1.call-done
  1165.8 37.2 %all_gather.31 = bf16[2,8,2,48,256]{4,3,2,0,1:T(8,128)(2,1)S(1)} all-gather(bf16[2,1,2,48,256]{4,3,2,0,1:T(8,128)(2,1)S(1)} %bitcast.881), channel_id=1, replica_groups=mesh['ctx'=8,'tp'=4] {'ctx'}, dimensions={1}, use_global_device_ids=true | all-gather | bytes 884736 | tf_op jit(solution)/shard_map/all_gather | solution.py:359
  1255.9 34.5 collective-permute-done.30
  1386.4 50.7 %collective-permute-done.45 = bf16[2,12,64,256]{3,2,1,0:T(8,128)(2,1)S(1)} collective-permute-done((bf16[2,12,64,256]{3,2,1,0:T(8,128)(2,1)S(1)}, bf16[2,12,64,256]{3,2,1,0:T(8,128)(2,1)S(1)}, u32[]{:S(2)}, u32[]{:S(2)}) %collective-permute-start.45) | collective-permute-done | bytes 786464 | tf_op jit(solution)/shard_map/ppermute | solution.py:30
  1508.3 29.9 all-reduce.62.cloned.1.call-done
  1906.1 28.6 all-reduce.68.cloned.1.call-done
  2084.2 30.7 collective-permute-done.71
  2290.9 49.1 %all-reduce.66.cloned.1.call-done = (bf16[192,2048]{1,0:T(8,128)(2,1)}, bf16[192,1072]{1,0:T(8,128)(2,1)}, bf16[192,2048]{1,0:T(8,128)(2,1)}) async-done(((bf16[192,2048]{1,0:T(8,128)(2,1)}, bf16[192,1072]{1,0:T(8,128)(2,1)}, bf16[192,2048]{1,0:T(8,128)(2,1)}), (bf16[192,2048]{1,0:T(8,128)(2,1)}, bf16[192,1072]{1,0:T(8,128)(2,1)}, bf16[192,2048]{1,0:T(8,128)(2,1)})) %all-reduce.66.cloned.1.call-update) | async-done | bytes 1984528 | tf_op jit(solution)/shard_map/psum | solution.py:382
  2423.3 40.3 %all-reduce.34 = (f32[2,5,512]{2,1,0:T(8,128)S(1)}, f32[2,3,48]{2,0,1:T(2,128)S(1)}) all-reduce(f32[2,5,512]{2,1,0:T(8,128)S(1)} %pad_maximum_fusion.35, f32[2,3,48]{2,0,1:T(2,128)S(1)} %dynamic_update_slice.58), channel_id=1, replica_groups=mesh['ctx'=8,'tp'=4] {'ctx','tp'}, use_global_device_ids=true, to_apply=%region_84.86 | all-reduce | flops 5408 | bytes 43264 | tf_op jit(solution)/shard_map/psum | solution.py:599
  2473.7 60.3 %reduce-scatter.25.cloned.1.call-done = bf16[256,4]{1,0:T(8,128)(2,1)} async-done(((bf16[2048,4]{1,0:T(8,128)(2,1)}), bf16[256,4]{1,0:T(8,128)(2,1)}) %reduce-scatter.25.cloned.1.call-update) | async-done | bytes 2064
  2535.6 150.6 %reduce-scatter.23.cloned.1.call-done = bf16[2,1024,256]{2,1,0:T(8,128)(2,1)} async-done(((bf16[2,1024,2048]{2,1,0:T(8,128)(2,1)}), bf16[2,1024,256]{2,1,0:T(8,128)(2,1)}) %reduce-scatter.23.cloned.1.call-update) | async-done | bytes 1048592 | tf_op jit(solution)/shard_map/reduce_scatter | solution.py:586
  2688.9 149.2 %reduce-scatter.19.cloned.1.call-done = bf16[2,1024,256]{2,1,0:T(8,128)(2,1)} async-done(((bf16[2,1024,2048]{2,1,0:T(8,128)(2,1)}), bf16[2,1024,256]{2,1,0:T(8,128)(2,1)}) %reduce-scatter.19.cloned.1.call-update) | async-done | bytes 1048592 | tf_op jit(solution)/shard_map/reduce_scatter | solution.py:580
  2840.8 155.2 %reduce-scatter.17.cloned.1.call-done = bf16[2,256,1072]{1,2,0:T(8,128)(2,1)} async-done(((bf16[2,2048,1072]{1,2,0:T(8,128)(2,1)}), bf16[2,256,1072]{1,2,0:T(8,128)(2,1)}) %reduce-scatter.17.cloned.1.call-update) | async-done | bytes 1097744 | tf_op jit(solution)/shard_map/reduce_scatter | solution.py:577
  2998.7 282.5 %reduce-scatter.21.cloned.1.call-done = bf16[2,256,2048]{2,1,0:T(8,128)(2,1)} async-done(((bf16[2,2048,2048]{2,1,0:T(8,128)(2,1)}), bf16[2,256,2048]{2,1,0:T(8,128)(2,1)}) %reduce-scatter.21.cloned.1.call-update) | async-done | bytes 2097168 | tf_op jit(solution)/shard_map/reduce_scatter | solution.py:583
  3285.4 235.1 %reduce-scatter.15.cloned.1.call-done = bf16[2,256,1792]{2,1,0:T(8,128)(2,1)} async-done(((bf16[2,2048,1792]{2,1,0:T(8,128)(2,1)}), bf16[2,256,1792]{2,1,0:T(8,128)(2,1)}) %reduce-scatter.15.cloned.1.call-update) | async-done | bytes 1835024 | tf_op jit(solution)/shard_map/reduce_scatter | solution.py:574
  (1589 shorter events, 1394.3 us)
Async XLA Ops:
  7.2 136.0 %all-gather.8.cloned.1.call-start = ((), (), s32[]{:S(2)}) async-start(), calls=%async_computation.7 | async-start | bytes 9879552 | tf_op jit(solution)/shard_map/all_gather | solution.py:290
  8.0 344.9 %all-gather.6.cloned.1.call-start = ((), (), s32[]{:S(2)}) async-start(), calls=%async_computation.6 | async-start | bytes 16515072 | tf_op jit(solution)/shard_map/all_gather | solution.py:289
  8.7 567.8 %all-gather.10.cloned.1.call-start = ((), (), s32[]{:S(2)}) async-start(), calls=%async_computation.8 | async-start | bytes 9437184 | tf_op jit(solution)/shard_map/all_gather | solution.py:291
  9.4 718.5 %all-reduce.64.cloned.1.call-start = ((), (), s32[]{:S(2)}) async-start(), calls=%async_computation.24 | async-start | bytes 6291456 | tf_op jit(solution)/shard_map/psum | solution.py:364
  203.7 178.7 %collective-permute-start.4 = (bf16[2,12]{1,0:T(2,128)(2,1)}, bf16[2,12]{1,0:T(2,128)(2,1)}, u32[]{:S(2)}, u32[]{:S(2)}) collective-permute-start(bf16[2,12]{1,0:T(2,128)(2,1)} %get-tuple-element.612), channel_id=1, source_target_pairs={{0,8},{4,12},{8,16},{12,20},{16,24},{20,28},{1,9},{5,13},{9,17},{1... | collective-permute-start | bytes 152 | tf_op jit(solution)/shard_map/ppermute | solution.py:30
  212.7 147.3 %collective-permute-start.11 = (bf16[2,12]{1,0:T(2,128)(2,1)S(1)}, bf16[2,12]{1,0:T(2,128)(2,1)S(1)}, u32[]{:S(2)}, u32[]{:S(2)}) collective-permute-start(bf16[2,12]{1,0:T(2,128)(2,1)S(1)} %get-tuple-element.618), channel_id=1, source_target_pairs={{8,0},{12,4},{16,8},{20,12},{24,16},{28,20},{9,1},{13,5},{17,9},{2... | collective-permute-start | bytes 152 | tf_op jit(solution)/shard_map/ppermute | solution.py:30
  217.3 170.3 %collective-permute-start.16 = (bf16[2,12]{1,0:T(2,128)(2,1)}, bf16[2,12]{1,0:T(2,128)(2,1)}, u32[]{:S(2)}, u32[]{:S(2)}) collective-permute-start(bf16[2,12]{1,0:T(2,128)(2,1)} %get-tuple-element.616), channel_id=1, source_target_pairs={{16,0},{20,4},{24,8},{28,12},{17,1},{21,5},{25,9},{29,13},{18,2},{... | collective-permute-start | bytes 152 | tf_op jit(solution)/shard_map/ppermute | solution.py:30
  661.9 295.8 %all-gather.12.cloned.1.call-start = ((), (), s32[]{:S(2)}) async-start(), calls=%async_computation.9 | async-start | bytes 18874368 | tf_op jit(solution)/shard_map/all_gather | solution.py:292
  662.5 420.7 %all-gather.14.cloned.1.call-start = ((), (), s32[]{:S(2)}) async-start(), calls=%async_computation.10 | async-start | bytes 9437184 | tf_op jit(solution)/shard_map/all_gather | solution.py:293
  663.1 457.2 %all-reduce.50.cloned.1.call-start = ((), (), s32[]{:S(2)}) async-start(), calls=%async_computation.11 | async-start | bytes 1572864 | tf_op jit(solution)/shard_map/psum | solution.py:382
  1087.3 450.9 %all-reduce.62.cloned.1.call-start = ((), (), s32[]{:S(2)}) async-start(), calls=%async_computation.23 | async-start | bytes 6291456 | tf_op jit(solution)/shard_map/psum | solution.py:364
  1290.4 93.7 %collective-permute-start.37 = (bf16[2,12]{1,0:T(2,128)(2,1)S(1)}, bf16[2,12]{1,0:T(2,128)(2,1)S(1)}, u32[]{:S(2)}, u32[]{:S(2)}) collective-permute-start(bf16[2,12]{1,0:T(2,128)(2,1)S(1)} %get-tuple-element.598), channel_id=1, source_target_pairs={{16,0},{20,4},{24,8},{28,12},{17,1},{21,5},{25,9},{29,13},{18,2},{... | collective-permute-start | bytes 152 | tf_op jit(solution)/shard_map/ppermute | solution.py:30
  1470.4 121.1 %all-reduce.52.cloned.1.call-start = ((), (), s32[]{:S(2)}) async-start(), calls=%async_computation.12 | async-start | bytes 1572864 | tf_op jit(solution)/shard_map/psum | solution.py:434
  1556.6 204.8 %all-reduce.58.cloned.1.call-start = ((), (), s32[]{:S(2)}) async-start(), calls=%async_computation.21 | async-start | bytes 1572864
  1654.8 279.9 %all-reduce.68.cloned.1.call-start = ((), (), s32[]{:S(2)}) async-start(), calls=%async_computation.26 | async-start | bytes 2457600 | tf_op jit(solution)/shard_map/psum | solution.py:534
  1953.6 200.8 %all-reduce.60.cloned.1.call-start = ((), (), s32[]{:S(2)}) async-start(), calls=%async_computation.22 | async-start | bytes 1572864
  2046.2 293.8 %all-reduce.66.cloned.1.call-start = ((), (), s32[]{:S(2)}) async-start(), calls=%async_computation.25 | async-start | bytes 4030464 | tf_op jit(solution)/shard_map/psum | solution.py:382
  2288.2 178.0 %all-reduce.56.cloned.1.call-start = ((), (), s32[]{:S(2)}) async-start(), calls=%async_computation.16 | async-start | bytes 294912 | tf_op jit(solution)/shard_map/psum | solution.py:599
  2290.8 243.1 %reduce-scatter.25.cloned.1.call-start = ((), (), s32[]{:S(2)}) async-start(), calls=%async_computation.20 | async-start | bytes 589824
  2348.4 337.8 %reduce-scatter.23.cloned.1.call-start = ((), (), s32[]{:S(2)}) async-start(), calls=%async_computation.19 | async-start | bytes 9437184 | tf_op jit(solution)/shard_map/reduce_scatter | solution.py:586
  2356.1 482.0 %reduce-scatter.19.cloned.1.call-start = ((), (), s32[]{:S(2)}) async-start(), calls=%async_computation.17 | async-start | bytes 9437184 | tf_op jit(solution)/shard_map/reduce_scatter | solution.py:580
  2375.5 620.4 %reduce-scatter.17.cloned.1.call-start = ((), (), s32[]{:S(2)}) async-start(), calls=%async_computation.15 | async-start | bytes 9879552 | tf_op jit(solution)/shard_map/reduce_scatter | solution.py:577
  2392.4 888.8 %reduce-scatter.21.cloned.1.call-start = ((), (), s32[]{:S(2)}) async-start(), calls=%async_computation.18 | async-start | bytes 18874368 | tf_op jit(solution)/shard_map/reduce_scatter | solution.py:583
  2406.7 1113.8 %reduce-scatter.15.cloned.1.call-start = ((), (), s32[]{:S(2)}) async-start(), calls=%async_computation.14 | async-start | bytes 16515072 | tf_op jit(solution)/shard_map/reduce_scatter | solution.py:574
  (503 other events, 14663.3 us)
Sparse Core Ops, SparseCore 0:
  10.1 133.0 all-gather.7
  145.4 207.4 all-gather.5
  354.9 212.5 all-gather.9
  662.0 65.8 all-reduce.63
  729.9 227.6 all-gather.11
  959.6 123.5 all-gather.13
  1087.4 32.8 all-reduce.49
  1470.4 67.6 all-reduce.61
  1556.7 34.6 all-reduce.51
  1655.0 106.3 all-reduce.57
  1896.0 38.6 all-reduce.67
  1953.7 34.6 all-reduce.53
  2046.3 108.0 all-reduce.59
  2288.3 51.6 all-reduce.65
  2345.4 120.7 all-reduce.55
  2469.9 63.9 reduce-scatter.24
  2537.8 148.3 reduce-scatter.22
  2689.7 148.3 reduce-scatter.18
  2842.2 153.7 reduce-scatter.16
  3000.1 281.1 reduce-scatter.20
  3284.8 235.5 reduce-scatter.14
where the time goes:
time: 3550 us; the launch traced here: 3530 us
  waiting for transfers between devices  2420 us (68%)
  starting transfers between devices  283 us (8%)
  other arithmetic  269 us (8%)
  matrix products  229 us (6%)
  local copies, waits for them, and re-layouts  157 us (4%)
  blocking collectives  151 us (4%)
    ppermute x76, waiting for transfers between devices, shifted(): return lax.ppermute(block, axis, route)  493 us
    reduce_scatter x1, waiting for transfers between devices, local(): lax.psum_scatter(stacked_up.astype(jnp.bfloat16), 'ctx', scatter_dimensio...  282 us
    ppermute x76, starting transfers between devices, shifted(): return lax.ppermute(block, axis, route)  257 us
    reduce_scatter x1, waiting for transfers between devices, local(): lax.psum_scatter(stacked_mix.astype(jnp.bfloat16), 'ctx', scatter_dimensi...  235 us
    all_gather x1, waiting for transfers between devices, local(): lax.all_gather(up_weight, 'ctx', axis=1, tiled=True)  227 us
    reduce_scatter x1, waiting for transfers between devices, local(): lax.psum_scatter(stacked_share.astype(jnp.bfloat16), 'ctx', scatter_dimen...  155 us
    reduce_scatter x1, waiting for transfers between devices, local(): lax.psum_scatter(stacked_down.astype(jnp.bfloat16), 'ctx', scatter_dimens...  151 us
    reduce_scatter x1, waiting for transfers between devices, local(): lax.psum_scatter(stacked_out.astype(jnp.bfloat16), 'ctx', scatter_dimensi...  149 us
  transfers between devices with their start and end apart: 105, of which 54 were waited for; matrix products, arithmetic and copies ran while one was open for 13% of the time, Pallas kernels for 0%

commit v1 on v0

v1 whole, which is shorter than its diff:
```python
import jax
import jax.numpy as jnp
from jax import lax
from jax.sharding import Mesh
from jax.sharding import PartitionSpec as P

D = 2048
MH = 48
P_SIZE = 64
N = 256
CONV = 4
AH = 8
KVH = 2
HD = 128
FF = 4096
LAYERS = 2
HGROUPS = 4
CHUNK = 128

eps_norm = 1e-05
rope_base = 100000000000.0
highest = lax.Precision.HIGHEST
SWAP = [(0, 1), (1, 0)]
bf16 = jnp.bfloat16
f32 = jnp.float32


def matmul(left_op, right_op):
    return jnp.dot(left_op, right_op, preferred_element_type=f32)


def matmul_tn(left_op, right_op):
    return lax.dot_general(left_op, right_op, (((0,), (0,)), ((), ())), preferred_element_type=f32)


def matmul_nt(left_op, right_op):
    return lax.dot_general(left_op, right_op, (((1,), (1,)), ((), ())), preferred_element_type=f32)


def silu_grad(inputs):
    sigmoid = jax.nn.sigmoid(inputs)
    return sigmoid * (1.0 + inputs * (1.0 - sigmoid))


def pick(x, dim, index):
    return lax.dynamic_index_in_dim(x, index, dim, keepdims=False)


def rope_tables(positions):
    half_dim = HD // 2
    inverse = jnp.exp(-jnp.log(rope_base) * (2.0 * jnp.arange(half_dim, dtype=f32) / HD))
    angles = positions.astype(f32)[..., None] * inverse
    return jnp.cos(angles), jnp.sin(angles)


def rotate(values, tables, sign):
    cosine, sine = tables
    sine = sine * sign
    half_dim = HD // 2
    front = values[..., :half_dim]
    back = values[..., half_dim:]
    return jnp.concatenate([front * cosine - back * sine, back * cosine + front * sine], axis=-1)


def norm_piece(stream, gain_row):
    factor = lax.rsqrt(jnp.mean(stream * stream, axis=-1, keepdims=True) + eps_norm)
    return stream * factor * gain_row


def causal_conv(pre, taps, bias):
    length = pre.shape[0]
    padded = jnp.concatenate([jnp.zeros((CONV - 1, pre.shape[1]), pre.dtype), pre], axis=0)
    running = bias + taps[0] * padded[0:length]
    for offset in range(1, CONV):
        running = running + taps[offset] * padded[offset : offset + length]
    return jax.nn.silu(running)


def ssm_piece(x_pre, bc_pre, dt_raw, taps, shared_taps, params):
    length, width = x_pre.shape
    heads = dt_raw.shape[1]
    chunks = length // CHUNK
    x_conv = causal_conv(x_pre, taps[:CONV], taps[CONV]).reshape(chunks, CHUNK, heads, width // heads)
    bc_conv = causal_conv(bc_pre, shared_taps[:CONV], shared_taps[CONV]).reshape(chunks, CHUNK, 2 * N)
    b_conv, c_conv = bc_conv[..., :N], bc_conv[..., N:]
    step_size = jax.nn.softplus(dt_raw + params[1]).reshape(chunks, CHUNK, heads)
    decay_rate = -jnp.exp(params[0])
    cumulative = jnp.cumsum(step_size * decay_rate, axis=1)
    total_log = cumulative[:, -1]
    weight = jnp.exp(total_log[:, None, :] - cumulative) * step_size
    states = jnp.einsum("bsn,bshp->bhpn", b_conv, x_conv * weight[..., None], precision=highest)
    decay = jnp.exp(total_log)
    entering = [jnp.zeros_like(states[0])]
    for index in range(chunks - 1):
        entering.append(decay[index][:, None, None] * entering[-1] + states[index])
    entering = jnp.stack(entering)
    segment = cumulative[:, :, None, :] - cumulative[:, None, :, :]
    lower = (jnp.arange(CHUNK)[:, None] >= jnp.arange(CHUNK)[None, :])[None, :, :, None]
    decay_mat = jnp.where(lower, jnp.exp(jnp.where(lower, segment, 0.0)), 0.0)
    inner = jnp.einsum("btn,bsn->bts", c_conv, b_conv, precision=highest)
    mixing = decay_mat * inner[..., None] * step_size[:, None, :, :]
    local_part = jnp.einsum("btsh,bshp->bthp", mixing, x_conv, precision=highest)
    carried = (
        jnp.einsum("btn,bhpn->bthp", c_conv, entering, precision=highest)
        * jnp.exp(cumulative)[..., None]
    )
    return (local_part + carried + params[2][:, None] * x_conv).reshape(length, width)


def build(ctx_axes, tp_axes):
    half_axis = ctx_axes[0]
    group_axes = ctx_axes[1:]
    t_half, t_core = tp_axes
    ring_axes = group_axes + (t_half,)
    slot_axes = group_axes + tp_axes
    all_axes = ctx_axes + tp_axes
    span = len(ring_axes)

    def column_parts(width):
        unit = width // 128
        marks = [0] + [128 * (unit * (k + 1) // 3) for k in range(3)]
        return list(zip(marks[:-1], marks[1:]))

    def rotated(part):
        turn = part % span
        return ring_axes[turn:] + ring_axes[:turn]

    def gather_rows(x):
        rows, width = x.shape
        parts = []
        for part, (low, high) in enumerate(column_parts(width)):
            held = x[:, low:high].reshape((1,) * span + (rows, high - low))
            for axis in rotated(part):
                dim = ring_axes.index(axis)
                got = lax.ppermute(held, axis, SWAP)
                first = lax.axis_index(axis) == 0
                held = jnp.where(
                    first, jnp.concatenate([held, got], dim), jnp.concatenate([got, held], dim)
                )
            parts.append(held)
        held = jnp.concatenate(parts, -1).reshape(-1, 1, rows, width)
        got = lax.ppermute(held, t_core, SWAP)
        first = lax.axis_index(t_core) == 0
        held = jnp.where(first, jnp.concatenate([held, got], 1), jnp.concatenate([got, held], 1))
        return held.reshape(-1, width)

    def scatter_product(left, right):
        total = left.shape[0]
        width = right.shape[0]
        peers = 2 ** (span + 1)
        rows = total // peers
        split = left.reshape(peers // 2, 2, rows, left.shape[1])
        core = lax.axis_index(t_core)
        flat = (total // 2, left.shape[1])
        sent = matmul_nt(pick(split, 1, 1 - core).reshape(flat), right).astype(bf16)
        kept = matmul_nt(pick(split, 1, core).reshape(flat), right)
        held = kept + lax.ppermute(sent, t_core, SWAP).astype(f32)
        parts = []
        for part, (low, high) in enumerate(column_parts(width)):
            piece = held[:, low:high].reshape((2,) * span + (rows, high - low))
            names = list(ring_axes)
            for axis in rotated(part):
                dim = names.index(axis)
                names.pop(dim)
                index = lax.axis_index(axis)
                got = lax.ppermute(pick(piece, dim, 1 - index).astype(bf16), axis, SWAP)
                piece = pick(piece, dim, index) + got.astype(f32)
            parts.append(piece)
        return jnp.concatenate(parts, -1)

    def sum_over(x, axes):
        for axis in axes:
            x = x + lax.ppermute(x, axis, SWAP)
        return x

    def group_index():
        return lax.axis_index(group_axes)

    def group_swap(blocks):
        members = blocks.shape[0]
        me = group_index()
        came = [pick(blocks, 0, me)]
        for offset in range(1, members):
            route = [(i, i ^ offset) for i in range(members)]
            came.append(lax.ppermute(pick(blocks, 0, me ^ offset), group_axes, route))
        stacked = jnp.stack(came)
        shape = stacked.shape
        stacked = stacked.reshape((2,) * len(group_axes) + shape[1:])
        for dim, axis in enumerate(group_axes):
            stacked = jnp.where(lax.axis_index(axis) == 0, stacked, jnp.flip(stacked, dim))
        return stacked.reshape(shape)

    def spread(blocks):
        came = group_swap(blocks)
        other = lax.ppermute(came, half_axis, SWAP)
        first = lax.axis_index(half_axis) == 0
        return jnp.where(first, jnp.concatenate([came, other]), jnp.concatenate([other, came]))

    def collect(blocks):
        half = lax.axis_index(half_axis)
        paired = blocks.reshape((2, blocks.shape[0] // 2) + blocks.shape[1:])
        got = lax.ppermute(pick(paired, 0, 1 - half).astype(bf16), half_axis, SWAP)
        summed = pick(paired, 0, half).astype(f32) + got.astype(f32)
        return group_swap(summed.astype(bf16)).astype(f32)

    def local(
        hidden,
        cotangent,
        lengths,
        norm_gains,
        mix_weight,
        share_weight,
        chan_params,
        shared_conv,
        head_params,
        out_weight,
        up_weight,
        down_weight,
    ):
        members = 2 ** len(group_axes)
        ctx_count = 2 * members
        replicas = members // HGROUPS
        slot = lax.axis_index(half_axis)
        me = group_index()
        head_group = me // replicas
        head_part = me % replicas
        tp_half = lax.axis_index(t_half)
        tp_core = lax.axis_index(t_core)
        tp_index = tp_half * 2 + tp_core
        block_len = hidden.shape[2]
        depth = mix_weight.shape[1]
        seq_len = 2 * ctx_count * block_len
        own_len = 4 * block_len
        tp_heads = chan_params.shape[2] // P_SIZE
        heads = tp_heads // HGROUPS
        lanes = P_SIZE // replicas
        width = heads * lanes
        ssm_cols = tp_heads * P_SIZE
        qheads = AH // 4
        q_cols = qheads * HD
        ff_tp = FF // 4
        ff_own = ff_tp // members
        kv_cols = 2 * N
        dt_cols = 2 * N + 2 * KVH * HD
        kv_head = tp_index * qheads // (AH // KVH)
        score_scale = HD ** (-0.5)

        def block_of(member, half, cube):
            near = cube * members + member
            return jnp.where(half == 0, near, 2 * ctx_count - 1 - near)

        within = jnp.arange(block_len)
        own_pos = block_of(me, tp_half, tp_core) * block_len + within
        own_valid = (own_pos < lengths[slot]).astype(f32)[:, None]
        quarter = jnp.arange(4)
        query_pos = (
            block_of(me, quarter // 2, quarter % 2)[:, None] * block_len + within[None, :]
        ).reshape(own_len)
        key_pos = jnp.arange(seq_len)
        causal = key_pos[None, :] <= query_pos[:, None]
        key_tables = rope_tables(key_pos)
        query_tables = tuple(table[:, None] for table in rope_tables(query_pos))

        def to_sequence(x):
            blocks = x.reshape(members, 4, block_len, x.shape[1])
            parts = [blocks[:, 0], blocks[:, 1], blocks[::-1, 3], blocks[::-1, 2]]
            return jnp.concatenate([part.reshape(-1, x.shape[1]) for part in parts])

        def from_sequence(x):
            blocks = x.reshape(4, members, block_len, x.shape[1])
            parts = [blocks[0], blocks[1], blocks[3, ::-1], blocks[2, ::-1]]
            return jnp.stack(parts, axis=1).reshape(x.shape)

        def own_rows(x):
            return lax.dynamic_slice_in_dim(x, me * own_len, own_len, 0)

        def at_own_rows(x):
            return lax.dynamic_update_slice_in_dim(
                jnp.zeros((seq_len, x.shape[1]), x.dtype), x, me * own_len, 0
            )

        def bring_in(x):
            got = lax.ppermute(
                pick(pick(x, 0, 1 - slot), 0, tp_half), (half_axis, t_core), [(0, 2), (3, 1)]
            )
            return jnp.where(tp_core == slot, pick(pick(x, 0, slot), 0, tp_half), got)

        def bring_out(x):
            x = x.astype(bf16)
            got = lax.ppermute(x, (half_axis, t_core), [(1, 3), (2, 0)])
            pair = jnp.where(slot == 0, jnp.stack([x, got]), jnp.stack([got, x]))
            other = lax.ppermute(pair, t_core, SWAP)
            pair = jnp.where(tp_core == slot, pair, other)
            other = lax.ppermute(pair, t_half, SWAP)
            both = jnp.where(tp_half == 0, jnp.stack([pair, other], 1), jnp.stack([other, pair], 1))
            return both.astype(f32)

        def cut_heads(x, axis):
            shape = x.shape
            split = x.reshape(
                shape[:axis] + (HGROUPS, heads, replicas, lanes) + shape[axis + 1 :]
            )
            split = jnp.moveaxis(split, (axis, axis + 2), (0, 1))
            return split.reshape((members,) + shape[:axis] + (width,) + shape[axis + 1 :])

        def join_heads(x, axis):
            shape = x.shape[1:]
            split = x.reshape(
                (HGROUPS, replicas) + shape[:axis] + (heads, lanes) + shape[axis + 1 :]
            )
            split = jnp.moveaxis(split, (0, 1), (axis, axis + 2))
            return split.reshape(shape[:axis] + (ssm_cols,) + shape[axis + 1 :])

        def attend(queries, key_rows, value_rows):
            scores = jnp.einsum("qhd,kd->hqk", queries, key_rows, preferred_element_type=f32)
            scores = jnp.where(causal[None], scores * score_scale, -1e30)
            row_peak = jnp.max(scores, axis=-1, keepdims=True)
            exp_scores = jnp.exp(scores - row_peak)
            row_total = jnp.sum(exp_scores, axis=-1, keepdims=True)
            probability = (exp_scores / row_total).astype(bf16)
            attended = jnp.einsum(
                "hqk,kd->qhd", probability, value_rows, preferred_element_type=f32
            )
            return attended, row_peak + jnp.log(row_total)

        def attend_back(queries, key_rows, value_rows, logsum, grad_out):
            scores = jnp.einsum("qhd,kd->hqk", queries, key_rows, preferred_element_type=f32)
            scores = jnp.where(causal[None], scores * score_scale, -1e30)
            probability = jnp.exp(scores - logsum)
            probs_low = probability.astype(bf16)
            grad_probs = jnp.einsum(
                "qhd,kd->hqk", grad_out, value_rows, preferred_element_type=f32
            )
            inner_sum = jnp.sum(probability * grad_probs, axis=-1, keepdims=True)
            grad_scores = (probability * (grad_probs - inner_sum)).astype(bf16)
            grad_q = (
                jnp.einsum("hqk,kd->qhd", grad_scores, key_rows, preferred_element_type=f32)
                * score_scale
            )
            grad_k = (
                jnp.einsum("hqk,qhd->kd", grad_scores, queries, preferred_element_type=f32)
                * score_scale
            )
            grad_v = jnp.einsum("hqk,qhd->kd", probs_low, grad_out, preferred_element_type=f32)
            return grad_q, grad_k, grad_v

        stream = bring_in(hidden).astype(f32)
        gains = lax.all_gather(norm_gains, ctx_axes, axis=2, tiled=True).astype(f32)
        own_chan = pick(cut_heads(chan_params, 2), 0, me)
        own_heads = pick(head_params.reshape(LAYERS, 3, HGROUPS, heads), 2, head_group)
        share_rows = lax.dynamic_slice_in_dim(share_weight, tp_index * (depth // 4), depth // 4, 1)
        dt_start = dt_cols + tp_index * tp_heads + head_group * heads

        weights = []
        for layer in range(LAYERS):
            mix = mix_weight[layer]
            mix_blocks = jnp.concatenate(
                [cut_heads(mix[:, :ssm_cols], 1), cut_heads(mix[:, ssm_cols : 2 * ssm_cols], 1)], 2
            )
            mix_own = spread(mix_blocks).reshape(D, 2 * width)
            query_w = lax.all_gather(mix[:, 2 * ssm_cols :], ctx_axes, axis=0, tiled=True)
            share = lax.all_gather(share_rows[layer], all_axes, axis=0, tiled=True)
            key_w = lax.dynamic_slice_in_dim(share, kv_cols + kv_head * HD, HD, 1)
            value_w = lax.dynamic_slice_in_dim(share, kv_cols + (KVH + kv_head) * HD, HD, 1)
            dt_w = lax.dynamic_slice_in_dim(share, dt_start, heads, 1)
            in_w = jnp.concatenate(
                [mix_own, share[:, :kv_cols], key_w, value_w, query_w, dt_w], axis=1
            )
            out = out_weight[layer]
            out_own = jnp.moveaxis(spread(cut_heads(out[:ssm_cols], 0)), 0, 1).reshape(width, D)
            out_att = lax.all_gather(out[ssm_cols:], ctx_axes, axis=1, tiled=True)
            up_blocks = jnp.moveaxis(
                up_weight[layer].reshape(depth, 2, members, ff_own), 2, 0
            ).reshape(members, depth, 2 * ff_own)
            up_own = spread(up_blocks).reshape(D, 2 * ff_own)
            down_blocks = down_weight[layer].reshape(members, ff_own, depth)
            down_own = jnp.moveaxis(spread(down_blocks), 0, 1).reshape(ff_own, D)
            weights.append((in_w, jnp.concatenate([out_own, out_att]), up_own, down_own))

        cuts = [0, width, 2 * width]
        for size in (kv_cols, HD, HD, q_cols, heads):
            cuts.append(cuts[-1] + size)

        records = []
        for layer in range(LAYERS):
            in_w, out_w, up_w, down_w = weights[layer]
            rec = {}
            normed_f, rec["norm_one_back"] = jax.vjp(norm_piece, stream, gains[layer, 0])
            normed_rows = gather_rows(normed_f.astype(bf16))
            normed = to_sequence(normed_rows)
            mixed = matmul(normed, in_w)
            gate_z, x_pre, bc_pre, key_pre, value_pre, _, dt_raw = (
                mixed[:, low:high] for low, high in zip(cuts[:-1], cuts[1:])
            )
            q_pre = own_rows(from_sequence(mixed[:, cuts[5] : cuts[6]]))
            taps = own_chan[layer]
            ssm_y, rec["ssm_back"] = jax.vjp(
                ssm_piece, x_pre, bc_pre, dt_raw, taps[: CONV + 1], shared_conv[layer], own_heads[layer]
            )
            gated = ssm_y * jax.nn.silu(gate_z)
            squares = jnp.sum(gated * gated, axis=-1).reshape(-1, 128)
            sum_squares = sum_over(squares, (t_core,) + ring_axes[::-1]).reshape(seq_len, 1)
            gated_scale = lax.rsqrt(sum_squares / (MH * P_SIZE) + eps_norm)
            gated_low = (gated * taps[CONV + 1]).astype(bf16)
            scaled_low = (gated_low.astype(f32) * gated_scale).astype(bf16)
            queries = rotate(q_pre.reshape(own_len, qheads, HD), query_tables, 1.0).astype(bf16)
            key_rows = rotate(key_pre, key_tables, 1.0).astype(bf16)
            value_rows = value_pre.astype(bf16)
            attended, logsum = attend(queries, key_rows, value_rows)
            att_low = attended.reshape(own_len, q_cols).astype(bf16)
            mixer = jnp.concatenate([from_sequence(scaled_low), at_own_rows(att_low)], axis=1)
            middle = stream + scatter_product(mixer, out_w.T)
            normed_two_f, rec["norm_two_back"] = jax.vjp(norm_piece, middle, gains[layer, 1])
            normed_two = gather_rows(normed_two_f.astype(bf16))
            gate_up = matmul(normed_two, up_w)
            gate_vals, up_vals = gate_up[:, :ff_own], gate_up[:, ff_own:]
            activation = (jax.nn.silu(gate_vals) * up_vals).astype(bf16)
            stream = (middle + scatter_product(activation, down_w.T)) * own_valid
            rec.update(
                normed=normed, gate_z=gate_z, ssm_y=ssm_y, gated=gated, gated_low=gated_low,
                scaled_low=scaled_low, gated_scale=gated_scale, queries=queries, key_rows=key_rows,
                value_rows=value_rows, logsum=logsum, att_low=att_low, normed_two=normed_two,
                gate_vals=gate_vals, up_vals=up_vals, activation=activation,
            )
            records.append(rec)
        activations = bring_out(stream)

        grad_stream = bring_in(cotangent).astype(f32)
        out_grads = [None] * LAYERS
        for layer in reversed(range(LAYERS)):
            in_w, out_w, up_w, down_w = weights[layer]
            rec = records[layer]
            taps = own_chan[layer]
            grad_masked = grad_stream * own_valid
            grad_ffn = gather_rows(grad_masked.astype(bf16))
            grad_activation = matmul_nt(grad_ffn, down_w)
            grad_down = matmul_tn(rec["activation"], grad_ffn)
            gate_vals = rec["gate_vals"]
            grad_gate = grad_activation * rec["up_vals"] * silu_grad(gate_vals)
            grad_upper = grad_activation * jax.nn.silu(gate_vals)
            grad_gate_up = jnp.concatenate([grad_gate, grad_upper], axis=1).astype(bf16)
            grad_upw = matmul_tn(rec["normed_two"], grad_gate_up)
            grad_normed_two = scatter_product(grad_gate_up, up_w)
            grad_middle_norm, grad_gain_two = rec["norm_two_back"](grad_normed_two)
            grad_middle = grad_masked + grad_middle_norm
            branch_rows = gather_rows(grad_middle.astype(bf16))
            branch = to_sequence(branch_rows)
            branch_own = own_rows(branch_rows)
            grad_low_raw = matmul_nt(branch, out_w[:width])
            gated_scale = rec["gated_scale"]
            scale_part = jnp.sum(grad_low_raw * rec["gated_low"].astype(f32), axis=-1)
            grad_scale = sum_over(
                scale_part.reshape(-1, 128), (t_core,) + ring_axes[::-1]
            ).reshape(seq_len, 1)
            grad_squares = grad_scale * -0.5 * gated_scale * gated_scale * gated_scale / (MH * P_SIZE)
            grad_gated_low = gated_scale * grad_low_raw
            grad_out_ssm = matmul_tn(rec["scaled_low"], branch)
            grad_out_att = matmul_tn(rec["att_low"], branch_own)
            grad_att = matmul_nt(branch_own, out_w[width:]).astype(bf16)
            gated, gate_z = rec["gated"], rec["gate_z"]
            grad_gated = grad_gated_low * taps[CONV + 1] + 2.0 * grad_squares * gated
            grad_chan_gain = jnp.sum(grad_gated_low * gated, axis=0)
            grad_ssm_y = grad_gated * jax.nn.silu(gate_z)
            grad_z = grad_gated * rec["ssm_y"] * silu_grad(gate_z)
            grad_q, grad_k, grad_v = attend_back(
                rec["queries"], rec["key_rows"], rec["value_rows"], rec["logsum"],
                grad_att.reshape(own_len, qheads, HD),
            )
            grad_q = rotate(grad_q, query_tables, -1.0).reshape(own_len, q_cols).astype(bf16)
            grad_k = rotate(grad_k, key_tables, -1.0)
            grad_x, grad_bc, grad_dt, grad_taps, grad_conv, grad_heads = rec["ssm_back"](grad_ssm_y)
            grad_mix_own = jnp.concatenate([grad_z, grad_x], axis=1).astype(bf16)
            grad_share_part = jnp.concatenate([grad_bc, grad_k, grad_v], axis=1).astype(bf16)
            grad_dt = grad_dt.astype(bf16)
            grad_in = jnp.concatenate(
                [
                    from_sequence(jnp.concatenate([grad_mix_own, grad_share_part], axis=1)),
                    at_own_rows(grad_q),
                    from_sequence(grad_dt),
                ],
                axis=1,
            )
            grad_normed_one = scatter_product(grad_in, in_w)
            grad_stream_norm, grad_gain_one = rec["norm_one_back"](grad_normed_one)
            grad_stream = grad_middle + grad_stream_norm
            grad_share = jnp.zeros((seq_len, share_weight.shape[2]), bf16)
            grad_share = lax.dynamic_update_slice(grad_share, grad_share_part[:, :kv_cols], (0, 0))
            grad_share = lax.dynamic_update_slice(
                grad_share, grad_share_part[:, kv_cols : kv_cols + HD], (0, kv_cols + kv_head * HD)
            )
            grad_share = lax.dynamic_update_slice(
                grad_share, grad_share_part[:, kv_cols + HD :], (0, kv_cols + (KVH + kv_head) * HD)
            )
            grad_share = lax.dynamic_update_slice(grad_share, grad_dt, (0, dt_start))
            grad_share = lax.psum(grad_share, slot_axes)
            normed = rec["normed"]
            near = lax.dynamic_slice_in_dim(normed, (slot * members + me) * depth, depth, 1)
            far = lax.dynamic_slice_in_dim(normed, ((1 - slot) * members + me) * depth, depth, 1)
            share_far = lax.ppermute(matmul_tn(far, grad_share).astype(bf16), half_axis, SWAP)
            grad_sharew = matmul_tn(near, grad_share) + share_far.astype(f32)

            mix_blocks = matmul_tn(normed, grad_mix_own).reshape(ctx_count, depth, 2 * width)
            mix_came = collect(mix_blocks)
            normed_own = own_rows(from_sequence(normed))
            grad_query_w = lax.psum_scatter(
                matmul_tn(normed_own, grad_q).astype(bf16), ctx_axes, scatter_dimension=0, tiled=True
            ).astype(f32)
            grad_mixw = jnp.concatenate(
                [
                    join_heads(mix_came[:, :, :width], 1),
                    join_heads(mix_came[:, :, width:], 1),
                    grad_query_w,
                ],
                axis=1,
            )
            out_came = collect(jnp.moveaxis(grad_out_ssm.reshape(width, ctx_count, depth), 1, 0))
            grad_out_att = lax.psum_scatter(
                grad_out_att.astype(bf16), ctx_axes, scatter_dimension=1, tiled=True
            ).astype(f32)
            grad_outw = jnp.concatenate([join_heads(out_came, 0), grad_out_att], axis=0)
            up_came = collect(grad_upw.reshape(ctx_count, depth, 2 * ff_own))
            grad_upw = jnp.moveaxis(up_came.reshape(members, depth, 2, ff_own), 0, 2).reshape(
                depth, 2 * ff_tp
            )
            down_came = collect(jnp.moveaxis(grad_down.reshape(ff_own, ctx_count, depth), 1, 0))
            grad_down = down_came.reshape(ff_tp, depth)
            chan_grad = jnp.concatenate([grad_taps, grad_chan_gain[None]], axis=0)
            out_grads[layer] = (
                jnp.stack([grad_gain_one, grad_gain_two]), grad_mixw, grad_sharew, chan_grad,
                grad_conv, grad_heads, grad_outw, grad_upw, grad_down,
            )
        input_grad = bring_out(grad_stream)
        stacked = [
            jnp.stack([out_grads[layer][index] for layer in range(LAYERS)]) for index in range(9)
        ]
        gain_g, mix_g, share_g, chan_g, conv_g, head_g, out_g, up_g, down_g = stacked
        chan_rows = jnp.zeros((LAYERS, CONV + 2, HGROUPS, heads, replicas, lanes), f32)
        chan_rows = lax.dynamic_update_slice(
            chan_rows,
            chan_g.reshape(LAYERS, CONV + 2, 1, heads, 1, lanes),
            (0, 0, head_group, 0, head_part, 0),
        ).reshape(LAYERS, CONV + 2, ssm_cols)
        head_rows = lax.dynamic_update_slice(
            jnp.zeros((LAYERS, 3, HGROUPS, heads), f32), head_g[:, :, None], (0, 0, head_group, 0)
        ).reshape(LAYERS, 3, tp_heads)
        chan_sum, head_sum = lax.psum((chan_rows, head_rows), ctx_axes)
        conv_sum, gain_sum = lax.psum((conv_g, gain_g), all_axes)
        ctx_index = slot * members + me
        gain_own = lax.dynamic_slice_in_dim(gain_sum, ctx_index * depth, depth, 2)
        return (
            activations,
            input_grad,
            gain_own,
            mix_g,
            share_g,
            chan_sum,
            conv_sum,
            head_sum,
            out_g,
            up_g,
            down_g,
        )

    return local


def solution(mesh):
    ctx_bits = mesh.shape["ctx"].bit_length() - 1
    tp_bits = mesh.shape["tp"].bit_length() - 1
    ctx_axes = tuple(f"c{k}" for k in range(ctx_bits))
    tp_axes = tuple(f"t{k}" for k in range(tp_bits))
    fine = Mesh(mesh.devices.reshape((2,) * (ctx_bits + tp_bits)), ctx_axes + tp_axes)
    return jax.shard_map(
        build(ctx_axes, tp_axes),
        mesh=fine,
        in_specs=(
            P(None, None, ctx_axes, None),
            P(None, None, ctx_axes, None),
            P(),
            P(None, None, ctx_axes),
            P(None, ctx_axes, tp_axes),
            P(None, ctx_axes, None),
            P(None, None, tp_axes),
            P(),
            P(None, None, tp_axes),
            P(None, tp_axes, ctx_axes),
            P(None, ctx_axes, tp_axes),
            P(None, tp_axes, ctx_axes),
        ),
        out_specs=(
            P(None, None, ctx_axes, None),
            P(None, None, ctx_axes, None),
            P(None, None, ctx_axes),
            P(None, ctx_axes, tp_axes),
            P(None, ctx_axes, None),
            P(None, None, tp_axes),
            P(),
            P(None, None, tp_axes),
            P(None, tp_axes, ctx_axes),
            P(None, ctx_axes, tp_axes),
            P(None, tp_axes, ctx_axes),
        ),
        check_vma=False,
    )
```

time: 3550 us -> 1790 us (0.50)
  waiting for transfers between devices: 2420 us -> 659 us
  local copies, waits for them, and re-layouts: 157 us -> 288 us
  matrix products: 229 us -> 177 us
    reduce_scatter x5 -> x4, waiting for transfers between devices: 973 us -> 0.05 us  [the longest x2 0.02 us: local(): lax.psum_scatter(matmul_tn(normed_own, grad_q).astype(bf16), ctx_axes, sc...]
    all_gather x5 -> x6, waiting for transfers between devices: 584 us -> 0.01 us  [the longest x2 0.01 us: local(): share = lax.all_gather(share_rows[layer], all_axes, axis=0, tiled=True)]
    psum x8 -> x1, waiting for transfers between devices: 248 us -> 0.01 us  [local(): grad_share = lax.psum(grad_share, slot_axes)]
    ppermute x84 -> x250, waiting for transfers between devices: 497 us -> 658 us  [the longest x8 207 us: spread(): other = lax.ppermute(came, half_axis, SWAP)]
    unnamed x24 -> x11, waiting for transfers between devices: 120 us -> 0.18 us
    convert_element_type x88 -> x28, other arithmetic: 103 us -> 17 us  [the longest x10 9.6 us: collect(): return group_swap(summed.astype(bf16)).astype(f32)]
    all_gather x3 -> x1, blocking collectives: 96.9 us -> 20.8 us  [local(): gains = lax.all_gather(norm_gains, ctx_axes, axis=2, tiled=True).astype(f32)]
    dot_general x62 -> x38, matrix products: 139 us -> 78.1 us  [the longest x4 22.9 us: matmul(): return jnp.dot(left_op, right_op, preferred_element_type=f32)]
  transfers between devices with their start and end apart: 105 -> 261, of which waited for: 54 -> 133; matrix products, arithmetic and copies ran while one was open for 13% -> 34% of each run, Pallas kernels for 0% -> 0%
where the time goes in v1:
time: 1790 us; the launch traced here: 1780 us
  waiting for transfers between devices  659 us (37%)
  local copies, waits for them, and re-layouts  288 us (16%)
  other arithmetic  255 us (14%)
  starting transfers between devices  253 us (14%)
  matrix products  177 us (10%)
  blocking collectives  125 us (7%)
  between operations  23.5 us (1%)
    ppermute x8, waiting for transfers between devices, spread(): other = lax.ppermute(came, half_axis, SWAP)  207 us
    ppermute x8, waiting for transfers between devices, collect(): got = lax.ppermute(pick(paired, 0, 1 - half).astype(bf16), half_axis, SWAP)  115 us
    ppermute x48, waiting for transfers between devices, group_swap(): came.append(lax.ppermute(pick(blocks, 0, me ^ offset), group_axes, route))  92.2 us
    ppermute x72, waiting for transfers between devices, gather_rows(): got = lax.ppermute(held, axis, SWAP)  90 us
    ppermute x72, waiting for transfers between devices, scatter_product(): got = lax.ppermute(pick(piece, dim, 1 - index).astype(bf16), axis, SWAP)  87.7 us
    unnamed x986, local copies, waits for them, and re-layouts  86.9 us
    ppermute x72, starting transfers between devices, scatter_product(): got = lax.ppermute(pick(piece, dim, 1 - index).astype(bf16), axis, SWAP)  73.3 us
    ppermute x72, starting transfers between devices, gather_rows(): got = lax.ppermute(held, axis, SWAP)  68.7 us
  transfers between devices with their start and end apart: 261, of which 133 were waited for; matrix products, arithmetic and copies ran while one was open for 34% of the time, Pallas kernels for 0%

profile of v1, /device:TPU:0, one launch (start us, length us, event | category | flops | bytes accessed | tf_op | source)
XLA Modules:
  0.0 1780.2 jit_solution(8423475104072897151)
XLA Ops:
  32.3 20.8 %all_gather.21 = bf16[2,2,2048]{2,1,0:T(2,128)(2,1)S(1)} all-gather(bf16[2,2,256]{2,1,0:T(2,128)(2,1)S(1)} %copy-done.453), channel_id=1, replica_groups=mesh['c0'=2,'c1'=2,'c2'=2,'t0'=2,'t1'=2] {'c0','c1','c2'}, dimensions={2}, use_global_device_ids=true | all-gather | bytes 18432 | tf_op jit(solution)/shard_map/all_gather | solution.py:348
  123.2 53.4 %collective-permute-done.22 = bf16[4,192,256]{2,0,1:T(4,128)(2,1)S(1)} collective-permute-done((bf16[4,192,256]{2,0,1:T(4,128)(2,1)S(1)}, bf16[4,192,256]{2,0,1:T(4,128)(2,1)S(1)}, u32[]{:S(2)}, u32[]{:S(2)}) %collective-permute-start.22) | collective-permute-done | bytes 393248 | tf_op jit(solution)/shard_map/ppermute | solution.py:195
  202.6 8.0 fusion.495
  274.1 10.0 collective-permute-done.73
  284.1 7.4 collective-permute-done.72
  377.2 64.7 %collective-permute-done.82 = bf16[4,192,256]{2,0,1:T(4,128)(2,1)} collective-permute-done((bf16[4,192,256]{2,0,1:T(4,128)(2,1)}, bf16[4,192,256]{2,0,1:T(4,128)(2,1)}, u32[]{:S(2)}, u32[]{:S(2)}) %collective-permute-start.82) | collective-permute-done | bytes 393248 | tf_op jit(solution)/shard_map/ppermute | solution.py:195
  444.9 58.8 %collective-permute-done.50 = bf16[4,256,256]{1,2,0:T(8,128)(2,1)} collective-permute-done((bf16[4,256,256]{1,2,0:T(8,128)(2,1)}, bf16[4,256,256]{1,2,0:T(8,128)(2,1)}, u32[]{:S(2)}, u32[]{:S(2)}) %collective-permute-start.50) | collective-permute-done | bytes 524320 | tf_op jit(solution)/shard_map/ppermute | solution.py:195
  522.2 9.5 collective-permute-done.74
  533.3 20.8 %collective-permute-done.106 = bf16[4,256,512]{2,1,0:T(8,128)(2,1)S(1)} collective-permute-done((bf16[4,256,512]{2,1,0:T(8,128)(2,1)S(1)}, bf16[4,256,512]{2,1,0:T(8,128)(2,1)S(1)}, u32[]{:S(2)}, u32[]{:S(2)}) %collective-permute-start.106) | collective-permute-done | bytes 1048608 | tf_op jit(solution)/shard_map/ppermute | solution.py:195
  633.6 8.6 fusion.494
  826.8 63.0 %collective-permute-done.246 = bf16[4,256,256]{2,1,0:T(8,128)(2,1)S(1)} collective-permute-done((bf16[4,256,256]{2,1,0:T(8,128)(2,1)S(1)}, bf16[4,256,256]{2,1,0:T(8,128)(2,1)S(1)}, u32[]{:S(2)}, u32[]{:S(2)}) %collective-permute-start.246) | collective-permute-done | bytes 524320 | tf_op jit(solution)/shard_map/ppermute | solution.py:202
  1000.5 11.0 collective-permute-done.123
  1090.9 8.6 reduce_window_sum.40
  1166.3 14.2 collective-permute-done.233
  1189.4 8.3 collective-permute-done.220
  1201.5 6.4 collective-permute-done.160
  1274.8 43.3 %collective-permute-done.242 = bf16[4,256,256]{2,1,0:T(8,128)(2,1)S(1)} collective-permute-done((bf16[4,256,256]{2,1,0:T(8,128)(2,1)S(1)}, bf16[4,256,256]{2,1,0:T(8,128)(2,1)S(1)}, u32[]{:S(2)}, u32[]{:S(2)}) %collective-permute-start.242) | collective-permute-done | bytes 524320 | tf_op jit(solution)/shard_map/ppermute | solution.py:202
  1327.5 16.1 collective-permute-done.245
  1478.4 7.8 reduce_window_sum.42
  1541.8 62.8 %all-reduce.79 = (f32[2,6,768]{2,0,1:T(2,128)}, f32[2,3,12]{2,0,1:T(2,128)}) all-reduce(f32[2,6,768]{2,0,1:T(2,128)S(1)} %reshape.7954, f32[2,3,12]{2,0,1:T(2,128)S(1)} %reshape.7967), channel_id=1, replica_groups=mesh['c0'=2,'c1'=2,'c2'=2,'t0'=2,'t1'=2] {'c0','c1','c2'}, use_global_device_ids=true, to_apply=%region_67.69 | all-reduce | flops 9288 | bytes 74304 | tf_op jit(solution)/shard_map/psum | solution.py:546
  1631.9 5.9 convert_add_fusion
  1675.1 41.1 %all-reduce.78 = (f32[2,2,2048]{2,1,0:T(2,128)S(1)}, f32[2,5,512]{2,1,0:T(8,128)S(1)}) all-reduce(f32[2,2,2048]{2,1,0:T(2,128)S(1)} %pad_maximum_fusion.62, f32[2,5,512]{2,1,0:T(8,128)S(1)} %pad_maximum_fusion.63), channel_id=1, replica_groups=mesh['c0'=2,'c1'=2,'c2'=2,'t0'=2,'t1'=2] {'c0','c1','c2','t0','t1'}, use_global_device_ids=true, to_apply=%region_50.52 | all-reduce | flops 13312 | bytes 106496 | tf_op jit(solution)/shard_map/psum | solution.py:547
  1729.0 29.7 %collective-permute-done.225 = bf16[256,1072]{0,1:T(8,128)(2,1)S(1)} collective-permute-done((bf16[256,1072]{0,1:T(8,128)(2,1)S(1)}, bf16[256,1072]{0,1:T(8,128)(2,1)S(1)}, u32[]{:S(2)}, u32[]{:S(2)}) %collective-permute-start.225) | collective-permute-done | bytes 548896 | tf_op jit(solution)/shard_map/ppermute | solution.py:499
  1760.3 10.1 collective-permute-done.224
  (2367 shorter events, 1166.4 us)
Async XLA Ops:
  7.2 175.5 %all-gather.11.cloned.1.call-start = ((), (), s32[]{:S(2)}) async-start(), calls=%async_computation.4 | async-start | bytes 1179648 | tf_op jit(solution)/shard_map/all_gather | solution.py:361
  10.0 181.3 %all-gather.15.cloned.1.call-start = ((), (), s32[]{:S(2)}) async-start(), calls=%async_computation.10 | async-start | bytes 4866048 | tf_op jit(solution)/shard_map/all_gather | solution.py:362
  12.2 249.4 %all-gather.17.cloned.1.call-start = ((), (), s32[]{:S(2)}) async-start(), calls=%async_computation.11 | async-start | bytes 1179648 | tf_op jit(solution)/shard_map/all_gather | solution.py:371
  13.9 541.8 %all-gather.13.cloned.1.call-start = ((), (), s32[]{:S(2)}) async-start(), calls=%async_computation.5 | async-start | bytes 1179648 | tf_op jit(solution)/shard_map/all_gather | solution.py:361
  15.2 596.2 %all-gather.19.cloned.1.call-start = ((), (), s32[]{:S(2)}) async-start(), calls=%async_computation.12 | async-start | bytes 4866048 | tf_op jit(solution)/shard_map/all_gather | solution.py:362
  16.1 690.0 %all-gather.21.cloned.1.call-start = ((), (), s32[]{:S(2)}) async-start(), calls=%async_computation.13 | async-start | bytes 1179648 | tf_op jit(solution)/shard_map/all_gather | solution.py:371
  27.1 1221.6 %reduce-scatter.7.cloned.1.call-start = ((), (), s32[]{:S(2)}) async-start(), calls=%async_computation.7 | async-start | bytes 1179648 | tf_op jit(solution)/shard_map/reduce_scatter | solution.py:505
  115.6 144.9 %collective-permute-start.49 = (bf16[256,256]{1,0:T(8,128)(2,1)}, bf16[256,256]{1,0:T(8,128)(2,1)}, u32[]{:S(2)}, u32[]{:S(2)}) collective-permute-start(bf16[256,256]{1,0:T(8,128)(2,1)} %get-tuple-element.386), channel_id=1, source_target_pairs={{0,12},{4,8},{8,4},{12,0},{1,13},{5,9},{9,5},{13,1},{2,14},{6,10},... | collective-permute-start | bytes 393224 | tf_op jit(solution)/shard_map/ppermute | solution.py:185
  115.7 149.6 %collective-permute-start.48 = (bf16[256,256]{1,0:T(8,128)(2,1)}, bf16[256,256]{1,0:T(8,128)(2,1)}, u32[]{:S(2)}, u32[]{:S(2)}) collective-permute-start(bf16[256,256]{1,0:T(8,128)(2,1)} %get-tuple-element.387), channel_id=1, source_target_pairs={{0,8},{4,12},{8,0},{12,4},{1,9},{5,13},{9,1},{13,5},{2,10},{6,14},... | collective-permute-start | bytes 393224 | tf_op jit(solution)/shard_map/ppermute | solution.py:185
  176.6 89.1 %collective-permute-start.47 = (bf16[256,256]{1,0:T(8,128)(2,1)}, bf16[256,256]{1,0:T(8,128)(2,1)}, u32[]{:S(2)}, u32[]{:S(2)}) collective-permute-start(bf16[256,256]{1,0:T(8,128)(2,1)} %get-tuple-element.388), channel_id=1, source_target_pairs={{0,4},{4,0},{8,12},{12,8},{1,5},{5,1},{9,13},{13,9},{2,6},{6,2},{1... | collective-permute-start | bytes 393224 | tf_op jit(solution)/shard_map/ppermute | solution.py:185
  361.1 149.5 %collective-permute-start.42 = (bf16[8,1,48,2048]{3,2,1,0:T(8,128)(2,1)}, bf16[8,1,48,2048]{3,2,1,0:T(8,128)(2,1)}, u32[]{:S(2)}, u32[]{:S(2)}) collective-permute-start(bf16[8,1,48,2048]{3,2,1,0:T(8,128)(2,1)} %pad_maximum_fusion.15), channel_id=1, source_target_pairs={{0,1},{1,0},{2,3},{3,2},{4,5},{5,4},{6,7},{7,6},{8,9},{9,8},{10,11... | collective-permute-start | bytes 4718600 | tf_op jit(solution)/shard_map/ppermute | solution.py:142
  362.3 142.8 %collective-permute-start.46 = (bf16[4,256,512]{2,1,0:T(8,128)(2,1)}, bf16[4,256,512]{2,1,0:T(8,128)(2,1)}, u32[]{:S(2)}, u32[]{:S(2)}) collective-permute-start(bf16[4,256,512]{2,1,0:T(8,128)(2,1)} %bitcast.158), channel_id=1, source_target_pairs={{0,16},{16,0},{1,17},{17,1},{2,18},{18,2},{3,19},{19,3},{4,20},{20... | collective-permute-start | bytes 3145736 | tf_op jit(solution)/shard_map/ppermute | solution.py:195
  363.8 224.3 %collective-permute-start.124 = (bf16[48,2048]{1,0:T(8,128)(2,1)}, bf16[48,2048]{1,0:T(8,128)(2,1)}, u32[]{:S(2)}, u32[]{:S(2)}) collective-permute-start(bf16[48,2048]{1,0:T(8,128)(2,1)} %dynamic-slice_bitcast_fusion.18), channel_id=1, source_target_pairs={{0,16},{17,1},{2,18},{19,3},{4,20},{21,5},{6,22},{23,7},{8,24},{25... | collective-permute-start | bytes 589832 | tf_op jit(solution)/shard_map/ppermute | solution.py:283
  369.1 134.6 %collective-permute-start.50 = (bf16[4,256,256]{1,2,0:T(8,128)(2,1)}, bf16[4,256,256]{1,2,0:T(8,128)(2,1)}, u32[]{:S(2)}, u32[]{:S(2)}) collective-permute-start(bf16[4,256,256]{1,2,0:T(8,128)(2,1)} %bitcast.2039), channel_id=1, source_target_pairs={{0,16},{16,0},{1,17},{17,1},{2,18},{18,2},{3,19},{19,3},{4,20},{20... | collective-permute-start | bytes 1572872 | tf_op jit(solution)/shard_map/ppermute | solution.py:195
  623.1 92.9 %collective-permute-start.131 = (bf16[1,1,1,48,768]{4,3,2,1,0:T(8,128)(2,1)}, bf16[1,1,1,48,768]{4,3,2,1,0:T(8,128)(2,1)}, u32[]{:S(2)}, u32[]{:S(2)}) collective-permute-start(bf16[1,1,1,48,768]{4,3,2,1,0:T(8,128)(2,1)} %get-tuple-element.449), channel_id=1, source_target_pairs={{0,2},{2,0},{1,3},{3,1},{4,6},{6,4},{5,7},{7,5},{8,10},{10,8},{9,1... | collective-permute-start | bytes 221192 | tf_op jit(solution)/shard_map/ppermute | solution.py:135
  826.1 93.7 %collective-permute-start.135 = (bf16[384,2048]{1,0:T(8,128)(2,1)}, bf16[384,2048]{1,0:T(8,128)(2,1)}, u32[]{:S(2)}, u32[]{:S(2)}) collective-permute-start(bf16[384,2048]{1,0:T(8,128)(2,1)} %convolution_convert_fusion.5), channel_id=1, source_target_pairs={{0,1},{1,0},{2,3},{3,2},{4,5},{5,4},{6,7},{7,6},{8,9},{9,8},{10,11... | collective-permute-start | bytes 4718600 | tf_op jit(solution)/shard_map/ppermute | solution.py:157
  1031.8 218.7 %reduce-scatter.11.cloned.1.call-start = ((), (), s32[]{:S(2)}) async-start(), calls=%async_computation.9 | async-start | bytes 1179648 | tf_op jit(solution)/shard_map/reduce_scatter | solution.py:517
  1054.0 107.0 %collective-permute-start.230 = (bf16[4,192,256]{2,1,0:T(8,128)(2,1)}, bf16[4,192,256]{2,1,0:T(8,128)(2,1)}, u32[]{:S(2)}, u32[]{:S(2)}) collective-permute-start(bf16[4,192,256]{2,1,0:T(8,128)(2,1)} %fusion.197), channel_id=1, source_target_pairs={{0,16},{16,0},{1,17},{17,1},{2,18},{18,2},{3,19},{19,3},{4,20},{20... | collective-permute-start | bytes 1179656 | tf_op jit(solution)/shard_map/ppermute | solution.py:202
  1056.9 602.8 %reduce-scatter.5.cloned.1.call-start = ((), (), s32[]{:S(2)}) async-start(), calls=%async_computation.6 | async-start | bytes 1179648 | tf_op jit(solution)/shard_map/reduce_scatter | solution.py:505
  1273.4 120.9 %collective-permute-start.234 = (bf16[4,256,512]{2,1,0:T(8,128)(2,1)}, bf16[4,256,512]{2,1,0:T(8,128)(2,1)}, u32[]{:S(2)}, u32[]{:S(2)}) collective-permute-start(bf16[4,256,512]{2,1,0:T(8,128)(2,1)} %fusion.46), channel_id=1, source_target_pairs={{0,16},{16,0},{1,17},{17,1},{2,18},{18,2},{3,19},{19,3},{4,20},{20... | collective-permute-start | bytes 3145736 | tf_op jit(solution)/shard_map/ppermute | solution.py:202
  1434.0 232.1 %reduce-scatter.9.cloned.1.call-start = ((), (), s32[]{:S(2)}) async-start(), calls=%async_computation.8 | async-start | bytes 1179648 | tf_op jit(solution)/shard_map/reduce_scatter | solution.py:517
  1453.9 150.7 %collective-permute-start.226 = (bf16[4,192,256]{2,1,0:T(8,128)(2,1)}, bf16[4,192,256]{2,1,0:T(8,128)(2,1)}, u32[]{:S(2)}, u32[]{:S(2)}) collective-permute-start(bf16[4,192,256]{2,1,0:T(8,128)(2,1)} %fusion.196), channel_id=1, source_target_pairs={{0,16},{16,0},{1,17},{17,1},{2,18},{18,2},{3,19},{19,3},{4,20},{20... | collective-permute-start | bytes 1179656 | tf_op jit(solution)/shard_map/ppermute | solution.py:202
  1455.3 264.6 %all-reduce.83.cloned.1.call-start = ((), (), s32[]{:S(2)}) async-start(), calls=%async_computation.14 | async-start | bytes 6586368 | tf_op jit(solution)/shard_map/psum | solution.py:495
  1533.3 97.6 %collective-permute-start.203 = (bf16[384,2048]{1,0:T(8,128)(2,1)}, bf16[384,2048]{1,0:T(8,128)(2,1)}, u32[]{:S(2)}, u32[]{:S(2)}) collective-permute-start(bf16[384,2048]{1,0:T(8,128)(2,1)} %convolution_convert_fusion.2), channel_id=1, source_target_pairs={{0,1},{1,0},{2,3},{3,2},{4,5},{5,4},{6,7},{7,6},{8,9},{9,8},{10,11... | collective-permute-start | bytes 4718600 | tf_op jit(solution)/shard_map/ppermute | solution.py:157
  (716 other events, 7556.5 us)
Sparse Core Ops, SparseCore 0:
  10.1 46.5 all-gather.10
  59.6 83.5 all-gather.14
  145.3 51.5 all-gather.16
  198.8 38.3 all-gather.12
  239.9 76.0 all-gather.18
  317.9 45.1 all-gather.20
  1032.0 69.9 reduce-scatter.6
  1105.7 78.9 reduce-scatter.10
  1434.1 69.6 reduce-scatter.4
  1507.4 73.7 reduce-scatter.8
  1583.7 123.1 all-reduce.82

commit v2 on v1

v2 whole, which is shorter than its diff:
```python
import functools

import jax
import jax.numpy as jnp
from jax import lax
from jax.experimental import pallas as pl
from jax.experimental.pallas import tpu as pltpu
from jax.sharding import Mesh
from jax.sharding import PartitionSpec as P

D = 2048
MH = 48
P_SIZE = 64
N = 256
CONV = 4
AH = 8
KVH = 2
HD = 128
FF = 4096
LAYERS = 2
HGROUPS = 4
PAD = 8

eps_norm = 1e-05
rope_base = 100000000000.0
highest = lax.Precision.HIGHEST
SWAP = [(0, 1), (1, 0)]
bf16 = jnp.bfloat16
f32 = jnp.float32


def matmul(left_op, right_op):
    return jnp.dot(left_op, right_op, preferred_element_type=f32)


def matmul_tn(left_op, right_op):
    return lax.dot_general(left_op, right_op, (((0,), (0,)), ((), ())), preferred_element_type=f32)


def matmul_nt(left_op, right_op):
    return lax.dot_general(left_op, right_op, (((1,), (1,)), ((), ())), preferred_element_type=f32)


def product_tn_block(left, right, out):
    out[...] = dot_tn(left[...], right[...]).astype(bf16)


def product_tn(left, right):
    rows, m = left.shape
    n = right.shape[1]
    block = min(m, 1024 if rows <= 768 else 256)
    return pl.pallas_call(
        product_tn_block,
        grid=(m // block,),
        in_specs=[
            pl.BlockSpec((rows, block), lambda i: (0, i)),
            pl.BlockSpec((rows, n), lambda i: (0, 0)),
        ],
        out_specs=pl.BlockSpec((block, n), lambda i: (i, 0)),
        out_shape=jax.ShapeDtypeStruct((m, n), bf16),
        compiler_params=pltpu.CompilerParams(vmem_limit_bytes=30 * 2**20),
        cost_estimate=pl.CostEstimate(
            flops=2 * rows * m * n, bytes_accessed=2 * (rows * m + rows * n + m * n), transcendentals=0
        ),
    )(left, right)


def silu_grad(inputs):
    sigmoid = jax.nn.sigmoid(inputs)
    return sigmoid * (1.0 + inputs * (1.0 - sigmoid))


def after(x, point):
    return lax.optimization_barrier((x, point))[0]


def pick(x, dim, index):
    return lax.dynamic_index_in_dim(x, index, dim, keepdims=False)


def norm_piece(stream, gain_row):
    factor = lax.rsqrt(jnp.mean(stream * stream, axis=-1, keepdims=True) + eps_norm)
    return stream * factor * gain_row


def dot_nn(a, b):
    return lax.dot_general(a, b, (((1,), (0,)), ((), ())), preferred_element_type=f32)


def dot_nt(a, b):
    return lax.dot_general(a, b, (((1,), (1,)), ((), ())), preferred_element_type=f32)


def dot_tn(a, b):
    return lax.dot_general(a, b, (((0,), (0,)), ((), ())), preferred_element_type=f32)


def dot_exact(a, b):
    return lax.dot_general(
        a, b, (((1,), (0,)), ((), ())), precision=highest, preferred_element_type=f32
    )


def sigmoid(v):
    return 1.0 / (1.0 + jnp.exp(-v))


def block_place(block, members):
    quarter, at = block // members, block % members
    if quarter < 2:
        return at, 0, quarter
    return members - 1 - at, 1, 3 - quarter


class Plan:
    def __init__(self, seq_len, block_len, heads, lanes):
        self.seq_len = seq_len
        self.block_len = block_len
        self.heads = heads
        self.lanes = lanes
        self.width = heads * lanes
        self.members = seq_len // (4 * block_len)
        self.chunk = 4 * block_len
        self.chunks = seq_len // self.chunk
        self.query_parts = self.members // 2
        self.query_rows = seq_len // self.query_parts
        self.bc = 2 * N
        self.key_at = self.bc
        self.value_at = self.bc + HD
        self.q_at = self.bc + 2 * HD
        self.gate_at = self.bc + 3 * HD
        self.pair_cols = 2 * self.width
        self.pair_tiles = self.pair_cols + -self.pair_cols % 128
        self.step_at = self.gate_at + self.pair_tiles
        self.cols = self.step_at + 128

    def rows(self, core, block):
        member, half, place = block_place(block, self.members)
        other = core if place == 0 else 1 - core
        start = other * (self.seq_len // 2) + (2 * member + half) * self.block_len
        return pl.ds(pl.multiple_of(start, 16), self.block_len)

    def blocks(self):
        return range(self.seq_len // self.block_len)


def head_masks(plan):
    lane = lax.broadcasted_iota(jnp.int32, (1, plan.width), 1)
    return [
        ((lane >= h * plan.lanes) & (lane < (h + 1) * plan.lanes)).astype(f32)
        for h in range(plan.heads)
    ]


def over_heads(plan, tile, masks):
    return sum(tile[:, h : h + 1] * masks[h] for h in range(plan.heads))


def per_head(plan, values, masks):
    lane = lax.broadcasted_iota(jnp.int32, (1, 128), 1)
    total = None
    for h in range(plan.heads):
        column = jnp.sum(values * masks[h], axis=1, keepdims=True)
        part = column * (lane == h).astype(f32)
        total = part if total is None else total + part
    return total


def conv_values(source, taps_ref, rows, start, low, high):
    total = taps_ref[CONV : CONV + 1, low:high]
    for k in range(CONV):
        at = PAD + start - (CONV - 1) + k
        total = total + taps_ref[k : k + 1, low:high] * source[pl.ds(at, rows), low:high]
    return total


def prepare(plan, core, mixed, nat_bc, nat_x, nat_step):
    width = plan.width
    nat_bc[0:PAD, :] = jnp.zeros((PAD, plan.bc), f32)
    nat_x[0:PAD, :] = jnp.zeros((PAD, width), f32)
    for block in plan.blocks():
        at = PAD + block * plan.block_len
        rows = plan.rows(core, block)
        nat_bc[pl.ds(at, plan.block_len), :] = mixed[rows, 0 : plan.bc]
        pair = mixed[rows, plan.gate_at : plan.gate_at + plan.pair_tiles]
        nat_x[pl.ds(at, plan.block_len), :] = pltpu.roll(pair, plan.pair_tiles - width, 1)[:, :width]
        nat_step[pl.ds(at - PAD, plan.block_len), :] = mixed[rows, plan.step_at : plan.step_at + 128]


def chunk_decays(plan, nat_step, head_rows, c, tri):
    q = plan.chunk
    real = lax.broadcasted_iota(jnp.int32, (1, 128), 1) < plan.heads
    raw = jnp.where(real, nat_step[pl.ds(c * q, q), :] + head_rows[1:2, :], 0.0)
    step = jnp.where(real, jnp.maximum(raw, 0.0) + jnp.log(1.0 + jnp.exp(-jnp.abs(raw))), 0.0)
    cumulative = dot_exact(tri, step * head_rows[0:1, :])
    return raw, step, cumulative


def triangle(plan):
    q = plan.chunk
    row = lax.broadcasted_iota(jnp.int32, (q, q), 0)
    col = lax.broadcasted_iota(jnp.int32, (q, q), 1)
    return row, col


def ssm_forward(plan, core_ref, mixed, taps, shared_taps, head_rows, y_out, low_out, states_out, squares_out,
                nat_bc, nat_x, nat_step):
    q = plan.chunk
    masks = head_masks(plan)
    core = core_ref[0]
    prepare(plan, core, mixed, nat_bc, nat_x, nat_step)
    row, col = triangle(plan)
    lower = row >= col
    tri = lower.astype(f32)
    state = jnp.zeros((N, plan.width), f32)
    for c in range(plan.chunks):
        start = c * q
        x = conv_values(nat_x, taps, q, start, 0, plan.width)
        x = x * sigmoid(x)
        bc = conv_values(nat_bc, shared_taps, q, start, 0, plan.bc)
        bc = (bc * sigmoid(bc)).astype(bf16)
        b, cc = bc[:, :N], bc[:, N:]
        _, step, cum = chunk_decays(plan, nat_step, head_rows, c, tri)
        cum_rows = cum.T
        cum_full = over_heads(plan, cum, masks)
        total_full = cum_full[q - 1 : q, :]
        u = x * over_heads(plan, step, masks)
        inner = dot_nt(cc, b)
        states_out[c] = state
        y = dot_nn(cc, state.astype(bf16)) * jnp.exp(cum_full) + taps[6:7, :] * x
        for h in range(plan.heads):
            seg = jnp.where(lower, cum[:, h : h + 1] - cum_rows[h : h + 1, :], -1e30)
            mixing = (jnp.exp(seg) * inner).astype(bf16)
            y = y + dot_nn(mixing, (u * masks[h]).astype(bf16))
        weighted = (u * jnp.exp(total_full - cum_full)).astype(bf16)
        state = jnp.exp(total_full) * state + dot_tn(b, weighted)
        for k in range(4):
            block = 4 * c + k
            y_out[plan.rows(core, block), :] = y[k * plan.block_len : (k + 1) * plan.block_len, :]
    z = mixed[:, plan.gate_at : plan.gate_at + plan.width]
    gated = y_out[...] * (z * sigmoid(z))
    low_out[...] = (gated * taps[5:6, :]).astype(bf16)
    squares_out[...] = lax.dot_general(
        jnp.ones((8, plan.width), f32), gated * gated, (((1,), (1,)), ((), ())),
        precision=highest, preferred_element_type=f32,
    )


def ssm_backward(plan, core_ref, mixed, taps, shared_taps, head_rows, y_in, states, grad_mixer, scales,
                 bc_out, pair_out, step_out, taps_out, shared_out, heads_out,
                 nat_bc, nat_x, nat_step, nat_dy, grad_x, grad_bc, grad_y_ref):
    q = plan.chunk
    width = plan.width
    masks = head_masks(plan)
    core = core_ref[0]
    prepare(plan, core, mixed, nat_bc, nat_x, nat_step)
    row, col = triangle(plan)
    lower, upper = row >= col, row <= col
    strict_lower, strict_upper = row > col, row < col
    tri, tri_back = lower.astype(f32), upper.astype(f32)

    z = mixed[:, plan.gate_at : plan.gate_at + width]
    y = y_in[...]
    sig = sigmoid(z)
    silu = z * sig
    gated = y * silu
    scaled = grad_mixer[:, HD : HD + width] * scales[:, 0:1]
    grad_gated = scaled * taps[5:6, :] + scales[:, 1:2] * gated
    gain_grad = jnp.sum(scaled * gated, axis=0, keepdims=True)
    grad_z = grad_gated * y * (sig * (1.0 + z * (1.0 - sig)))
    spare = plan.pair_tiles - width
    pair_out[...] = jnp.concatenate(
        [grad_z, jnp.zeros((plan.seq_len, spare), f32)], axis=1
    ).astype(bf16)
    grad_y_ref[...] = grad_gated * silu
    for block in plan.blocks():
        at = block * plan.block_len
        nat_dy[pl.ds(at, plan.block_len), :] = grad_y_ref[plan.rows(core, block), :]

    grad_x[plan.seq_len : plan.seq_len + PAD, :] = jnp.zeros((PAD, width), f32)
    grad_bc[plan.seq_len : plan.seq_len + PAD, :] = jnp.zeros((PAD, plan.bc), f32)
    grad_state = jnp.zeros((N, width), f32)
    skip_grad = jnp.zeros((1, width), f32)
    rate_grad = jnp.zeros((1, 128), f32)
    bias_grad = jnp.zeros((1, 128), f32)
    for c in reversed(range(plan.chunks)):
        start = c * q
        x_lin = conv_values(nat_x, taps, q, start, 0, width)
        x_sig = sigmoid(x_lin)
        x = x_lin * x_sig
        bc_lin = conv_values(nat_bc, shared_taps, q, start, 0, plan.bc)
        bc_sig = sigmoid(bc_lin)
        bc = (bc_lin * bc_sig).astype(bf16)
        b, cc = bc[:, :N], bc[:, N:]
        raw, step, cum = chunk_decays(plan, nat_step, head_rows, c, tri)
        cum_rows = cum.T
        cum_full = over_heads(plan, cum, masks)
        total_full = cum_full[q - 1 : q, :]
        step_full = over_heads(plan, step, masks)
        u = x * step_full
        u_low = u.astype(bf16)
        dy = nat_dy[pl.ds(start, q), :]
        dy_low = dy.astype(bf16)
        state = states[c]
        state_low = state.astype(bf16)
        grad_state_low = grad_state.astype(bf16)
        entry = jnp.exp(cum_full)
        exit_w = jnp.exp(total_full - cum_full)
        total_decay = jnp.exp(total_full)
        dy_entry = (dy * entry).astype(bf16)
        grad_c = dot_nt(dy_entry, state_low)
        carried = dot_nn(cc, state_low) * entry
        du_state = dot_nn(b, grad_state_low) * exit_w
        grad_b = dot_nt((u * exit_w).astype(bf16), grad_state_low)
        inner = dot_nt(cc, b)
        inner_t = dot_nt(b, cc)
        du = du_state
        grad_inner = jnp.zeros((q, q), f32)
        grad_inner_t = jnp.zeros((q, q), f32)
        lane = lax.broadcasted_iota(jnp.int32, (1, 128), 1)
        dcum = per_head(plan, dy * carried - u * du_state, masks)
        for h in range(plan.heads):
            here = (lane == h).astype(f32)
            u_head = (u * masks[h]).astype(bf16)
            dy_head = (dy * masks[h]).astype(bf16)
            seg = cum[:, h : h + 1] - cum_rows[h : h + 1, :]
            decay = jnp.exp(jnp.where(lower, seg, -1e30))
            decay_t = jnp.exp(jnp.where(upper, -seg, -1e30))
            grad_mix = dot_nt(dy_head, u_low) * decay
            grad_mix_t = dot_nt(u_head, dy_low) * decay_t
            grad_inner = grad_inner + grad_mix
            grad_inner_t = grad_inner_t + grad_mix_t
            du = du + dot_nn((decay_t * inner_t).astype(bf16), dy_head)
            out_sum = jnp.sum(jnp.where(strict_lower, grad_mix * inner, 0.0), axis=1, keepdims=True)
            in_sum = jnp.sum(
                jnp.where(strict_upper, grad_mix_t * inner_t, 0.0), axis=1, keepdims=True
            )
            dcum = dcum + (out_sum - in_sum) * here
        grad_c = grad_c + dot_nn(grad_inner.astype(bf16), b)
        grad_b = grad_b + dot_nn(grad_inner_t.astype(bf16), cc)
        whole = jnp.sum(u * du_state, axis=0, keepdims=True) + jnp.sum(
            grad_state * state, axis=0, keepdims=True
        ) * total_decay
        dlog = dot_exact(tri_back, dcum) + per_head(plan, whole, masks)
        rate_grad = rate_grad + jnp.sum(dlog * step, axis=0, keepdims=True)
        grad_step = dlog * head_rows[0:1, :] + per_head(plan, du * x, masks)
        grad_raw = grad_step * sigmoid(raw)
        bias_grad = bias_grad + jnp.sum(grad_raw, axis=0, keepdims=True)
        grad_xc = du * step_full + taps[6:7, :] * dy
        skip_grad = skip_grad + jnp.sum(dy * x, axis=0, keepdims=True)
        grad_state = total_decay * grad_state + dot_tn(cc, dy_entry)
        grad_x[pl.ds(start, q), :] = grad_xc * (x_sig * (1.0 + x_lin * (1.0 - x_sig)))
        grad_bc[pl.ds(start, q), :] = jnp.concatenate([grad_b, grad_c], axis=1) * (
            bc_sig * (1.0 + bc_lin * (1.0 - bc_sig))
        )
        for k in range(4):
            step_out[plan.rows(core, 4 * c + k), :] = grad_raw[
                k * plan.block_len : (k + 1) * plan.block_len, :
            ].astype(bf16)

    size = plan.block_len
    tap_grads = [jnp.zeros((1, width), f32) for _ in range(CONV + 1)]
    shared_grads = [jnp.zeros((1, plan.bc), f32) for _ in range(CONV + 1)]
    lane = lax.broadcasted_iota(jnp.int32, (1, plan.pair_tiles), 1)
    for c in range(plan.chunks):
        start = c * q
        dx = grad_x[pl.ds(start, q), :]
        dbc = grad_bc[pl.ds(start, q), :]
        tap_grads[CONV] += jnp.sum(dx, axis=0, keepdims=True)
        shared_grads[CONV] += jnp.sum(dbc, axis=0, keepdims=True)
        pre_dx = None
        pre_dbc = None
        for k in range(CONV):
            at = PAD + start - (CONV - 1) + k
            tap_grads[k] += jnp.sum(dx * nat_x[pl.ds(at, q), :], axis=0, keepdims=True)
            shared_grads[k] += jnp.sum(dbc * nat_bc[pl.ds(at, q), :], axis=0, keepdims=True)
            ahead = start + (CONV - 1) - k
            part = taps[k : k + 1, :] * grad_x[pl.ds(ahead, q), :]
            pre_dx = part if k == 0 else pre_dx + part
            part = shared_taps[k : k + 1, :] * grad_bc[pl.ds(ahead, q), :]
            pre_dbc = part if k == 0 else pre_dbc + part
        tile = jnp.concatenate([pre_dx, jnp.zeros((q, spare), f32)], axis=1)
        tile = pltpu.roll(tile, width, 1).astype(bf16)
        for k in range(4):
            rows = plan.rows(core, 4 * c + k)
            pair_out[rows, :] = jnp.where(
                lane < width, pair_out[rows, :], tile[k * size : (k + 1) * size, :]
            )
            bc_out[rows, :] = pre_dbc[k * size : (k + 1) * size, :].astype(bf16)
    for k in range(CONV + 1):
        taps_out[k : k + 1, :] = tap_grads[k]
        shared_out[k : k + 1, :] = shared_grads[k]
    taps_out[5:6, :] = gain_grad
    taps_out[6:7, :] = skip_grad
    heads_out[0:1, :] = rate_grad * head_rows[0:1, :]
    heads_out[1:2, :] = bias_grad


def whole_specs(arrays):
    def spec(array):
        zeros = (0,) * len(array.shape)
        return pl.BlockSpec(array.shape, lambda i: zeros, pipeline_mode=pl.Buffered(1))

    return [spec(array) for array in arrays]


def call_whole(plan, kernel, outs, scratch, flops, inputs, scalars=()):
    return pl.pallas_call(
        kernel,
        grid=(1,),
        in_specs=[pl.BlockSpec(memory_space=pltpu.SMEM) for _ in scalars] + whole_specs(inputs),
        out_specs=tuple(whole_specs(outs)),
        out_shape=tuple(outs),
        scratch_shapes=scratch,
        compiler_params=ssm_params(plan),
        cost_estimate=pl.CostEstimate(
            flops=flops, bytes_accessed=plan.seq_len * 8192, transcendentals=0
        ),
    )(*scalars, *inputs)


def ssm_params(plan):
    limit = 30 * 2**20 if plan.seq_len <= 768 else 58 * 2**20
    return pltpu.CompilerParams(vmem_limit_bytes=limit)


def run_forward(plan, core, *inputs):
    t, w = plan.seq_len, plan.width
    outs = [
        jax.ShapeDtypeStruct((t, w), f32),
        jax.ShapeDtypeStruct((t, w), bf16),
        jax.ShapeDtypeStruct((plan.chunks, N, w), f32),
        jax.ShapeDtypeStruct((8, t), f32),
    ]
    scratch = [
        pltpu.VMEM((PAD + t, plan.bc), f32),
        pltpu.VMEM((PAD + t, w), f32),
        pltpu.VMEM((t, 128), f32),
    ]
    return call_whole(
        plan, functools.partial(ssm_forward, plan), outs, scratch, 40000 * t * w, inputs, (core,)
    )


def run_backward(plan, core, *inputs):
    t, w = plan.seq_len, plan.width
    outs = [
        jax.ShapeDtypeStruct((t, plan.bc), bf16),
        jax.ShapeDtypeStruct((t, plan.pair_tiles), bf16),
        jax.ShapeDtypeStruct((t, 128), bf16),
        jax.ShapeDtypeStruct((8, w), f32),
        jax.ShapeDtypeStruct((8, plan.bc), f32),
        jax.ShapeDtypeStruct((8, 128), f32),
    ]
    scratch = [
        pltpu.VMEM((PAD + t, plan.bc), f32),
        pltpu.VMEM((PAD + t, w), f32),
        pltpu.VMEM((t, 128), f32),
        pltpu.VMEM((t, w), f32),
        pltpu.VMEM((t + PAD, w), f32),
        pltpu.VMEM((t + PAD, plan.bc), f32),
        pltpu.VMEM((t, w), f32),
    ]
    return call_whole(
        plan, functools.partial(ssm_backward, plan), outs, scratch, 90000 * t * w, inputs, (core,)
    )


def attend_scores(plan, queries, keys, query_pos, key_pos):
    scores = dot_nt(queries, keys) * HD ** (-0.5)
    return jnp.where(key_pos <= query_pos, scores, -1e30)


def turned(x, cosine, sine):
    return x * cosine + pltpu.roll(x, HD // 2, 1) * sine


def attend_forward(plan, part, mixed, cosine, sine, query_pos, key_pos,
                   att_out, log_out, q_out, kv_out):
    rows = pl.ds(pl.multiple_of(part[0] * plan.query_rows, 8), plan.query_rows)
    keys = turned(mixed[:, plan.key_at : plan.key_at + HD], cosine[...], sine[...]).astype(bf16)
    values = mixed[:, plan.value_at : plan.value_at + HD].astype(bf16)
    kv_out[:, :HD] = keys
    kv_out[:, HD:] = values
    queries = mixed[rows, plan.q_at : plan.q_at + HD]
    queries = turned(queries, cosine[rows, :], sine[rows, :]).astype(bf16)
    q_out[...] = queries
    scores = attend_scores(plan, queries, keys, query_pos[rows, :], key_pos[...])
    peak = jnp.max(scores, axis=1, keepdims=True)
    weights = jnp.exp(scores - peak)
    total = jnp.sum(weights, axis=1, keepdims=True)
    probs = (weights / total).astype(bf16)
    att_out[...] = jnp.zeros((plan.seq_len, HD), bf16)
    att_out[rows, :] = dot_nn(probs, values).astype(bf16)
    log_out[...] = peak + jnp.log(total)


def attend_backward(plan, part, queries, kv, logs, grad_mixer, cosine, sine, query_pos, key_pos,
                    q_out, kv_out):
    rows = pl.ds(pl.multiple_of(part[0] * plan.query_rows, 8), plan.query_rows)
    keys, values = kv[:, :HD], kv[:, HD:]
    scale = HD ** (-0.5)
    q, grad = queries[...], grad_mixer[rows, :HD].astype(bf16)
    probs = jnp.exp(attend_scores(plan, q, keys, query_pos[rows, :], key_pos[...]) - logs[...])
    grad_probs = dot_nt(grad, values)
    inner = jnp.sum(probs * grad_probs, axis=1, keepdims=True)
    grad_scores = (probs * (grad_probs - inner)).astype(bf16)
    grad_q = dot_nn(grad_scores, keys) * scale
    q_out[...] = jnp.zeros((plan.seq_len, HD), bf16)
    q_out[rows, :] = turned(grad_q, cosine[rows, :], -sine[rows, :]).astype(bf16)
    grad_k = dot_tn(grad_scores, q) * scale
    kv_out[:, :HD] = turned(grad_k, cosine[...], -sine[...]).astype(bf16)
    kv_out[:, HD:] = dot_tn(probs.astype(bf16), grad).astype(bf16)


def run_attend(plan, part, *inputs):
    t, rows = plan.seq_len, plan.query_rows
    outs = [
        jax.ShapeDtypeStruct((t, HD), bf16),
        jax.ShapeDtypeStruct((rows, 1), f32),
        jax.ShapeDtypeStruct((rows, HD), bf16),
        jax.ShapeDtypeStruct((t, 2 * HD), bf16),
    ]
    kernel = functools.partial(attend_forward, plan)
    return call_whole(plan, kernel, outs, [], 4 * rows * t * HD, inputs, (part,))


def run_attend_back(plan, part, *inputs):
    t = plan.seq_len
    outs = [jax.ShapeDtypeStruct((t, HD), bf16), jax.ShapeDtypeStruct((t, 2 * HD), bf16)]
    kernel = functools.partial(attend_backward, plan)
    return call_whole(plan, kernel, outs, [], 10 * plan.query_rows * t * HD, inputs, (part,))


def build(ctx_axes, tp_axes):
    half_axis = ctx_axes[0]
    group_axes = ctx_axes[1:]
    t_half, t_core = tp_axes
    ring_axes = group_axes + (t_half,)
    slot_axes = group_axes + tp_axes
    all_axes = ctx_axes + tp_axes
    span = len(ring_axes)

    def column_parts(width):
        unit = width // 128
        marks = [0] + [128 * (unit * (k + 1) // 3) for k in range(3)]
        return list(zip(marks[:-1], marks[1:]))

    def rotated(part):
        turn = part % span
        return ring_axes[turn:] + ring_axes[:turn]

    def gather_rows(x):
        rows, width = x.shape
        parts = []
        for part, (low, high) in enumerate(column_parts(width)):
            held = x[:, low:high].reshape((1,) * span + (rows, high - low))
            for axis in rotated(part):
                dim = ring_axes.index(axis)
                got = lax.ppermute(held, axis, SWAP)
                first = lax.axis_index(axis) == 0
                held = jnp.where(
                    first, jnp.concatenate([held, got], dim), jnp.concatenate([got, held], dim)
                )
            parts.append(held)
        held = lax.optimization_barrier(jnp.concatenate(parts, -1).reshape(-1, width))
        return jnp.concatenate([held, lax.ppermute(held, t_core, SWAP)])

    def scatter_product(left, right, extra=None):
        total = left.shape[0]
        width = right.shape[0]
        peers = 2 ** (span + 1)
        rows = total // peers
        own = total // 2
        sent = matmul_nt(left[own:], right).astype(bf16)
        kept = matmul_nt(left[:own], right)
        if extra is not None:
            width += extra.shape[1]
            sent = jnp.concatenate([sent, extra[own:]], axis=1)
            kept = jnp.concatenate([kept, extra[:own].astype(f32)], axis=1)
        held = kept + lax.ppermute(sent, t_core, SWAP).astype(f32)
        parts = []
        for part, (low, high) in enumerate(column_parts(width)):
            piece = held[:, low:high].reshape((2,) * span + (rows, high - low))
            names = list(ring_axes)
            for axis in rotated(part):
                dim = names.index(axis)
                names.pop(dim)
                index = lax.axis_index(axis)
                got = lax.ppermute(pick(piece, dim, 1 - index).astype(bf16), axis, SWAP)
                piece = pick(piece, dim, index) + got.astype(f32)
            parts.append(piece)
        return jnp.concatenate(parts, -1)

    def sum_slot(x):
        turn = lax.axis_index(t_core) == 1
        x = x.reshape(2, -1, 128)
        x = jnp.where(turn, x[::-1], x)
        came = lax.all_to_all(
            jnp.broadcast_to(x[None], (2 ** (span + 1),) + x.shape), slot_axes, 0, 0, tiled=True
        )
        x = jnp.sum(came, axis=0)
        return jnp.where(turn, x[::-1], x).reshape(-1, 1)

    def sum_over(x, axes):
        for axis in axes:
            x = x + lax.ppermute(x, axis, SWAP)
        return x

    def group_index():
        return lax.axis_index(group_axes)

    def group_swap(blocks):
        return lax.all_to_all(blocks, group_axes, 0, 0, tiled=True)

    def both_halves(came):
        return lax.all_gather(came, half_axis, axis=0, tiled=True)

    def spread_first(blocks):
        return lax.all_to_all(jnp.concatenate([blocks, blocks]), ctx_axes, 0, 0, tiled=True)

    def fold_halves(blocks):
        return lax.psum_scatter(blocks.astype(bf16), half_axis, scatter_dimension=0, tiled=True)

    def fold_last(blocks):
        half = lax.axis_index(half_axis)
        paired = blocks.reshape((2, blocks.shape[0] // 2) + blocks.shape[1:])
        got = lax.ppermute(pick(paired, 0, 1 - half).astype(bf16), half_axis, SWAP)
        return pick(paired, 0, half).astype(f32), got

    def gather_lanes(x):
        for axis in ctx_axes[::-1]:
            got = lax.ppermute(x, axis, SWAP)
            first = lax.axis_index(axis) == 0
            x = jnp.where(first, jnp.concatenate([x, got], -1), jnp.concatenate([got, x], -1))
        return x

    def local(
        hidden,
        cotangent,
        lengths,
        norm_gains,
        mix_weight,
        share_weight,
        chan_params,
        shared_conv,
        head_params,
        out_weight,
        up_weight,
        down_weight,
    ):
        members = 2 ** len(group_axes)
        ctx_count = 2 * members
        replicas = members // HGROUPS
        slot = lax.axis_index(half_axis)
        me = group_index()
        head_group = me // replicas
        head_part = me % replicas
        tp_half = lax.axis_index(t_half)
        tp_core = lax.axis_index(t_core)
        tp_index = tp_half * 2 + tp_core
        block_len = hidden.shape[2]
        depth = mix_weight.shape[1]
        seq_len = 2 * ctx_count * block_len
        own_len = 4 * block_len
        tp_heads = chan_params.shape[2] // P_SIZE
        heads = tp_heads // HGROUPS
        lanes = P_SIZE // replicas
        width = heads * lanes
        ssm_cols = tp_heads * P_SIZE
        qheads = AH // 4
        q_cols = qheads * HD
        ff_tp = FF // 4
        ff_own = ff_tp // members
        plan = Plan(seq_len, block_len, heads, lanes)
        own_head = me // plan.query_parts
        core_scalar = tp_core.astype(jnp.int32).reshape(1)
        query_part = (me % plan.query_parts).astype(jnp.int32).reshape(1)
        share_cols = share_weight.shape[2]
        kv_cols = 2 * N
        dt_cols = 2 * N + 2 * KVH * HD
        kv_head = tp_index * qheads // (AH // KVH)
        score_scale = HD ** (-0.5)

        def block_of(member, half, cube):
            near = cube * members + member
            return jnp.where(half == 0, near, 2 * ctx_count - 1 - near)

        within = jnp.arange(block_len)
        own_pos = block_of(me, tp_half, tp_core) * block_len + within
        own_valid = (own_pos < lengths[slot]).astype(f32)[:, None]
        ring = jnp.arange(2 * members)

        def core_positions(core):
            first = block_of(ring // 2, ring % 2, core) * block_len
            return (first[:, None] + within[None, :]).reshape(-1)

        key_pos = jnp.concatenate([core_positions(tp_core), core_positions(1 - tp_core)])
        half_dim = HD // 2
        inverse = jnp.exp(-jnp.log(rope_base) * (2.0 * jnp.arange(half_dim, dtype=f32) / HD))
        angles = key_pos.astype(f32)[:, None] * inverse
        cosine = jnp.concatenate([jnp.cos(angles)] * 2, axis=1)
        sine = jnp.concatenate([-jnp.sin(angles), jnp.sin(angles)], axis=1)

        tables = (cosine, sine, key_pos[:, None], key_pos[None, :])

        def cut_query_heads(x, axis):
            shape = x.shape
            split = x.reshape(shape[:axis] + (qheads, HD) + shape[axis + 1 :])
            return jnp.repeat(jnp.moveaxis(split, axis, 0), plan.query_parts, axis=0)

        def join_query_heads(x, axis):
            summed = jnp.sum(x.astype(f32).reshape((qheads, plan.query_parts) + x.shape[1:]), axis=1)
            joined = jnp.moveaxis(summed, 0, axis)
            shape = joined.shape
            return joined.reshape(shape[:axis] + (q_cols,) + shape[axis + 2 :])

        def bring_in(x):
            got = lax.ppermute(
                pick(pick(x, 0, 1 - slot), 0, tp_half), (half_axis, t_core), [(0, 2), (3, 1)]
            )
            return jnp.where(tp_core == slot, pick(pick(x, 0, slot), 0, tp_half), got)

        def bring_out(x, points=None):
            x = x.astype(bf16)
            got = lax.ppermute(x, (half_axis, t_core), [(1, 3), (2, 0)])
            if points is not None:
                got = after(got, points[0])
            pair = jnp.where(slot == 0, jnp.stack([x, got]), jnp.stack([got, x]))
            other = lax.ppermute(pair, t_core, SWAP)
            pair = jnp.where(tp_core == slot, pair, other)
            other = lax.ppermute(pair, t_half, SWAP)
            if points is not None:
                other = after(other, points[1])
            both = jnp.where(tp_half == 0, jnp.stack([pair, other], 1), jnp.stack([other, pair], 1))
            return both.astype(f32)

        def cut_heads(x, axis):
            shape = x.shape
            split = x.reshape(
                shape[:axis] + (HGROUPS, heads, replicas, lanes) + shape[axis + 1 :]
            )
            split = jnp.moveaxis(split, (axis, axis + 2), (0, 1))
            return split.reshape((members,) + shape[:axis] + (width,) + shape[axis + 1 :])

        def join_heads(x, axis):
            if replicas == 1:
                return jnp.concatenate([x[g] for g in range(members)], axis=axis)
            shape = x.shape[1:]
            split = x.reshape(
                (HGROUPS, replicas) + shape[:axis] + (heads, lanes) + shape[axis + 1 :]
            )
            split = jnp.moveaxis(split, (0, 1), (axis, axis + 2))
            return split.reshape(shape[:axis] + (ssm_cols,) + shape[axis + 1 :])

        gains = gather_lanes(norm_gains).astype(f32)
        hidden_rows = bring_in(after(hidden, gains))
        stream = hidden_rows.astype(f32)
        own_chan = pick(cut_heads(chan_params, 2), 0, me)
        own_heads = pick(head_params.reshape(LAYERS, 3, HGROUPS, heads), 2, head_group)
        skip_full = jnp.repeat(own_heads[:, 2], lanes, axis=1)[:, None]
        tap_rows = jnp.concatenate([own_chan, skip_full, jnp.zeros_like(skip_full)], axis=1)
        shared_rows = jnp.pad(shared_conv, ((0, 0), (0, 3), (0, 0)))
        head_rows = jnp.pad(
            jnp.stack([-jnp.exp(own_heads[:, 0]), own_heads[:, 1]], axis=1),
            ((0, 0), (0, 6), (0, 128 - heads)),
        )
        share_rows = lax.dynamic_slice_in_dim(share_weight, tp_core * (depth // 2), depth // 2, 1)
        dt_start = dt_cols + tp_index * tp_heads + head_group * heads

        def weight_blocks(layer):
            mix = mix_weight[layer]
            mix_blocks = jnp.concatenate(
                [
                    cut_query_heads(mix[:, 2 * ssm_cols :], 1),
                    cut_heads(mix[:, :ssm_cols], 1),
                    cut_heads(mix[:, ssm_cols : 2 * ssm_cols], 1),
                ],
                2,
            )
            out = out_weight[layer].T
            out_blocks = jnp.concatenate(
                [cut_query_heads(out[:, ssm_cols:], 1), cut_heads(out[:, :ssm_cols], 1)], 2
            )
            up = up_weight[layer]
            down = down_weight[layer].T
            ffn_blocks = jnp.stack(
                [
                    jnp.concatenate(
                        [
                            up[:, g * ff_own : (g + 1) * ff_own],
                            up[:, ff_tp + g * ff_own : ff_tp + (g + 1) * ff_own],
                            down[:, g * ff_own : (g + 1) * ff_own],
                        ],
                        axis=1,
                    )
                    for g in range(members)
                ]
            )
            return mix_blocks, out_blocks, ffn_blocks

        def share_whole(share):
            share = jnp.concatenate(
                [
                    share[:, :kv_cols],
                    lax.dynamic_slice_in_dim(share, kv_cols + kv_head * HD, HD, 1),
                    lax.dynamic_slice_in_dim(share, kv_cols + (KVH + kv_head) * HD, HD, 1),
                    share[:, dt_cols:],
                ],
                axis=1,
            )
            return lax.all_gather(share, ctx_axes + (t_core,), axis=0, tiled=True)

        def input_weights(mix_own, share):
            dt_w = lax.dynamic_slice_in_dim(share, kv_cols + 2 * HD + dt_start - dt_cols, heads, 1)
            return jnp.concatenate(
                [
                    share[:, : plan.q_at],
                    jnp.pad(
                        mix_own.reshape(D, HD + 2 * width),
                        ((0, 0), (0, plan.pair_tiles - plan.pair_cols)),
                    ),
                    jnp.pad(dt_w, ((0, 0), (0, 128 - heads))),
                ],
                axis=1,
            )

        def ffn_weights(ffn_own):
            ffn_own = ffn_own.reshape(D, 3 * ff_own)
            return ffn_own[:, : 2 * ff_own], ffn_own[:, 2 * ff_own :]

        blocks = [weight_blocks(layer) for layer in range(LAYERS)]
        mix_own = [None] * LAYERS
        out_own = [None] * LAYERS
        ffn_own = [None] * LAYERS
        shares = [None] * LAYERS
        blocks = after(blocks, hidden_rows)
        mix_own[0] = spread_first(blocks[0][0])
        swapped = [[group_swap(x) for x in blocks[layer][layer == 0 :]] for layer in range(LAYERS)]
        for layer in range(LAYERS):
            if layer > 0:
                mix_own[layer] = both_halves(swapped[layer][0])
            shares[layer] = share_whole(share_rows[layer])
            out_own[layer] = both_halves(swapped[layer][-2])
            ffn_own[layer] = both_halves(swapped[layer][-1])

        records = []
        for layer in range(LAYERS):
            rec = {}
            normed_f, rec["norm_one_back"] = jax.vjp(norm_piece, stream, gains[layer, 0])
            if layer == 0:
                normed = norm_piece(gather_rows(hidden_rows).astype(f32), gains[0, 0]).astype(bf16)
            else:
                normed = gather_rows(normed_f.astype(bf16))
            in_w = input_weights(*after((mix_own[layer], shares[layer]), normed))
            mixed = matmul(normed, in_w)
            ssm_y, gated_low, states, squares = run_forward(
                plan, core_scalar, mixed, tap_rows[layer], shared_rows[layer], head_rows[layer]
            )
            sum_squares = sum_slot(squares[0])
            gated_scale = lax.rsqrt(sum_squares / (MH * P_SIZE) + eps_norm)
            scaled_low = (gated_low.astype(f32) * gated_scale).astype(bf16)
            attended, logsum, queries, keyval = run_attend(plan, query_part, mixed, *tables)
            mixer = jnp.concatenate([attended, scaled_low], axis=1)
            out_w = after(out_own[layer], gated_low).reshape(D, HD + width)
            middle = stream + scatter_product(mixer, out_w)
            normed_two_f, rec["norm_two_back"] = jax.vjp(norm_piece, middle, gains[layer, 1])
            normed_two = gather_rows(normed_two_f.astype(bf16))
            up_w, down_w = ffn_weights(after(ffn_own[layer], normed_two))
            gate_up = matmul(normed_two, up_w)
            gate_vals, up_vals = gate_up[:, :ff_own], gate_up[:, ff_own:]
            activation = (jax.nn.silu(gate_vals) * up_vals).astype(bf16)
            stream = (middle + scatter_product(activation, down_w)) * own_valid
            rec.update(
                normed=normed, mixed=mixed, ssm_y=ssm_y, gated_low=gated_low, states=states,
                mixer=mixer, gated_scale=gated_scale, queries=queries, keyval=keyval,
                logsum=logsum, normed_two=normed_two,
                gate_vals=gate_vals, up_vals=up_vals, activation=activation,
            )
            rec["weights"] = (in_w, out_w, up_w, down_w)
            records.append(rec)

        grad_stream = bring_in(cotangent).astype(f32)
        out_grads = [None] * LAYERS
        share_sums = []
        folded = [None] * LAYERS
        points = []
        came = [[] for _ in range(LAYERS)]
        for layer in reversed(range(LAYERS)):
            rec = records[layer]
            in_w, out_w, up_w, down_w = rec["weights"]
            grad_masked = grad_stream * own_valid
            if layer == LAYERS - 1:
                grad_ffn = gather_rows(grad_masked.astype(bf16))
            else:
                gathered = jnp.concatenate([grad_masked, share_own], axis=1).astype(bf16)
                gathered = gather_rows(after(gathered, folded[layer + 1][1]))
                grad_ffn = gathered[:, :D]
                share_sums.append(gathered[:, D:])
            points.append([grad_ffn])
            grad_activation = matmul(grad_ffn, down_w)
            grad_down = product_tn(grad_ffn, rec["activation"])
            gate_vals = rec["gate_vals"]
            grad_gate = grad_activation * rec["up_vals"] * silu_grad(gate_vals)
            grad_upper = grad_activation * jax.nn.silu(gate_vals)
            grad_gate_up = jnp.concatenate([grad_gate, grad_upper], axis=1).astype(bf16)
            if layer + 1 < LAYERS:
                came[layer + 1].append(
                    after(group_swap(after(folded[layer + 1][0], grad_ffn)), grad_gate_up)
                )
            grad_upw = product_tn(rec["normed_two"], grad_gate_up)
            grad_normed_two = scatter_product(grad_gate_up, up_w)
            grad_middle_norm, grad_gain_two = rec["norm_two_back"](grad_normed_two)
            grad_middle = grad_masked + grad_middle_norm
            ffn_blocks = jnp.concatenate([grad_upw, grad_down], axis=1).reshape(
                ctx_count, depth, 3 * ff_own
            )
            folded[layer] = [fold_halves(ffn_blocks)]
            branch_rows = gather_rows(after(grad_middle.astype(bf16), ffn_blocks))
            points[-1].append(branch_rows)
            grad_mixer = matmul(branch_rows, out_w)
            out_blocks = product_tn(branch_rows, rec["mixer"]).reshape(
                ctx_count, depth, HD + width
            )
            folded[layer].append(fold_halves(out_blocks))
            gated_scale = rec["gated_scale"]
            scale_part = jnp.sum(grad_mixer[:, HD:] * rec["gated_low"].astype(f32), axis=-1)
            grad_scale = after(sum_slot(scale_part), out_blocks)
            grad_squares = grad_scale * -0.5 * gated_scale * gated_scale * gated_scale / (MH * P_SIZE)
            grad_mixer_here = grad_mixer
            if layer + 1 < LAYERS:
                earlier = after(folded[layer + 1][1:], branch_rows)
                came[layer + 1] += [group_swap(x) for x in earlier]
                grad_mixer_here = after(grad_mixer, came[layer + 1][1:])
            grad_q, grad_kv = run_attend_back(
                plan, query_part, rec["queries"], rec["keyval"], rec["logsum"], grad_mixer_here,
                *tables,
            )
            grad_bc, grad_pair, grad_step, taps_grad, grad_conv, heads_grad = run_backward(
                plan, core_scalar, rec["mixed"], tap_rows[layer], shared_rows[layer], head_rows[layer],
                rec["ssm_y"], rec["states"], grad_mixer,
                jnp.concatenate([gated_scale, 2.0 * grad_squares], axis=1),
            )
            chan_grad = taps_grad[: CONV + 2]
            grad_conv = grad_conv[: CONV + 1]
            grad_heads = jnp.concatenate(
                [heads_grad[:2, :heads], jnp.sum(taps_grad[6].reshape(heads, lanes), axis=1)[None]]
            )
            grad_mix_own = jnp.concatenate([grad_q, grad_pair], axis=1)
            grad_in = jnp.concatenate([grad_bc, grad_kv, grad_mix_own, grad_step], axis=1)
            grad_in = after(grad_in, folded[layer][0])
            at_heads = [
                jnp.where(kv_head == head, grad_kv[:, part * HD : (part + 1) * HD], 0)
                for part in range(2)
                for head in range(KVH)
            ]
            step_cols = lax.dynamic_update_slice(
                jnp.zeros((seq_len, 128), bf16), grad_step[:, :heads], (0, dt_start - dt_cols)
            )
            grad_share = jnp.concatenate([grad_bc] + at_heads + [step_cols], axis=1)
            scattered = scatter_product(grad_in, in_w, grad_share)
            grad_normed_one, share_own = scattered[:, :D], scattered[:, D:]
            points[-1] += [grad_in, grad_normed_one]
            grad_stream_norm, grad_gain_one = rec["norm_one_back"](grad_normed_one)
            grad_stream = grad_middle + grad_stream_norm
            grad_mix = product_tn(rec["normed"], grad_mix_own)[:, : HD + 2 * width]
            fold = fold_last if layer == 0 else fold_halves
            folded[layer].append(fold(grad_mix.reshape(ctx_count, depth, HD + 2 * width)))
            out_grads[layer] = (
                jnp.stack([grad_gain_one, grad_gain_two]), chan_grad, grad_conv, grad_heads,
            )
        share_sums.append(gather_rows(share_own.astype(bf16)))
        last = points[-1]
        activations = bring_out(stream, (points[0][1], last[1]))
        share_grads = []
        for layer in range(LAYERS):
            normed = records[layer]["normed"]
            grad_share = share_sums[LAYERS - 1 - layer]
            near = lax.dynamic_slice_in_dim(normed, (slot * members + me) * depth, depth, 1)
            far = lax.dynamic_slice_in_dim(normed, ((1 - slot) * members + me) * depth, depth, 1)
            share_far = lax.ppermute(product_tn(far, grad_share), half_axis, SWAP)
            if layer > 0:
                share_far = after(share_far, last[3])
            share_sum = product_tn(near, grad_share).astype(f32) + share_far.astype(f32)
            share_grads.append(share_sum[:, :share_cols])
        share_g = jnp.stack(share_grads)
        input_grad = bring_out(grad_stream)

        mix_kept, mix_got = folded[0][2]
        mix_sum = (mix_kept + after(mix_got, share_sums[-1]).astype(f32)).astype(bf16)
        came[0] = [
            group_swap(after(folded[0][0], last[3])),
            group_swap(after(folded[0][1], last[3])),
            group_swap(mix_sum),
        ]

        def weight_grads(layer):
            got = came[layer] if layer == 0 else after(came[layer], last[3])
            ffn_came, out_came, mix_came = got
            mix = jnp.concatenate(
                [
                    join_heads(mix_came[:, :, HD : HD + width], 1),
                    join_heads(mix_came[:, :, HD + width :], 1),
                    join_query_heads(mix_came[:, :, :HD], 1),
                ],
                axis=1,
            ).astype(f32)
            out = jnp.concatenate(
                [join_heads(out_came[:, :, HD:], 1), join_query_heads(out_came[:, :, :HD], 1)],
                axis=1,
            )
            up = jnp.concatenate(
                [
                    ffn_came[g, :, part * ff_own : (part + 1) * ff_own]
                    for part in range(2)
                    for g in range(members)
                ],
                axis=1,
            ).astype(f32)
            down = jnp.concatenate([ffn_came[g, :, 2 * ff_own :] for g in range(members)], axis=1)
            return mix, out.T.astype(f32), up, down.T.astype(f32)

        by_layer = [weight_grads(layer) for layer in range(LAYERS)]
        mix_g, out_g, up_g, down_g = (jnp.stack(grads) for grads in zip(*by_layer))
        gain_g, chan_g, conv_g, head_g = (jnp.stack(grads) for grads in zip(*out_grads))
        chan_rows = jnp.zeros((LAYERS, CONV + 2, HGROUPS, heads, replicas, lanes), f32)
        chan_rows = lax.dynamic_update_slice(
            chan_rows,
            chan_g.reshape(LAYERS, CONV + 2, 1, heads, 1, lanes),
            (0, 0, head_group, 0, head_part, 0),
        ).reshape(LAYERS, CONV + 2, ssm_cols)
        head_rows = lax.dynamic_update_slice(
            jnp.zeros((LAYERS, 3, HGROUPS, heads), f32), head_g[:, :, None], (0, 0, head_group, 0)
        ).reshape(LAYERS, 3, tp_heads)

        def packed(arrays):
            flat = jnp.concatenate([a.reshape(-1) for a in arrays])
            return jnp.pad(flat, (0, -flat.shape[0] % 1024)).reshape(-1, 128)

        def unpacked(flat, arrays):
            flat, marks = flat.reshape(-1), [0]
            for a in arrays:
                marks.append(marks[-1] + a.size)
            return [flat[marks[k] : marks[k + 1]].reshape(a.shape) for k, a in enumerate(arrays)]

        early = (conv_g, gain_g[0, 1], gain_g[1:])
        whole = sum_over(packed(early), tp_axes[::-1])
        local_sums = (chan_rows, head_rows, whole)
        chan_sum, head_sum, whole = unpacked(
            sum_over(packed(local_sums), group_axes[::-1] + (half_axis,)), local_sums
        )
        conv_sum, gain_two, gain_rest = unpacked(whole, early)
        ctx_index = slot * members + me
        last_gain = jnp.repeat(gain_g[0, 0].reshape(ctx_count, 1, depth), 4, axis=1)
        last_gain = lax.all_to_all(
            last_gain.reshape(4 * ctx_count, 1, depth), all_axes, 0, 0, tiled=True
        )
        last_gain = jnp.sum(last_gain, axis=0)
        gain_rest = lax.dynamic_slice_in_dim(gain_rest, ctx_index * depth, depth, 2)
        gain_two = lax.dynamic_slice_in_dim(gain_two, ctx_index * depth, depth, 0)
        gain_own = jnp.concatenate([jnp.concatenate([last_gain, gain_two[None]])[None], gain_rest])
        return (
            activations,
            input_grad,
            gain_own,
            mix_g,
            share_g,
            chan_sum,
            conv_sum,
            head_sum,
            out_g,
            up_g,
            down_g,
        )

    return local


def solution(mesh):
    ctx_bits = mesh.shape["ctx"].bit_length() - 1
    tp_bits = mesh.shape["tp"].bit_length() - 1
    ctx_axes = tuple(f"c{k}" for k in range(ctx_bits))
    tp_axes = tuple(f"t{k}" for k in range(tp_bits))
    fine = Mesh(mesh.devices.reshape((2,) * (ctx_bits + tp_bits)), ctx_axes + tp_axes)
    return jax.shard_map(
        build(ctx_axes, tp_axes),
        mesh=fine,
        in_specs=(
            P(None, None, ctx_axes, None),
            P(None, None, ctx_axes, None),
            P(),
            P(None, None, ctx_axes),
            P(None, ctx_axes, tp_axes),
            P(None, ctx_axes, None),
            P(None, None, tp_axes),
            P(),
            P(None, None, tp_axes),
            P(None, tp_axes, ctx_axes),
            P(None, ctx_axes, tp_axes),
            P(None, tp_axes, ctx_axes),
        ),
        out_specs=(
            P(None, None, ctx_axes, None),
            P(None, None, ctx_axes, None),
            P(None, None, ctx_axes),
            P(None, ctx_axes, tp_axes),
            P(None, ctx_axes, None),
            P(None, None, tp_axes),
            P(),
            P(None, None, tp_axes),
            P(None, tp_axes, ctx_axes),
            P(None, ctx_axes, tp_axes),
            P(None, tp_axes, ctx_axes),
        ),
        check_vma=False,
    )
```

time: 1790 us -> 1300 us (0.73)
  waiting for transfers between devices: 659 us -> 437 us
  other arithmetic: 255 us -> 130 us
  matrix products: 177 us -> 76.2 us
  blocking collectives: 125 us -> 35.4 us
  Pallas kernels: 0 us -> 61.9 us
  local copies, waits for them, and re-layouts: 288 us -> 244 us
  starting transfers between devices: 253 us -> 288 us
    ppermute x74 -> x15, waiting for transfers between devices: 454 us -> 41.6 us  [the longest x2 31.7 us: local(): share_far = lax.ppermute(product_tn(far, grad_share), half_axis, SWAP)]
    psum x2 -> x0, blocking collectives: 104 us -> none  [the longest x1 62.8 us: local(): chan_sum, head_sum = lax.psum((chan_rows, head_rows), ctx_axes)]
    dot_general x52 -> x0, matrix products: 89.8 us -> none  [the longest x16 31.6 us: matmul_tn(): lax.dot_general(left_op, right_op, (((0,), (0,)), ((), ())), preferred_el...]
    ppermute x74 -> x15, starting transfers between devices: 81.6 us -> 10.6 us  [the longest x3 7.36 us: gather_lanes(): got = lax.ppermute(x, axis, SWAP)]
    ppermute x72 -> x81, waiting for transfers between devices: 90 us -> 159 us  [gather_rows(): got = lax.ppermute(held, axis, SWAP)]
    all_to_all x0 -> x15, starting transfers between devices: none -> 65.5 us  [the longest x10 44.5 us: group_swap(): return lax.all_to_all(blocks, group_axes, 0, 0, tiled=True)]
    pallas_call x0 -> x20, Pallas kernels: none -> 61.9 us  [the longest x8 40.8 us: call_whole(): pl.pallas_call(kernel, grid=(1,), in_specs=[pl.BlockSpec(memory_space=plt...]
    all_to_all x0 -> x15, waiting for transfers between devices: none -> 51.4 us  [the longest x10 49.5 us: group_swap(): return lax.all_to_all(blocks, group_axes, 0, 0, tiled=True)]
  transfers between devices with their start and end apart: 261 -> 216, of which waited for: 133 -> 108; matrix products, arithmetic and copies ran while one was open for 34% -> 26% of each run, Pallas kernels for 0% -> 5%
where the time goes in v2:
time: 1300 us; the launch traced here: 1290 us
  waiting for transfers between devices  437 us (34%)
  starting transfers between devices  288 us (22%)
  local copies, waits for them, and re-layouts  244 us (19%)
  other arithmetic  130 us (10%)
  matrix products  76.2 us (6%)
  Pallas kernels  61.9 us (5%)
  blocking collectives  35.4 us (3%)
  between operations  20.2 us (2%)
    ppermute x81, waiting for transfers between devices, gather_rows(): got = lax.ppermute(held, axis, SWAP)  159 us
    ppermute x72, waiting for transfers between devices, scatter_product(): got = lax.ppermute(pick(piece, dim, 1 - index).astype(bf16), axis, SWAP)  137 us
    unnamed x551, local copies, waits for them, and re-layouts  123 us
    ppermute x72, starting transfers between devices, scatter_product(): got = lax.ppermute(pick(piece, dim, 1 - index).astype(bf16), axis, SWAP)  104 us
    ppermute x81, starting transfers between devices, gather_rows(): got = lax.ppermute(held, axis, SWAP)  89 us
    all_to_all x10, waiting for transfers between devices, group_swap(): return lax.all_to_all(blocks, group_axes, 0, 0, tiled=True)  49.5 us
    all_to_all x10, starting transfers between devices, group_swap(): return lax.all_to_all(blocks, group_axes, 0, 0, tiled=True)  44.5 us
    pallas_call x8, Pallas kernels, call_whole(): pl.pallas_call(kernel, grid=(1,), in_specs=[pl.BlockSpec(memory_space=plt...  40.8 us
  transfers between devices with their start and end apart: 216, of which 108 were waited for; matrix products, arithmetic and copies ran while one was open for 26% of the time, Pallas kernels for 5%

profile of v2, /device:TPU:0, one launch (start us, length us, event | category | flops | bytes accessed | tf_op | source)
XLA Modules:
  0.0 1292.4 jit_solution(5734115516864281819)
XLA Ops:
  59.3 7.1 all-to-all-start.2
  93.8 32.4 %collective-permute-done.9 = bf16[1,2,2,48,640]{4,3,2,1,0:T(8,128)(2,1)S(1)} collective-permute-done((bf16[1,2,2,48,640]{4,3,2,1,0:T(8,128)(2,1)S(1)}, bf16[1,2,2,48,640]{4,3,2,1,0:T(8,128)(2,1)S(1)}, u32[]{:S(2)}, u32[]{:S(2)}) %collective-permute-start.9) | collective-permute-done | bytes 245792 | tf_op jit(solution)/shard_map/ppermute | solution.py:560
  160.6 12.0 all-gather.10.cloned.1.call-done
  192.9 14.6 %all-to-all-done.3 = bf16[4,256,768]{2,1,0:T(8,128)(2,1)} async-done(((bf16[4,256,768]{2,1,0:T(8,128)(2,1)}), bf16[4,256,768]{2,1,0:T(8,128)(2,1)}, u32[]{:S(2)}, u32[]{:S(2)}) %all-to-all-start.3) | async-done | bytes 1572896 | tf_op jit(solution)/shard_map/all_to_all | solution.py:614
  264.0 23.5 %all-to-all-done.4 = bf16[4,256,512]{2,1,0:T(8,128)(2,1)S(1)} async-done(((bf16[4,256,512]{2,1,0:T(8,128)(2,1)}), bf16[4,256,512]{2,1,0:T(8,128)(2,1)S(1)}, u32[]{:S(2)}, u32[]{:S(2)}) %all-to-all-start.4) | async-done | bytes 1048608 | tf_op jit(solution)/shard_map/all_to_all | solution.py:614
  314.0 7.6 collective-permute-done.35
  332.7 16.5 %collective-permute-done.40 = bf16[48,640]{1,0:T(8,128)(2,1)S(1)} collective-permute-done((bf16[48,640]{1,0:T(8,128)(2,1)S(1)}, bf16[48,640]{1,0:T(8,128)(2,1)S(1)}, u32[]{:S(2)}, u32[]{:S(2)}) %collective-permute-start.40) | collective-permute-done | bytes 61472 | tf_op jit(solution)/shard_map/ppermute | solution.py:590
  374.1 21.7 %all_to_all.85 = bf16[4,256,320]{1,2,0:T(8,128)(2,1)} all-to-all(bf16[4,256,320]{1,2,0:T(8,128)(2,1)S(1)} %copy-done.147), channel_id=1, replica_groups=mesh['c0'=2,'c1'=2,'c2'=2,'t0'=2,'t1'=2] {'c1','c2'}, dimensions={0} | all-to-all | bytes 1310720 | tf_op jit(solution)/shard_map/all_to_all | solution.py:614
  399.9 7.6 all-gather.16.cloned.1.call-done
  416.9 8.6 fusion.223.mixed
  434.6 13.7 %all_to_all.86 = f32[16,2,3,128]{3,1,2,0:T(2,128)} all-to-all(f32[16,2,3,128]{3,1,2,0:T(2,128)S(1)} %broadcast_in_dim.116), channel_id=1, replica_groups=mesh['c0'=2,'c1'=2,'c2'=2,'t0'=2,'t1'=2] {'c1','c2','t0','t1'}, dimensions={0} | all-to-all | bytes 98304 | tf_op jit(solution)/shard_map/all_to_all | solution.py:599
  488.7 10.9 collective-permute-done.55
  530.2 19.9 %collective-permute-done.64 = bf16[1,1,1,48,640]{4,3,0,2,1:T(8,128)(2,1)S(1)} collective-permute-done((bf16[1,1,1,48,640]{4,3,0,2,1:T(8,128)(2,1)S(1)}, bf16[1,1,1,48,640]{4,3,0,2,1:T(8,128)(2,1)S(1)}, u32[]{:S(2)}, u32[]{:S(2)}) %collective-permute-start.64) | collective-permute-done | bytes 61472 | tf_op jit(solution)/shard_map/ppermute | solution.py:560
  571.3 7.7 collective-permute-done.94
  715.9 12.2 shard_map.210
  740.0 6.7 reduce-scatter.6.cloned.1.call-done
  793.1 9.3 collective-permute-done.124
  860.8 6.6 collective-permute-done.139
  892.2 7.0 collective-permute-done.148
  999.1 12.2 shard_map.215
  1084.7 9.5 collective-permute-done.159
  1105.7 15.7 %collective-permute-done.175 = bf16[2,48,1152]{2,1,0:T(8,128)(2,1)S(1)} collective-permute-done((bf16[2,48,1152]{2,1,0:T(8,128)(2,1)S(1)}, bf16[2,48,1152]{2,1,0:T(8,128)(2,1)S(1)}, u32[]{:S(2)}, u32[]{:S(2)}) %collective-permute-start.175) | collective-permute-done | bytes 221216 | tf_op jit(solution)/shard_map/ppermute | solution.py:590
  1124.3 8.8 collective-permute-done.188
  1234.3 22.9 %collective-permute-done.187 = bf16[256,1152]{1,0:T(8,128)(2,1)S(1)} collective-permute-done((bf16[256,1152]{1,0:T(8,128)(2,1)S(1)}, bf16[256,1152]{1,0:T(8,128)(2,1)S(1)}, u32[]{:S(2)}, u32[]{:S(2)}) %collective-permute-start.187) | collective-permute-done | bytes 589856 | tf_op jit(solution)/shard_map/ppermute | solution.py:981
  (1627 shorter events, 957.6 us)
Async XLA Ops:
  7.2 129.5 %all-gather.8.cloned.1.call-start = ((), (), s32[]{:S(2)}) async-start(), calls=%async_computation.22 | async-start | bytes 3551232 | tf_op jit(solution)/shard_map/all_gather | solution.py:812
  81.7 55.0 %all-to-all-start = ((bf16[8,256,512]{1,2,0:T(8,128)(2,1)}), bf16[8,256,512]{1,2,0:T(8,128)(2,1)}, u32[]{:S(2)}, u32[]{:S(2)}) async-start(bf16[8,256,512]{1,2,0:T(8,128)(2,1)} %pad_maximum_fusion.14), calls=%async_computation | async-start | bytes 4194304 | tf_op jit(solution)/shard_map/all_to_all | solution.py:620
  86.1 86.5 %all-gather.10.cloned.1.call-start = ((), (), s32[]{:S(2)}) async-start(), calls=%async_computation.23 | async-start | bytes 1966080 | tf_op jit(solution)/shard_map/all_gather | solution.py:617
  186.8 103.9 %all-gather.12.cloned.1.call-start = ((), (), s32[]{:S(2)}) async-start(), calls=%async_computation.24 | async-start | bytes 4718592 | tf_op jit(solution)/shard_map/all_gather | solution.py:617
  257.3 142.6 %all-gather.14.cloned.1.call-start = ((), (), s32[]{:S(2)}) async-start(), calls=%async_computation.25 | async-start | bytes 3145728 | tf_op jit(solution)/shard_map/all_gather | solution.py:617
  288.5 119.0 %all-gather.16.cloned.1.call-start = ((), (), s32[]{:S(2)}) async-start(), calls=%async_computation.26 | async-start | bytes 3551232 | tf_op jit(solution)/shard_map/all_gather | solution.py:812
  300.8 48.5 %collective-permute-start.85 = (bf16[48,2048]{1,0:T(8,128)(2,1)}, bf16[48,2048]{1,0:T(8,128)(2,1)}, u32[]{:S(2)}, u32[]{:S(2)}) collective-permute-start(bf16[48,2048]{1,0:T(8,128)(2,1)} %dynamic-slice_bitcast_fusion.3), channel_id=1, source_target_pairs={{0,16},{17,1},{2,18},{19,3},{4,20},{21,5},{6,22},{23,7},{8,24},{25... | collective-permute-start | bytes 589832 | tf_op jit(solution)/shard_map/ppermute | solution.py:719
  305.0 148.1 %all-gather.18.cloned.1.call-start = ((), (), s32[]{:S(2)}) async-start(), calls=%async_computation.27 | async-start | bytes 1966080 | tf_op jit(solution)/shard_map/all_gather | solution.py:617
  452.6 131.0 %all-gather.20.cloned.1.call-start = ((), (), s32[]{:S(2)}) async-start(), calls=%async_computation.28 | async-start | bytes 4718592 | tf_op jit(solution)/shard_map/all_gather | solution.py:617
  472.2 274.4 %reduce-scatter.6.cloned.1.call-start = ((), (), s32[]{:S(2)}) async-start(), calls=%async_computation.29 | async-start | bytes 4718592 | tf_op jit(solution)/shard_map/reduce_scatter | solution.py:623
  477.6 84.8 %collective-permute-start.90 = (bf16[1,2,1,48,640]{4,3,1,2,0:T(8,128)(2,1)S(1)}, bf16[1,2,1,48,640]{4,3,1,2,0:T(8,128)(2,1)S(1)}, u32[]{:S(2)}, u32[]{:S(2)}) collective-permute-start(bf16[1,2,1,48,640]{4,3,1,2,0:T(8,128)(2,1)S(1)} %bitcast_select_fusion.5), channel_id=1, source_target_pairs={{0,2},{2,0},{1,3},{3,1},{4,6},{6,4},{5,7},{7,5},{8,10},{10,8},{9,1... | collective-permute-start | bytes 368648 | tf_op jit(solution)/shard_map/ppermute | solution.py:560
  481.0 88.5 %collective-permute-start.93 = (bf16[1,1,2,48,768]{4,3,2,1,0:T(8,128)(2,1)S(1)}, bf16[1,1,2,48,768]{4,3,2,1,0:T(8,128)(2,1)S(1)}, u32[]{:S(2)}, u32[]{:S(2)}) collective-permute-start(bf16[1,1,2,48,768]{4,3,2,1,0:T(8,128)(2,1)S(1)} %maximum_select_fusion.70), channel_id=1, source_target_pairs={{0,8},{8,0},{1,9},{9,1},{2,10},{10,2},{3,11},{11,3},{4,12},{12,4},... | collective-permute-start | bytes 442376 | tf_op jit(solution)/shard_map/ppermute | solution.py:560
  485.9 84.6 %collective-permute-start.88 = (bf16[2,2,1,48,640]{4,3,0,2,1:T(8,128)(2,1)S(1)}, bf16[2,2,1,48,640]{4,3,0,2,1:T(8,128)(2,1)S(1)}, u32[]{:S(2)}, u32[]{:S(2)}) collective-permute-start(bf16[2,2,1,48,640]{4,3,0,2,1:T(8,128)(2,1)S(1)} %maximum_select_fusion.49), channel_id=1, source_target_pairs={{0,2},{2,0},{1,3},{3,1},{4,6},{6,4},{5,7},{7,5},{8,10},{10,8},{9,1... | collective-permute-start | bytes 737288 | tf_op jit(solution)/shard_map/ppermute | solution.py:560
  687.1 117.8 %reduce-scatter.8.cloned.1.call-start = ((), (), s32[]{:S(2)}) async-start(), calls=%async_computation.30 | async-start | bytes 1966080 | tf_op jit(solution)/shard_map/reduce_scatter | solution.py:623
  765.0 196.2 %reduce-scatter.10.cloned.1.call-start = ((), (), s32[]{:S(2)}) async-start(), calls=%async_computation.31 | async-start | bytes 3145728 | tf_op jit(solution)/shard_map/reduce_scatter | solution.py:623
  844.2 201.1 %reduce-scatter.12.cloned.1.call-start = ((), (), s32[]{:S(2)}) async-start(), calls=%async_computation.32 | async-start | bytes 4718592 | tf_op jit(solution)/shard_map/reduce_scatter | solution.py:623
  969.4 91.4 %collective-permute-start.117 = (bf16[2,48,2048]{2,1,0:T(8,128)(2,1)}, bf16[2,48,2048]{2,1,0:T(8,128)(2,1)}, u32[]{:S(2)}, u32[]{:S(2)}) collective-permute-start(bf16[2,48,2048]{2,1,0:T(8,128)(2,1)} %broadcast_select_fusion.1), channel_id=1, source_target_pairs={{0,2},{2,0},{1,3},{3,1},{4,6},{6,4},{5,7},{7,5},{8,10},{10,8},{9,1... | collective-permute-start | bytes 1179656 | tf_op jit(solution)/shard_map/ppermute | solution.py:732
  983.3 42.4 %all-to-all-start.11 = ((bf16[4,256,512]{2,1,0:T(8,128)(2,1)}), bf16[4,256,512]{2,1,0:T(8,128)(2,1)}, u32[]{:S(2)}, u32[]{:S(2)}) async-start(bf16[4,256,512]{2,1,0:T(8,128)(2,1)} %reduce-scatter.10.cloned.1.call-done), calls=%async_computation.14 | async-start | bytes 2097152 | tf_op jit(solution)/shard_map/all_to_all | solution.py:614
  1030.1 109.8 %reduce-scatter.14.cloned.1.call-start = ((), (), s32[]{:S(2)}) async-start(), calls=%async_computation.33 | async-start | bytes 1966080 | tf_op jit(solution)/shard_map/reduce_scatter | solution.py:623
  1055.9 77.1 %collective-permute-start.188 = (bf16[256,1152]{1,0:T(8,128)(2,1)}, bf16[256,1152]{1,0:T(8,128)(2,1)}, u32[]{:S(2)}, u32[]{:S(2)}) collective-permute-start(bf16[256,1152]{1,0:T(8,128)(2,1)} %shard_map.222), channel_id=1, source_target_pairs={{0,16},{16,0},{1,17},{17,1},{2,18},{18,2},{3,19},{19,3},{4,20},{20... | collective-permute-start | bytes 1769480 | tf_op jit(solution)/shard_map/ppermute | solution.py:981
  1078.9 151.1 %collective-permute-start.173 = (bf16[4,256,512]{2,1,0:T(8,128)(2,1)}, bf16[4,256,512]{2,1,0:T(8,128)(2,1)}, u32[]{:S(2)}, u32[]{:S(2)}) collective-permute-start(bf16[4,256,512]{2,1,0:T(8,128)(2,1)} %dynamic-slice_bitcast_fusion), channel_id=1, source_target_pairs={{0,16},{16,0},{1,17},{17,1},{2,18},{18,2},{3,19},{19,3},{4,20},{20... | collective-permute-start | bytes 3145736 | tf_op jit(solution)/shard_map/ppermute | solution.py:628
  1122.2 49.1 %collective-permute-start.176 = (bf16[48,1152]{1,0:T(8,128)(2,1)}, bf16[48,1152]{1,0:T(8,128)(2,1)}, u32[]{:S(2)}, u32[]{:S(2)}) collective-permute-start(bf16[48,1152]{1,0:T(8,128)(2,1)} %fusion.168), channel_id=1, source_target_pairs={{0,4},{4,0},{1,5},{5,1},{2,6},{6,2},{3,7},{7,3},{8,12},{12,8},{9,1... | collective-permute-start | bytes 331784 | tf_op jit(solution)/shard_map/ppermute | solution.py:590
  1166.3 47.1 %all-to-all-start.15 = ((bf16[4,256,320]{1,2,0:T(8,128)(2,1)}), bf16[4,256,320]{1,2,0:T(8,128)(2,1)S(1)}, u32[]{:S(2)}, u32[]{:S(2)}) async-start(bf16[4,256,320]{1,2,0:T(8,128)(2,1)} %reduce-scatter.14.cloned.1.call-done), calls=%async_computation.20 | async-start | bytes 1310720 | tf_op jit(solution)/shard_map/all_to_all | solution.py:614
  1213.4 46.0 %all-to-all-start.16 = ((bf16[4,256,768]{1,2,0:T(8,128)(2,1)}), bf16[4,256,768]{1,2,0:T(8,128)(2,1)}, u32[]{:S(2)}, u32[]{:S(2)}) async-start(bf16[4,256,768]{1,2,0:T(8,128)(2,1)} %reduce-scatter.12.cloned.1.call-done), calls=%async_computation.21 | async-start | bytes 3145728 | tf_op jit(solution)/shard_map/all_to_all | solution.py:614
  (450 other events, 3601.5 us)
Sparse Core Ops, SparseCore 0:
  14.4 51.0 all-gather.7
  132.9 39.5 all-gather.9
  207.6 77.7 all-gather.11
  288.6 60.3 all-gather.13
  351.6 55.8 all-gather.15
  408.9 37.2 all-gather.17
  472.3 77.0 all-gather.19
  670.5 76.1 reduce-scatter.5
  765.1 37.8 reduce-scatter.7
  844.3 55.0 reduce-scatter.9
  943.4 75.4 reduce-scatter.11
  1063.5 76.2 reduce-scatter.13

commit v3 on v2

--- a/solution.py
+++ b/solution.py
@@ -420,7 +420,7 @@
 
 
 def ssm_params(plan):
-    limit = 30 * 2**20 if plan.seq_len <= 768 else 58 * 2**20
+    limit = 58 * 2**20
     return pltpu.CompilerParams(vmem_limit_bytes=limit)
 
 
@@ -721,17 +721,23 @@
             )
             return jnp.where(tp_core == slot, pick(pick(x, 0, slot), 0, tp_half), got)
 
-        def bring_out(x, points=None):
+        def share_columns(own):
+            quarter = own.shape[1] // 4
+            chunks = jnp.moveaxis(own.reshape(block_len, 4, quarter), 1, 0)
+            chunks = jnp.broadcast_to(chunks[None], (members,) + chunks.shape)
+            rows = lax.all_to_all(
+                chunks.reshape(4 * members, block_len, quarter), slot_axes, 0, 0, tiled=True
+            )
+            rows = jnp.moveaxis(rows.reshape(2 * members, 2, block_len, quarter), 1, 0)
+            return jnp.where(tp_core == 0, rows, rows[::-1]).reshape(seq_len, quarter)
+
+        def bring_out(x):
             x = x.astype(bf16)
             got = lax.ppermute(x, (half_axis, t_core), [(1, 3), (2, 0)])
-            if points is not None:
-                got = after(got, points[0])
             pair = jnp.where(slot == 0, jnp.stack([x, got]), jnp.stack([got, x]))
             other = lax.ppermute(pair, t_core, SWAP)
             pair = jnp.where(tp_core == slot, pair, other)
             other = lax.ppermute(pair, t_half, SWAP)
-            if points is not None:
-                other = after(other, points[1])
             both = jnp.where(tp_half == 0, jnp.stack([pair, other], 1), jnp.stack([other, pair], 1))
             return both.astype(f32)
 
@@ -834,15 +840,17 @@
         out_own = [None] * LAYERS
         ffn_own = [None] * LAYERS
         shares = [None] * LAYERS
-        blocks = after(blocks, hidden_rows)
-        mix_own[0] = spread_first(blocks[0][0])
-        swapped = [[group_swap(x) for x in blocks[layer][layer == 0 :]] for layer in range(LAYERS)]
+        mix_own[0] = spread_first(after(blocks[0][0], hidden_rows))
+        out_cols = HD + width
+        swapped = [[group_swap(x) for x in after(blocks[0][1:], hidden_rows)]]
+        for layer in range(1, LAYERS):
+            both = group_swap(jnp.concatenate(blocks[layer][:2], axis=2))
+            swapped.append([both[:, :, -out_cols:], group_swap(blocks[layer][2])])
+            mix_own[layer] = both_halves(both[:, :, :-out_cols])
         for layer in range(LAYERS):
-            if layer > 0:
-                mix_own[layer] = both_halves(swapped[layer][0])
             shares[layer] = share_whole(share_rows[layer])
-            out_own[layer] = both_halves(swapped[layer][-2])
-            ffn_own[layer] = both_halves(swapped[layer][-1])
+            out_own[layer] = both_halves(swapped[layer][0])
+            ffn_own[layer] = both_halves(swapped[layer][1])
 
         records = []
         for layer in range(LAYERS):
@@ -854,13 +862,16 @@
                 normed = gather_rows(normed_f.astype(bf16))
             in_w = input_weights(*after((mix_own[layer], shares[layer]), normed))
             mixed = matmul(normed, in_w)
+            mixed_here = mixed
+            if layer == 0:
+                mixed_here = after(mixed, (swapped[0][1], swapped[1][0]))
             ssm_y, gated_low, states, squares = run_forward(
                 plan, core_scalar, mixed, tap_rows[layer], shared_rows[layer], head_rows[layer]
             )
             sum_squares = sum_slot(squares[0])
             gated_scale = lax.rsqrt(sum_squares / (MH * P_SIZE) + eps_norm)
             scaled_low = (gated_low.astype(f32) * gated_scale).astype(bf16)
-            attended, logsum, queries, keyval = run_attend(plan, query_part, mixed, *tables)
+            attended, logsum, queries, keyval = run_attend(plan, query_part, mixed_here, *tables)
             mixer = jnp.concatenate([attended, scaled_low], axis=1)
             out_w = after(out_own[layer], gated_low).reshape(D, HD + width)
             middle = stream + scatter_product(mixer, out_w)
@@ -893,10 +904,7 @@
             if layer == LAYERS - 1:
                 grad_ffn = gather_rows(grad_masked.astype(bf16))
             else:
-                gathered = jnp.concatenate([grad_masked, share_own], axis=1).astype(bf16)
-                gathered = gather_rows(after(gathered, folded[layer + 1][1]))
-                grad_ffn = gathered[:, :D]
-                share_sums.append(gathered[:, D:])
+                grad_ffn = gather_rows(grad_masked.astype(bf16))
             points.append([grad_ffn])
             grad_activation = matmul(grad_ffn, down_w)
             grad_down = product_tn(grad_ffn, rec["activation"])
@@ -916,24 +924,23 @@
                 ctx_count, depth, 3 * ff_own
             )
             folded[layer] = [fold_halves(ffn_blocks)]
-            branch_rows = gather_rows(after(grad_middle.astype(bf16), ffn_blocks))
+            early = (ffn_blocks,) if layer + 1 == LAYERS else (ffn_blocks, folded[layer + 1][1])
+            branch_rows = gather_rows(after(grad_middle.astype(bf16), early))
             points[-1].append(branch_rows)
             grad_mixer = matmul(branch_rows, out_w)
             out_blocks = product_tn(branch_rows, rec["mixer"]).reshape(
                 ctx_count, depth, HD + width
             )
-            folded[layer].append(fold_halves(out_blocks))
+            if layer == 0:
+                folded[layer].append(fold_halves(out_blocks))
             gated_scale = rec["gated_scale"]
             scale_part = jnp.sum(grad_mixer[:, HD:] * rec["gated_low"].astype(f32), axis=-1)
             grad_scale = after(sum_slot(scale_part), out_blocks)
             grad_squares = grad_scale * -0.5 * gated_scale * gated_scale * gated_scale / (MH * P_SIZE)
-            grad_mixer_here = grad_mixer
             if layer + 1 < LAYERS:
-                earlier = after(folded[layer + 1][1:], branch_rows)
-                came[layer + 1] += [group_swap(x) for x in earlier]
-                grad_mixer_here = after(grad_mixer, came[layer + 1][1:])
+                came[layer + 1].append(group_swap(after(folded[layer + 1][1], branch_rows)))
             grad_q, grad_kv = run_attend_back(
-                plan, query_part, rec["queries"], rec["keyval"], rec["logsum"], grad_mixer_here,
+                plan, query_part, rec["queries"], rec["keyval"], rec["logsum"], grad_mixer,
                 *tables,
             )
             grad_bc, grad_pair, grad_step, taps_grad, grad_conv, heads_grad = run_backward(
@@ -948,7 +955,8 @@
             )
             grad_mix_own = jnp.concatenate([grad_q, grad_pair], axis=1)
             grad_in = jnp.concatenate([grad_bc, grad_kv, grad_mix_own, grad_step], axis=1)
-            grad_in = after(grad_in, folded[layer][0])
+            if layer == 0:
+                grad_in = after(grad_in, folded[layer][0])
             at_heads = [
                 jnp.where(kv_head == head, grad_kv[:, part * HD : (part + 1) * HD], 0)
                 for part in range(2)
@@ -958,45 +966,65 @@
                 jnp.zeros((seq_len, 128), bf16), grad_step[:, :heads], (0, dt_start - dt_cols)
             )
             grad_share = jnp.concatenate([grad_bc] + at_heads + [step_cols], axis=1)
+            if layer == 0:
+                grad_share = after(grad_share, folded[0][1])
             scattered = scatter_product(grad_in, in_w, grad_share)
-            grad_normed_one, share_own = scattered[:, :D], scattered[:, D:]
+            if layer > 0:
+                scattered = after(scattered, folded[layer][0])
+            grad_normed_one = scattered[:, :D]
+            share_sums.append(share_columns(scattered[:, D:].astype(bf16)))
             points[-1] += [grad_in, grad_normed_one]
             grad_stream_norm, grad_gain_one = rec["norm_one_back"](grad_normed_one)
             grad_stream = grad_middle + grad_stream_norm
             grad_mix = product_tn(rec["normed"], grad_mix_own)[:, : HD + 2 * width]
-            fold = fold_last if layer == 0 else fold_halves
-            folded[layer].append(fold(grad_mix.reshape(ctx_count, depth, HD + 2 * width)))
+            mix_blocks = grad_mix.reshape(ctx_count, depth, HD + 2 * width)
+            if layer == 0:
+                folded[layer].append(fold_last(mix_blocks))
+            else:
+                folded[layer].append(fold_halves(jnp.concatenate([out_blocks, mix_blocks], axis=2)))
             out_grads[layer] = (
                 jnp.stack([grad_gain_one, grad_gain_two]), chan_grad, grad_conv, grad_heads,
             )
-        share_sums.append(gather_rows(share_own.astype(bf16)))
         last = points[-1]
-        activations = bring_out(stream, (points[0][1], last[1]))
+        mix_kept, mix_got = folded[0][2]
+        mix_sum = (mix_kept + after(mix_got, last[3]).astype(f32)).astype(bf16)
+        out_sum, mix_sum = after((folded[0][1], mix_sum), last[3])
+        came[0] = [
+            group_swap(after(folded[0][0], last[3])),
+            group_swap(jnp.concatenate([out_sum, mix_sum], axis=2)),
+        ]
+
         share_grads = []
         for layer in range(LAYERS):
             normed = records[layer]["normed"]
             grad_share = share_sums[LAYERS - 1 - layer]
             near = lax.dynamic_slice_in_dim(normed, (slot * members + me) * depth, depth, 1)
             far = lax.dynamic_slice_in_dim(normed, ((1 - slot) * members + me) * depth, depth, 1)
-            share_far = lax.ppermute(product_tn(far, grad_share), half_axis, SWAP)
+            share_far = product_tn(far, grad_share)
+            if layer == 0:
+                share_far = after(share_far, came[0][1])
+            share_far = lax.ppermute(share_far, half_axis, SWAP)
             if layer > 0:
                 share_far = after(share_far, last[3])
             share_sum = product_tn(near, grad_share).astype(f32) + share_far.astype(f32)
-            share_grads.append(share_sum[:, :share_cols])
+            share_sum = share_sum.astype(bf16)
+            for axis in tp_axes[::-1]:
+                got = lax.ppermute(share_sum, axis, SWAP)
+                first = lax.axis_index(axis) == 0
+                share_sum = jnp.where(
+                    first,
+                    jnp.concatenate([share_sum, got], 1),
+                    jnp.concatenate([got, share_sum], 1),
+                )
+            share_grads.append(share_sum[:, :share_cols].astype(f32))
         share_g = jnp.stack(share_grads)
-        input_grad = bring_out(grad_stream)
-
-        mix_kept, mix_got = folded[0][2]
-        mix_sum = (mix_kept + after(mix_got, share_sums[-1]).astype(f32)).astype(bf16)
-        came[0] = [
-            group_swap(after(folded[0][0], last[3])),
-            group_swap(after(folded[0][1], last[3])),
-            group_swap(mix_sum),
-        ]
+        both_out = bring_out(jnp.stack([stream, grad_stream]))
+        activations, input_grad = both_out[:, :, 0], both_out[:, :, 1]
 
         def weight_grads(layer):
             got = came[layer] if layer == 0 else after(came[layer], last[3])
-            ffn_came, out_came, mix_came = got
+            ffn_came, both_came = got
+            out_came, mix_came = both_came[:, :, : HD + width], both_came[:, :, HD + width :]
             mix = jnp.concatenate(
                 [
                     join_heads(mix_came[:, :, HD : HD + width], 1),

time: 1300 us -> 1270 us (0.977)
  blocking collectives: 35.4 us -> 0 us
  local copies, waits for them, and re-layouts: 244 us -> 213 us
  Pallas kernels: 61.9 us -> 86 us
  waiting for transfers between devices: 437 us -> 415 us
  starting transfers between devices: 288 us -> 306 us
  other arithmetic: 130 us -> 143 us
    unnamed x551 -> x374, local copies, waits for them, and re-layouts: 123 us -> 75.5 us
    all_to_all x2 -> x0, blocking collectives: 35.4 us -> none  [the longest x1 21.7 us: group_swap(): return lax.all_to_all(blocks, group_axes, 0, 0, tiled=True)]
    all_to_all x10 -> x8, waiting for transfers between devices: 49.5 us -> 23.7 us  [group_swap(): return lax.all_to_all(blocks, group_axes, 0, 0, tiled=True)]
    pallas_call x8, Pallas kernels: 40.8 us -> 66.1 us  [call_whole(): pl.pallas_call(kernel, grid=(1,), in_specs=[pl.BlockSpec(memory_space=plt...]
    ppermute x72, waiting for transfers between devices: 137 us -> 114 us  [scatter_product(): got = lax.ppermute(pick(piece, dim, 1 - index).astype(bf16), axis, SWAP)]
    ppermute x2 -> x6, waiting for transfers between devices: 31.7 us -> 13.1 us  [the longest x4 7.1 us: local(): got = lax.ppermute(share_sum, axis, SWAP)]
    ppermute x5, waiting for transfers between devices: 5.57 us -> 23.5 us  [sum_over(): x = x + lax.ppermute(x, axis, SWAP)]
    all_gather x2, waiting for transfers between devices: 7.63 us -> 21.3 us  [share_whole(): return lax.all_gather(share, ctx_axes + (t_core,), axis=0, tiled=True)]
  transfers between devices with their start and end apart: 216 -> 207, of which waited for: 108 -> 108; matrix products, arithmetic and copies ran while one was open for 26% -> 31% of each run, Pallas kernels for 5% -> 7%
where the time goes in v3:
time: 1270 us; the launch traced here: 1260 us
  waiting for transfers between devices  415 us (33%)
  starting transfers between devices  306 us (24%)
  local copies, waits for them, and re-layouts  213 us (17%)
  other arithmetic  143 us (11%)
  Pallas kernels  86 us (7%)
  matrix products  79.5 us (6%)
  between operations  19 us (1%)
    ppermute x72, waiting for transfers between devices, gather_rows(): got = lax.ppermute(held, axis, SWAP)  155 us
    ppermute x72, waiting for transfers between devices, scatter_product(): got = lax.ppermute(pick(piece, dim, 1 - index).astype(bf16), axis, SWAP)  114 us
    ppermute x72, starting transfers between devices, scatter_product(): got = lax.ppermute(pick(piece, dim, 1 - index).astype(bf16), axis, SWAP)  94.2 us
    ppermute x72, starting transfers between devices, gather_rows(): got = lax.ppermute(held, axis, SWAP)  92.8 us
    unnamed x374, local copies, waits for them, and re-layouts  75.5 us
    pallas_call x8, Pallas kernels, call_whole(): pl.pallas_call(kernel, grid=(1,), in_specs=[pl.BlockSpec(memory_space=plt...  66.1 us
    dot_general x16, matrix products, matmul_nt(): lax.dot_general(left_op, right_op, (((1,), (1,)), ((), ())), preferred_el...  40.3 us
    dot_general x8, matrix products, matmul(): return jnp.dot(left_op, right_op, preferred_element_type=f32)  39.1 us
  transfers between devices with their start and end apart: 207, of which 108 were waited for; matrix products, arithmetic and copies ran while one was open for 31% of the time, Pallas kernels for 7%

profile of v3, /device:TPU:0, one launch (start us, length us, event | category | flops | bytes accessed | tf_op | source)
XLA Modules:
  0.0 1260.8 jit_solution(7087186397726791860)
XLA Ops:
  76.5 11.4 collective-permute-done.7
  97.4 16.5 %collective-permute-done.5 = bf16[2,1,1,48,640]{4,3,2,1,0:T(8,128)(2,1)S(1)} collective-permute-done((bf16[2,1,1,48,640]{4,3,2,1,0:T(8,128)(2,1)S(1)}, bf16[2,1,1,48,640]{4,3,2,1,0:T(8,128)(2,1)S(1)}, u32[]{:S(2)}, u32[]{:S(2)}) %collective-permute-start.5) | collective-permute-done | bytes 122912 | tf_op jit(solution)/shard_map/ppermute | solution.py:560
  115.9 16.3 %collective-permute-done.11 = bf16[1,1,2,48,768]{4,3,2,1,0:T(8,128)(2,1)S(1)} collective-permute-done((bf16[1,1,2,48,768]{4,3,2,1,0:T(8,128)(2,1)S(1)}, bf16[1,1,2,48,768]{4,3,2,1,0:T(8,128)(2,1)S(1)}, u32[]{:S(2)}, u32[]{:S(2)}) %collective-permute-start.11) | collective-permute-done | bytes 147488 | tf_op jit(solution)/shard_map/ppermute | solution.py:560
  159.6 7.2 fusion.227.mixed
  166.7 8.6 shard_map.204
  176.3 10.8 all-to-all-done.1
  256.7 8.1 collective-permute-done.29
  270.9 21.8 %all-gather.12.cloned.1.call-done = bf16[8,256,768]{2,1,0:T(8,128)(2,1)} async-done(((bf16[4,256,768]{2,1,0:T(8,128)(2,1)}), bf16[8,256,768]{2,1,0:T(8,128)(2,1)}) %all-gather.12.cloned.1.call-update) | async-done | bytes 3145744 | tf_op jit(solution)/shard_map/all_gather | solution.py:617
  346.6 9.1 collective-permute-done.44
  384.1 21.3 %all-gather.16.cloned.1.call-done = bf16[2048,816]{0,1:T(8,128)(2,1)} async-done(((bf16[128,816]{0,1:T(8,128)(2,1)}), bf16[2048,816]{0,1:T(8,128)(2,1)}) %all-gather.16.cloned.1.call-update) | async-done | bytes 3342352 | tf_op jit(solution)/shard_map/all_gather | solution.py:818
  415.3 10.6 fusion.221.mixed
  425.9 8.5 shard_map.206
  487.0 10.7 collective-permute-done.55
  539.7 11.5 collective-permute-done.71
  692.1 16.0 %shard_map.210 = (bf16[768,512]{1,0:T(8,128)(2,1)}, bf16[768,384]{1,0:T(8,128)(2,1)}, bf16[768,128]{1,0:T(8,128)(2,1)}, f32[8,192]{1,0:T(8,128)}, f32[8,512]{1,0:T(8,128)}, /*index=5*/f32[8,128]{1,0:T(8,128)}) custom-call(s32[1]{0:T(128)} %bitcast.72.core_ref, f32[768,1408]{1,0:T(8,128)} %fusion.221.mixed, f32[8,192]{1,0:T(8,128)} %get-tuple-element.392.taps, ...), custom_call_target="tpu_custom_call" | custom-call | flops 13271040000 | bytes 6291456 | tf_op jit(solution)/shard_map/pallas_call | solution.py:408
  816.9 7.0 collective-permute-done.130
  889.3 8.7 collective-permute-done.150
  953.3 16.0 %shard_map.216 = (bf16[768,512]{1,0:T(8,128)(2,1)}, bf16[768,384]{1,0:T(8,128)(2,1)}, bf16[768,128]{1,0:T(8,128)(2,1)}, f32[8,192]{1,0:T(8,128)}, f32[8,512]{1,0:T(8,128)}, /*index=5*/f32[8,128]{1,0:T(8,128)}) custom-call(s32[1]{0:T(128)} %bitcast.72.core_ref, f32[768,1408]{1,0:T(8,128)} %fusion.227.mixed, f32[8,192]{1,0:T(8,128)} %get-tuple-element.393.taps, ...), custom_call_target="tpu_custom_call" | custom-call | flops 13271040000 | bytes 6291456 | tf_op jit(solution)/shard_map/pallas_call | solution.py:408
  1063.3 9.7 collective-permute-done.172
  1076.5 12.9 %collective-permute-done.170 = bf16[4,256,512]{1,2,0:T(8,128)(2,1)} collective-permute-done((bf16[4,256,512]{1,2,0:T(8,128)(2,1)}, bf16[4,256,512]{1,2,0:T(8,128)(2,1)}, u32[]{:S(2)}, u32[]{:S(2)}) %collective-permute-start.170) | collective-permute-done | bytes 1048608 | tf_op jit(solution)/shard_map/ppermute | solution.py:628
  1137.9 7.8 collective-permute-done.167
  1159.6 14.6 %collective-permute-done.169 = f32[168,128]{1,0:T(8,128)S(1)} collective-permute-done((f32[168,128]{1,0:T(8,128)S(1)}, f32[168,128]{1,0:T(8,128)S(1)}, u32[]{:S(2)}, u32[]{:S(2)}) %collective-permute-start.169) | collective-permute-done | bytes 86048 | tf_op jit(solution)/shard_map/ppermute | solution.py:607
  1182.2 14.4 %collective-permute-done.164 = bf16[2,2,48,2048]{3,2,0,1:T(8,128)(2,1)S(1)} collective-permute-done((bf16[2,2,48,2048]{3,2,0,1:T(8,128)(2,1)S(1)}, bf16[2,2,48,2048]{3,2,0,1:T(8,128)(2,1)S(1)}, u32[]{:S(2)}, u32[]{:S(2)}) %collective-permute-start.164) | collective-permute-done | bytes 786464 | tf_op jit(solution)/shard_map/ppermute | solution.py:740
  1244.5 7.1 collective-permute-done.176
  (1422 shorter events, 955.3 us)
Async XLA Ops:
  7.2 147.4 %all-gather.8.cloned.1.call-start = ((), (), s32[]{:S(2)}) async-start(), calls=%async_computation.20 | async-start | bytes 3551232 | tf_op jit(solution)/shard_map/all_gather | solution.py:818
  89.4 57.2 %all-to-all-start = ((bf16[8,256,512]{1,2,0:T(8,128)(2,1)}), bf16[8,256,512]{1,2,0:T(8,128)(2,1)}, u32[]{:S(2)}, u32[]{:S(2)}) async-start(bf16[8,256,512]{1,2,0:T(8,128)(2,1)} %pad_maximum_fusion.14), calls=%async_computation | async-start | bytes 4194304 | tf_op jit(solution)/shard_map/all_to_all | solution.py:620
  93.8 99.8 %all-gather.10.cloned.1.call-start = ((), (), s32[]{:S(2)}) async-start(), calls=%async_computation.21 | async-start | bytes 1966080 | tf_op jit(solution)/shard_map/all_gather | solution.py:617
  146.6 40.4 %all-to-all-start.1 = ((bf16[4,256,768]{2,1,0:T(8,128)(2,1)}), bf16[4,256,768]{2,1,0:T(8,128)(2,1)}, u32[]{:S(2)}, u32[]{:S(2)}) async-start(bf16[4,256,768]{2,1,0:T(8,128)(2,1)} %pad_maximum_fusion.18), calls=%async_computation.1 | async-start | bytes 3145728 | tf_op jit(solution)/shard_map/all_to_all | solution.py:614
  191.2 101.5 %all-gather.12.cloned.1.call-start = ((), (), s32[]{:S(2)}) async-start(), calls=%async_computation.22 | async-start | bytes 4718592 | tf_op jit(solution)/shard_map/all_gather | solution.py:617
  212.9 171.2 %all-gather.14.cloned.1.call-start = ((), (), s32[]{:S(2)}) async-start(), calls=%async_computation.23 | async-start | bytes 3145728 | tf_op jit(solution)/shard_map/all_gather | solution.py:617
  267.8 137.7 %all-gather.16.cloned.1.call-start = ((), (), s32[]{:S(2)}) async-start(), calls=%async_computation.24 | async-start | bytes 3551232 | tf_op jit(solution)/shard_map/all_gather | solution.py:818
  305.2 145.9 %all-gather.18.cloned.1.call-start = ((), (), s32[]{:S(2)}) async-start(), calls=%async_computation.25 | async-start | bytes 1966080 | tf_op jit(solution)/shard_map/all_gather | solution.py:617
  450.9 124.0 %all-gather.20.cloned.1.call-start = ((), (), s32[]{:S(2)}) async-start(), calls=%async_computation.26 | async-start | bytes 4718592 | tf_op jit(solution)/shard_map/all_gather | solution.py:617
  470.4 322.6 %reduce-scatter.5.cloned.1.call-start = ((), (), s32[]{:S(2)}) async-start(), calls=%async_computation.27 | async-start | bytes 4718592 | tf_op jit(solution)/shard_map/reduce_scatter | solution.py:623
  475.8 75.4 %collective-permute-start.89 = (bf16[1,2,1,48,640]{4,3,2,1,0:T(8,128)(2,1)S(1)}, bf16[1,2,1,48,640]{4,3,2,1,0:T(8,128)(2,1)S(1)}, u32[]{:S(2)}, u32[]{:S(2)}) collective-permute-start(bf16[1,2,1,48,640]{4,3,2,1,0:T(8,128)(2,1)S(1)} %maximum_select_fusion.82), channel_id=1, source_target_pairs={{0,2},{2,0},{1,3},{3,1},{4,6},{6,4},{5,7},{7,5},{8,10},{10,8},{9,1... | collective-permute-start | bytes 368648 | tf_op jit(solution)/shard_map/ppermute | solution.py:560
  479.2 81.4 %collective-permute-start.92 = (bf16[1,1,2,48,768]{4,3,2,1,0:T(8,128)(2,1)S(1)}, bf16[1,1,2,48,768]{4,3,2,1,0:T(8,128)(2,1)S(1)}, u32[]{:S(2)}, u32[]{:S(2)}) collective-permute-start(bf16[1,1,2,48,768]{4,3,2,1,0:T(8,128)(2,1)S(1)} %maximum_select_fusion.61), channel_id=1, source_target_pairs={{0,8},{8,0},{1,9},{9,1},{2,10},{10,2},{3,11},{11,3},{4,12},{12,4},... | collective-permute-start | bytes 442376 | tf_op jit(solution)/shard_map/ppermute | solution.py:560
  484.2 78.0 %collective-permute-start.87 = (bf16[2,2,1,48,640]{4,3,0,2,1:T(8,128)(2,1)S(1)}, bf16[2,2,1,48,640]{4,3,0,2,1:T(8,128)(2,1)S(1)}, u32[]{:S(2)}, u32[]{:S(2)}) collective-permute-start(bf16[2,2,1,48,640]{4,3,0,2,1:T(8,128)(2,1)S(1)} %maximum_select_fusion.44), channel_id=1, source_target_pairs={{0,2},{2,0},{1,3},{3,1},{4,6},{6,4},{5,7},{7,5},{8,10},{10,8},{9,1... | collective-permute-start | bytes 737288 | tf_op jit(solution)/shard_map/ppermute | solution.py:560
  677.2 194.0 %reduce-scatter.7.cloned.1.call-start = ((), (), s32[]{:S(2)}) async-start(), calls=%async_computation.28 | async-start | bytes 5111808 | tf_op jit(solution)/shard_map/reduce_scatter | solution.py:623
  760.2 223.7 %reduce-scatter.9.cloned.1.call-start = ((), (), s32[]{:S(2)}) async-start(), calls=%async_computation.29 | async-start | bytes 4718592 | tf_op jit(solution)/shard_map/reduce_scatter | solution.py:623
  928.9 66.1 %reduce-scatter.11.cloned.1.call-start = ((), (), s32[]{:S(2)}) async-start(), calls=%async_computation.30 | async-start | bytes 1966080 | tf_op jit(solution)/shard_map/reduce_scatter | solution.py:623
  943.0 40.9 %all-to-all-start.14 = ((bf16[16,48,288]{2,1,0:T(8,128)(2,1)}), bf16[16,48,288]{2,1,0:T(8,128)(2,1)}, u32[]{:S(2)}, u32[]{:S(2)}) async-start(bf16[16,48,288]{2,1,0:T(8,128)(2,1)} %bitcast.1029), calls=%async_computation.18 | async-start | bytes 1179648 | tf_op jit(solution)/shard_map/all_to_all | solution.py:728
  1005.6 88.9 %collective-permute-start.177 = (bf16[256,288]{1,0:T(8,128)(2,1)}, bf16[256,288]{1,0:T(8,128)(2,1)}, u32[]{:S(2)}, u32[]{:S(2)}) collective-permute-start(bf16[256,288]{1,0:T(8,128)(2,1)} %shard_map.222), channel_id=1, source_target_pairs={{0,16},{16,0},{1,17},{17,1},{2,18},{18,2},{3,19},{19,3},{4,20},{20... | collective-permute-start | bytes 442376 | tf_op jit(solution)/shard_map/ppermute | solution.py:1006
  1013.2 62.4 %all-to-all-start.12 = ((bf16[4,256,832]{1,2,0:T(8,128)(2,1)}), bf16[4,256,832]{1,2,0:T(8,128)(2,1)}, u32[]{:S(2)}, u32[]{:S(2)}) async-start(bf16[4,256,832]{1,2,0:T(8,128)(2,1)} %reduce-scatter.7.cloned.1.call-done), calls=%async_computation.16 | async-start | bytes 3407872 | tf_op jit(solution)/shard_map/all_to_all | solution.py:614
  1041.4 48.0 %collective-permute-start.170 = (bf16[4,256,512]{1,2,0:T(8,128)(2,1)}, bf16[4,256,512]{1,2,0:T(8,128)(2,1)}, u32[]{:S(2)}, u32[]{:S(2)}) collective-permute-start(bf16[4,256,512]{1,2,0:T(8,128)(2,1)} %bitcast.1071), channel_id=1, source_target_pairs={{0,16},{16,0},{1,17},{17,1},{2,18},{18,2},{3,19},{19,3},{4,20},{20... | collective-permute-start | bytes 3145736 | tf_op jit(solution)/shard_map/ppermute | solution.py:628
  1073.7 50.5 %collective-permute-start.173 = (bf16[48,1152]{1,0:T(8,128)(2,1)}, bf16[48,1152]{1,0:T(8,128)(2,1)}, u32[]{:S(2)}, u32[]{:S(2)}) collective-permute-start(bf16[48,1152]{1,0:T(8,128)(2,1)} %fusion.169), channel_id=1, source_target_pairs={{0,4},{4,0},{1,5},{5,1},{2,6},{6,2},{3,7},{7,3},{8,12},{12,8},{9,1... | collective-permute-start | bytes 331784 | tf_op jit(solution)/shard_map/ppermute | solution.py:590
  1103.1 53.5 %collective-permute-start.178 = (bf16[256,288]{1,0:T(8,128)(2,1)}, bf16[256,288]{1,0:T(8,128)(2,1)}, u32[]{:S(2)}, u32[]{:S(2)}) collective-permute-start(bf16[256,288]{1,0:T(8,128)(2,1)} %add_convert_fusion), channel_id=1, source_target_pairs={{0,1},{1,0},{2,3},{3,2},{4,5},{5,4},{6,7},{7,6},{8,9},{9,8},{10,11... | collective-permute-start | bytes 442376 | tf_op jit(solution)/shard_map/ppermute | solution.py:1012
  1105.1 43.1 %collective-permute-start.162 = (bf16[2,48,2048]{2,1,0:T(8,128)(2,1)}, bf16[2,48,2048]{2,1,0:T(8,128)(2,1)S(1)}, u32[]{:S(2)}, u32[]{:S(2)}) collective-permute-start(bf16[2,48,2048]{2,1,0:T(8,128)(2,1)} %pad_maximum_fusion.45), channel_id=1, source_target_pairs={{1,17},{16,0},{3,19},{18,2},{5,21},{20,4},{7,23},{22,6},{9,25},{24... | collective-permute-start | bytes 1179656 | tf_op jit(solution)/shard_map/ppermute | solution.py:736
  1150.0 46.9 %all-to-all-start.15 = ((bf16[4,256,768]{1,2,0:T(8,128)(2,1)}), bf16[4,256,768]{1,2,0:T(8,128)(2,1)}, u32[]{:S(2)}, u32[]{:S(2)}) async-start(bf16[4,256,768]{1,2,0:T(8,128)(2,1)} %reduce-scatter.9.cloned.1.call-done), calls=%async_computation.19 | async-start | bytes 3145728 | tf_op jit(solution)/shard_map/all_to_all | solution.py:614
  (351 other events, 3107.7 us)
Sparse Core Ops, SparseCore 0:
  14.4 56.6 all-gather.7
  145.4 39.0 all-gather.9
  213.1 79.6 all-gather.11
  294.7 59.8 all-gather.13
  357.2 48.2 all-gather.15
  406.9 37.4 all-gather.17
  470.5 77.8 all-gather.19
  663.7 83.1 reduce-scatter.4
  760.3 89.2 reduce-scatter.6
  851.7 77.0 reduce-scatter.8
  937.4 43.6 reduce-scatter.10

commit v4 on v3

--- a/solution.py
+++ b/solution.py
@@ -710,7 +710,9 @@
             return jnp.repeat(jnp.moveaxis(split, axis, 0), plan.query_parts, axis=0)
 
         def join_query_heads(x, axis):
-            summed = jnp.sum(x.astype(f32).reshape((qheads, plan.query_parts) + x.shape[1:]), axis=1)
+            summed = jnp.sum(
+                x.astype(f32).reshape((qheads, plan.query_parts) + x.shape[1:]), axis=1
+            ).astype(bf16)
             joined = jnp.moveaxis(summed, 0, axis)
             shape = joined.shape
             return joined.reshape(shape[:axis] + (q_cols,) + shape[axis + 2 :])
@@ -842,7 +844,8 @@
         shares = [None] * LAYERS
         mix_own[0] = spread_first(after(blocks[0][0], hidden_rows))
         out_cols = HD + width
-        swapped = [[group_swap(x) for x in after(blocks[0][1:], hidden_rows)]]
+        hidden_all = gather_rows(hidden_rows)
+        swapped = [[group_swap(x) for x in after(blocks[0][1:], hidden_all)]]
         for layer in range(1, LAYERS):
             both = group_swap(jnp.concatenate(blocks[layer][:2], axis=2))
             swapped.append([both[:, :, -out_cols:], group_swap(blocks[layer][2])])
@@ -857,7 +860,7 @@
             rec = {}
             normed_f, rec["norm_one_back"] = jax.vjp(norm_piece, stream, gains[layer, 0])
             if layer == 0:
-                normed = norm_piece(gather_rows(hidden_rows).astype(f32), gains[0, 0]).astype(bf16)
+                normed = norm_piece(hidden_all.astype(f32), gains[0, 0]).astype(bf16)
             else:
                 normed = gather_rows(normed_f.astype(bf16))
             in_w = input_weights(*after((mix_own[layer], shares[layer]), normed))
@@ -1032,7 +1035,7 @@
                     join_query_heads(mix_came[:, :, :HD], 1),
                 ],
                 axis=1,
-            ).astype(f32)
+            )
             out = jnp.concatenate(
                 [join_heads(out_came[:, :, HD:], 1), join_query_heads(out_came[:, :, :HD], 1)],
                 axis=1,
@@ -1044,12 +1047,12 @@
                     for g in range(members)
                 ],
                 axis=1,
-            ).astype(f32)
+            )
             down = jnp.concatenate([ffn_came[g, :, 2 * ff_own :] for g in range(members)], axis=1)
-            return mix, out.T.astype(f32), up, down.T.astype(f32)
+            return mix, out.T, up, down.T
 
         by_layer = [weight_grads(layer) for layer in range(LAYERS)]
-        mix_g, out_g, up_g, down_g = (jnp.stack(grads) for grads in zip(*by_layer))
+        mix_g, out_g, up_g, down_g = (jnp.stack(grads).astype(f32) for grads in zip(*by_layer))
         gain_g, chan_g, conv_g, head_g = (jnp.stack(grads) for grads in zip(*out_grads))
         chan_rows = jnp.zeros((LAYERS, CONV + 2, HGROUPS, heads, replicas, lanes), f32)
         chan_rows = lax.dynamic_update_slice(

time: 1270 us -> 1250 us (0.984)
  waiting for transfers between devices: 415 us -> 383 us
    ppermute x5, waiting for transfers between devices: 23.5 us -> 1.88 us  [sum_over(): x = x + lax.ppermute(x, axis, SWAP)]
    ppermute x72, waiting for transfers between devices: 155 us -> 136 us  [gather_rows(): got = lax.ppermute(held, axis, SWAP)]
    ppermute x3, waiting for transfers between devices: 2.9 us -> 20 us  [gather_lanes(): got = lax.ppermute(x, axis, SWAP)]
    unnamed x374 -> x399, local copies, waits for them, and re-layouts: 75.5 us -> 71.4 us
  transfers between devices with their start and end apart: 207 -> 207, of which waited for: 108 -> 104; matrix products, arithmetic and copies ran while one was open for 31% -> 32% of each run, Pallas kernels for 7% -> 7%
where the time goes in v4:
time: 1250 us; the launch traced here: 1240 us
  waiting for transfers between devices  383 us (31%)
  starting transfers between devices  307 us (25%)
  local copies, waits for them, and re-layouts  222 us (18%)
  other arithmetic  143 us (11%)
  Pallas kernels  86 us (7%)
  matrix products  79.5 us (6%)
  between operations  19.1 us (2%)
    ppermute x72, waiting for transfers between devices, gather_rows(): got = lax.ppermute(held, axis, SWAP)  136 us
    ppermute x72, waiting for transfers between devices, scatter_product(): got = lax.ppermute(pick(piece, dim, 1 - index).astype(bf16), axis, SWAP)  116 us
    ppermute x72, starting transfers between devices, gather_rows(): got = lax.ppermute(held, axis, SWAP)  95.7 us
    ppermute x72, starting transfers between devices, scatter_product(): got = lax.ppermute(pick(piece, dim, 1 - index).astype(bf16), axis, SWAP)  93 us
    unnamed x399, local copies, waits for them, and re-layouts  71.4 us
    pallas_call x8, Pallas kernels, call_whole(): pl.pallas_call(kernel, grid=(1,), in_specs=[pl.BlockSpec(memory_space=plt...  66.1 us
    dot_general x16, matrix products, matmul_nt(): lax.dot_general(left_op, right_op, (((1,), (1,)), ((), ())), preferred_el...  40.3 us
    dot_general x8, matrix products, matmul(): return jnp.dot(left_op, right_op, preferred_element_type=f32)  39.1 us
  transfers between devices with their start and end apart: 207, of which 104 were waited for; matrix products, arithmetic and copies ran while one was open for 32% of the time, Pallas kernels for 7%

profile of v4, /device:TPU:0, one launch (start us, length us, event | category | flops | bytes accessed | tf_op | source)
XLA Modules:
  0.0 1240.9 jit_solution(14421775347760982197)
XLA Ops:
  31.6 6.7 all-to-all-done.4
  49.3 19.1 %collective-permute-done.1 = bf16[2,2,512]{2,1,0:T(2,128)(2,1)S(1)} collective-permute-done((bf16[2,2,512]{2,1,0:T(2,128)(2,1)S(1)}, bf16[2,2,512]{2,1,0:T(2,128)(2,1)S(1)}, u32[]{:S(2)}, u32[]{:S(2)}) %collective-permute-start.1) | collective-permute-done | bytes 4128 | tf_op jit(solution)/shard_map/ppermute | solution.py:633
  103.7 8.2 collective-permute-done.5
  117.6 16.9 %collective-permute-done.11 = bf16[1,1,2,48,768]{4,3,2,1,0:T(8,128)(2,1)S(1)} collective-permute-done((bf16[1,1,2,48,768]{4,3,2,1,0:T(8,128)(2,1)S(1)}, bf16[1,1,2,48,768]{4,3,2,1,0:T(8,128)(2,1)S(1)}, u32[]{:S(2)}, u32[]{:S(2)}) %collective-permute-start.11) | collective-permute-done | bytes 147488 | tf_op jit(solution)/shard_map/ppermute | solution.py:560
  161.3 7.1 fusion.235.mixed
  168.4 8.6 shard_map.204
  177.8 11.8 all-to-all-done.2
  260.4 8.0 collective-permute-done.29
  274.5 22.1 %all-gather.12.cloned.1.call-done = bf16[8,256,768]{2,1,0:T(8,128)(2,1)} async-done(((bf16[4,256,768]{2,1,0:T(8,128)(2,1)}), bf16[8,256,768]{2,1,0:T(8,128)(2,1)}) %all-gather.12.cloned.1.call-update) | async-done | bytes 3145744 | tf_op jit(solution)/shard_map/all_gather | solution.py:617
  318.9 6.8 collective-permute-done.35
  350.5 9.1 collective-permute-done.44
  388.0 21.3 %all-gather.16.cloned.1.call-done = bf16[2048,816]{0,1:T(8,128)(2,1)} async-done(((bf16[128,816]{0,1:T(8,128)(2,1)}), bf16[2048,816]{0,1:T(8,128)(2,1)}) %all-gather.16.cloned.1.call-update) | async-done | bytes 3342352 | tf_op jit(solution)/shard_map/all_gather | solution.py:820
  419.2 10.7 fusion.229.mixed
  429.9 8.5 shard_map.206
  490.9 10.6 collective-permute-done.55
  503.0 6.7 collective-permute-done.61
  543.6 11.5 collective-permute-done.71
  696.0 16.0 %shard_map.210 = (bf16[768,512]{1,0:T(8,128)(2,1)}, bf16[768,384]{1,0:T(8,128)(2,1)}, bf16[768,128]{1,0:T(8,128)(2,1)}, f32[8,192]{1,0:T(8,128)}, f32[8,512]{1,0:T(8,128)}, /*index=5*/f32[8,128]{1,0:T(8,128)}) custom-call(s32[1]{0:T(128)} %bitcast.72.core_ref, f32[768,1408]{1,0:T(8,128)} %fusion.229.mixed, f32[8,192]{1,0:T(8,128)} %get-tuple-element.382.taps, ...), custom_call_target="tpu_custom_call" | custom-call | flops 13271040000 | bytes 6291456 | tf_op jit(solution)/shard_map/pallas_call | solution.py:408
  820.7 7.0 collective-permute-done.130
  893.1 8.7 collective-permute-done.150
  957.1 16.0 %shard_map.216 = (bf16[768,512]{1,0:T(8,128)(2,1)}, bf16[768,384]{1,0:T(8,128)(2,1)}, bf16[768,128]{1,0:T(8,128)(2,1)}, f32[8,192]{1,0:T(8,128)}, f32[8,512]{1,0:T(8,128)}, /*index=5*/f32[8,128]{1,0:T(8,128)}) custom-call(s32[1]{0:T(128)} %bitcast.72.core_ref, f32[768,1408]{1,0:T(8,128)} %fusion.235.mixed, f32[8,192]{1,0:T(8,128)} %get-tuple-element.383.taps, ...), custom_call_target="tpu_custom_call" | custom-call | flops 13271040000 | bytes 6291456 | tf_op jit(solution)/shard_map/pallas_call | solution.py:408
  992.2 6.6 convolution_convert_fusion.2
  1067.6 9.2 collective-permute-done.172
  1163.3 14.8 %collective-permute-done.164 = bf16[2,2,48,2048]{3,2,0,1:T(8,128)(2,1)S(1)} collective-permute-done((bf16[2,2,48,2048]{3,2,0,1:T(8,128)(2,1)S(1)}, bf16[2,2,48,2048]{3,2,0,1:T(8,128)(2,1)S(1)}, u32[]{:S(2)}, u32[]{:S(2)}) %collective-permute-start.164) | collective-permute-done | bytes 786464 | tf_op jit(solution)/shard_map/ppermute | solution.py:742
  (1460 shorter events, 949.9 us)
Async XLA Ops:
  7.2 149.1 %all-gather.8.cloned.1.call-start = ((), (), s32[]{:S(2)}) async-start(), calls=%async_computation.20 | async-start | bytes 3551232 | tf_op jit(solution)/shard_map/all_gather | solution.py:820
  7.2 39.3 %collective-permute-start = (bf16[2,2,256]{2,1,0:T(2,128)(2,1)}, bf16[2,2,256]{2,1,0:T(2,128)(2,1)S(1)}, u32[]{:S(2)}, u32[]{:S(2)}) collective-permute-start(bf16[2,2,256]{2,1,0:T(2,128)(2,1)} %param.15), channel_id=1, source_target_pairs={{0,4},{4,0},{1,5},{5,1},{2,6},{6,2},{3,7},{7,3},{8,12},{12,8},{9,1... | collective-permute-start | bytes 6152 | tf_op jit(solution)/shard_map/ppermute | solution.py:633
  38.3 55.9 %all-to-all-start.1 = ((bf16[4,256,768]{2,1,0:T(8,128)(2,1)}), bf16[4,256,768]{2,1,0:T(8,128)(2,1)S(1)}, u32[]{:S(2)}, u32[]{:S(2)}) async-start(bf16[4,256,768]{2,1,0:T(8,128)(2,1)} %pad_maximum_fusion.16), calls=%async_computation.1 | async-start | bytes 3145728 | tf_op jit(solution)/shard_map/all_to_all | solution.py:614
  94.2 54.2 %all-to-all-start = ((bf16[8,256,512]{1,2,0:T(8,128)(2,1)}), bf16[8,256,512]{1,2,0:T(8,128)(2,1)}, u32[]{:S(2)}, u32[]{:S(2)}) async-start(bf16[8,256,512]{1,2,0:T(8,128)(2,1)} %pad_maximum_fusion.13), calls=%async_computation | async-start | bytes 4194304 | tf_op jit(solution)/shard_map/all_to_all | solution.py:620
  100.0 97.2 %all-gather.10.cloned.1.call-start = ((), (), s32[]{:S(2)}) async-start(), calls=%async_computation.21 | async-start | bytes 1966080 | tf_op jit(solution)/shard_map/all_gather | solution.py:617
  148.4 41.2 %all-to-all-start.2 = ((bf16[4,256,832]{1,2,0:T(8,128)(2,1)}), bf16[4,256,832]{1,2,0:T(8,128)(2,1)}, u32[]{:S(2)}, u32[]{:S(2)}) async-start(bf16[4,256,832]{1,2,0:T(8,128)(2,1)} %constant_dynamic-update-slice_fusion), calls=%async_computation.2 | async-start | bytes 3407872 | tf_op jit(solution)/shard_map/all_to_all | solution.py:614
  193.8 102.9 %all-gather.12.cloned.1.call-start = ((), (), s32[]{:S(2)}) async-start(), calls=%async_computation.22 | async-start | bytes 4718592 | tf_op jit(solution)/shard_map/all_gather | solution.py:617
  216.6 171.4 %all-gather.14.cloned.1.call-start = ((), (), s32[]{:S(2)}) async-start(), calls=%async_computation.23 | async-start | bytes 3145728 | tf_op jit(solution)/shard_map/all_gather | solution.py:617
  272.0 137.3 %all-gather.16.cloned.1.call-start = ((), (), s32[]{:S(2)}) async-start(), calls=%async_computation.24 | async-start | bytes 3551232 | tf_op jit(solution)/shard_map/all_gather | solution.py:820
  309.1 145.9 %all-gather.18.cloned.1.call-start = ((), (), s32[]{:S(2)}) async-start(), calls=%async_computation.25 | async-start | bytes 1966080 | tf_op jit(solution)/shard_map/all_gather | solution.py:617
  454.8 124.0 %all-gather.20.cloned.1.call-start = ((), (), s32[]{:S(2)}) async-start(), calls=%async_computation.26 | async-start | bytes 4718592 | tf_op jit(solution)/shard_map/all_gather | solution.py:617
  474.3 322.5 %reduce-scatter.5.cloned.1.call-start = ((), (), s32[]{:S(2)}) async-start(), calls=%async_computation.27 | async-start | bytes 4718592 | tf_op jit(solution)/shard_map/reduce_scatter | solution.py:623
  479.7 75.4 %collective-permute-start.89 = (bf16[1,2,1,48,640]{4,3,2,1,0:T(8,128)(2,1)S(1)}, bf16[1,2,1,48,640]{4,3,2,1,0:T(8,128)(2,1)S(1)}, u32[]{:S(2)}, u32[]{:S(2)}) collective-permute-start(bf16[1,2,1,48,640]{4,3,2,1,0:T(8,128)(2,1)S(1)} %maximum_select_fusion.82), channel_id=1, source_target_pairs={{0,2},{2,0},{1,3},{3,1},{4,6},{6,4},{5,7},{7,5},{8,10},{10,8},{9,1... | collective-permute-start | bytes 368648 | tf_op jit(solution)/shard_map/ppermute | solution.py:560
  483.1 81.4 %collective-permute-start.92 = (bf16[1,1,2,48,768]{4,3,2,1,0:T(8,128)(2,1)S(1)}, bf16[1,1,2,48,768]{4,3,2,1,0:T(8,128)(2,1)S(1)}, u32[]{:S(2)}, u32[]{:S(2)}) collective-permute-start(bf16[1,1,2,48,768]{4,3,2,1,0:T(8,128)(2,1)S(1)} %maximum_select_fusion.61), channel_id=1, source_target_pairs={{0,8},{8,0},{1,9},{9,1},{2,10},{10,2},{3,11},{11,3},{4,12},{12,4},... | collective-permute-start | bytes 442376 | tf_op jit(solution)/shard_map/ppermute | solution.py:560
  488.1 78.1 %collective-permute-start.87 = (bf16[2,2,1,48,640]{4,3,0,2,1:T(8,128)(2,1)S(1)}, bf16[2,2,1,48,640]{4,3,0,2,1:T(8,128)(2,1)S(1)}, u32[]{:S(2)}, u32[]{:S(2)}) collective-permute-start(bf16[2,2,1,48,640]{4,3,0,2,1:T(8,128)(2,1)S(1)} %maximum_select_fusion.44), channel_id=1, source_target_pairs={{0,2},{2,0},{1,3},{3,1},{4,6},{6,4},{5,7},{7,5},{8,10},{10,8},{9,1... | collective-permute-start | bytes 737288 | tf_op jit(solution)/shard_map/ppermute | solution.py:560
  681.1 193.9 %reduce-scatter.7.cloned.1.call-start = ((), (), s32[]{:S(2)}) async-start(), calls=%async_computation.28 | async-start | bytes 5111808 | tf_op jit(solution)/shard_map/reduce_scatter | solution.py:623
  764.0 223.7 %reduce-scatter.9.cloned.1.call-start = ((), (), s32[]{:S(2)}) async-start(), calls=%async_computation.29 | async-start | bytes 4718592 | tf_op jit(solution)/shard_map/reduce_scatter | solution.py:623
  932.8 66.1 %reduce-scatter.11.cloned.1.call-start = ((), (), s32[]{:S(2)}) async-start(), calls=%async_computation.30 | async-start | bytes 1966080 | tf_op jit(solution)/shard_map/reduce_scatter | solution.py:623
  946.8 40.9 %all-to-all-start.14 = ((bf16[16,48,288]{2,1,0:T(8,128)(2,1)}), bf16[16,48,288]{2,1,0:T(8,128)(2,1)}, u32[]{:S(2)}, u32[]{:S(2)}) async-start(bf16[16,48,288]{2,1,0:T(8,128)(2,1)} %bitcast.1081), calls=%async_computation.18 | async-start | bytes 1179648 | tf_op jit(solution)/shard_map/all_to_all | solution.py:730
  1009.4 84.7 %collective-permute-start.177 = (bf16[256,288]{1,0:T(8,128)(2,1)}, bf16[256,288]{1,0:T(8,128)(2,1)}, u32[]{:S(2)}, u32[]{:S(2)}) collective-permute-start(bf16[256,288]{1,0:T(8,128)(2,1)} %shard_map.222), channel_id=1, source_target_pairs={{0,16},{16,0},{1,17},{17,1},{2,18},{18,2},{3,19},{19,3},{4,20},{20... | collective-permute-start | bytes 442376 | tf_op jit(solution)/shard_map/ppermute | solution.py:1009
  1017.0 62.8 %all-to-all-start.12 = ((bf16[4,256,832]{1,2,0:T(8,128)(2,1)}), bf16[4,256,832]{1,2,0:T(8,128)(2,1)}, u32[]{:S(2)}, u32[]{:S(2)}) async-start(bf16[4,256,832]{1,2,0:T(8,128)(2,1)} %reduce-scatter.7.cloned.1.call-done), calls=%async_computation.16 | async-start | bytes 3407872 | tf_op jit(solution)/shard_map/all_to_all | solution.py:614
  1044.6 48.0 %collective-permute-start.170 = (bf16[4,256,512]{1,2,0:T(8,128)(2,1)}, bf16[4,256,512]{1,2,0:T(8,128)(2,1)}, u32[]{:S(2)}, u32[]{:S(2)}) collective-permute-start(bf16[4,256,512]{1,2,0:T(8,128)(2,1)} %bitcast.1123), channel_id=1, source_target_pairs={{0,16},{16,0},{1,17},{17,1},{2,18},{18,2},{3,19},{19,3},{4,20},{20... | collective-permute-start | bytes 3145736 | tf_op jit(solution)/shard_map/ppermute | solution.py:628
  1077.5 50.4 %collective-permute-start.173 = (bf16[48,1152]{1,0:T(8,128)(2,1)}, bf16[48,1152]{1,0:T(8,128)(2,1)}, u32[]{:S(2)}, u32[]{:S(2)}) collective-permute-start(bf16[48,1152]{1,0:T(8,128)(2,1)} %fusion.177), channel_id=1, source_target_pairs={{0,4},{4,0},{1,5},{5,1},{2,6},{6,2},{3,7},{7,3},{8,12},{12,8},{9,1... | collective-permute-start | bytes 331784 | tf_op jit(solution)/shard_map/ppermute | solution.py:590
  1102.0 41.6 %collective-permute-start.178 = (bf16[256,288]{1,0:T(8,128)(2,1)}, bf16[256,288]{1,0:T(8,128)(2,1)}, u32[]{:S(2)}, u32[]{:S(2)}) collective-permute-start(bf16[256,288]{1,0:T(8,128)(2,1)} %add_convert_fusion), channel_id=1, source_target_pairs={{0,1},{1,0},{2,3},{3,2},{4,5},{5,4},{6,7},{7,6},{8,9},{9,8},{10,11... | collective-permute-start | bytes 442376 | tf_op jit(solution)/shard_map/ppermute | solution.py:1015
  (359 other events, 3181.3 us)
Sparse Core Ops, SparseCore 0:
  14.4 66.9 all-gather.7
  147.2 39.0 all-gather.9
  216.7 79.9 all-gather.11
  298.6 59.8 all-gather.13
  361.1 48.2 all-gather.15
  410.8 37.4 all-gather.17
  474.4 77.8 all-gather.19
  667.6 83.2 reduce-scatter.4
  764.1 89.2 reduce-scatter.6
  855.5 77.0 reduce-scatter.8
  941.3 43.5 reduce-scatter.10

commit v5 on v4

--- a/solution.py
+++ b/solution.py
@@ -72,6 +72,11 @@
 
 def after(x, point):
     return lax.optimization_barrier((x, point))[0]
+
+
+def following(x, *points):
+    zero = sum(jnp.minimum(jnp.abs(p.reshape(-1)[0].astype(f32)), 0.0) for p in points)
+    return x + zero.astype(x.dtype)
 
 
 def pick(x, dim, index):
@@ -842,13 +847,17 @@
         out_own = [None] * LAYERS
         ffn_own = [None] * LAYERS
         shares = [None] * LAYERS
-        mix_own[0] = spread_first(after(blocks[0][0], hidden_rows))
+        mix_own[0] = spread_first(following(blocks[0][0], hidden_rows, gains))
         out_cols = HD + width
         hidden_all = gather_rows(hidden_rows)
-        swapped = [[group_swap(x) for x in after(blocks[0][1:], hidden_all)]]
+        first_out = group_swap(following(blocks[0][1], mix_own[0]))
+        first_ffn = group_swap(following(blocks[0][2], first_out))
+        swapped = [[first_out, first_ffn]]
         for layer in range(1, LAYERS):
-            both = group_swap(jnp.concatenate(blocks[layer][:2], axis=2))
-            swapped.append([both[:, :, -out_cols:], group_swap(blocks[layer][2])])
+            both = jnp.concatenate(blocks[layer][:2], axis=2)
+            both = group_swap(following(both, swapped[-1][1]))
+            ffn_came = group_swap(following(blocks[layer][2], both))
+            swapped.append([both[:, :, -out_cols:], ffn_came])
             mix_own[layer] = both_halves(both[:, :, :-out_cols])
         for layer in range(LAYERS):
             shares[layer] = share_whole(share_rows[layer])

time: 1250 us -> 1310 us (1.048)
  local copies, waits for them, and re-layouts: 222 us -> 245 us
  other arithmetic: 143 us -> 157 us
    all_gather x5, waiting for transfers between devices: 22.2 us -> 93.1 us  [both_halves(): return lax.all_gather(came, half_axis, axis=0, tiled=True)]
    all_gather x2, waiting for transfers between devices: 21.4 us -> 0.02 us  [share_whole(): return lax.all_gather(share, ctx_axes + (t_core,), axis=0, tiled=True)]
    ppermute x3, waiting for transfers between devices: 20 us -> 2.95 us  [gather_lanes(): got = lax.ppermute(x, axis, SWAP)]
    unnamed x399 -> x410, local copies, waits for them, and re-layouts: 71.4 us -> 69.9 us
  transfers between devices with their start and end apart: 207 -> 207, of which waited for: 104 -> 105; matrix products, arithmetic and copies ran while one was open for 32% -> 33% of each run, Pallas kernels for 7% -> 6%
where the time goes in v5:
time: 1310 us; the launch traced here: 1290 us
  waiting for transfers between devices  395 us (30%)
  starting transfers between devices  304 us (23%)
  local copies, waits for them, and re-layouts  245 us (19%)
  other arithmetic  157 us (12%)
  Pallas kernels  85.6 us (7%)
  matrix products  82.1 us (6%)
  between operations  24.6 us (2%)
    ppermute x72, waiting for transfers between devices, gather_rows(): got = lax.ppermute(held, axis, SWAP)  123 us
    ppermute x72, waiting for transfers between devices, scatter_product(): got = lax.ppermute(pick(piece, dim, 1 - index).astype(bf16), axis, SWAP)  112 us
    all_gather x5, waiting for transfers between devices, both_halves(): return lax.all_gather(came, half_axis, axis=0, tiled=True)  93.1 us
    ppermute x72, starting transfers between devices, gather_rows(): got = lax.ppermute(held, axis, SWAP)  93.1 us
    ppermute x72, starting transfers between devices, scatter_product(): got = lax.ppermute(pick(piece, dim, 1 - index).astype(bf16), axis, SWAP)  92.1 us
    unnamed x410, local copies, waits for them, and re-layouts  69.9 us
    pallas_call x8, Pallas kernels, call_whole(): pl.pallas_call(kernel, grid=(1,), in_specs=[pl.BlockSpec(memory_space=plt...  65.7 us
    dot_general x8, matrix products, matmul(): return jnp.dot(left_op, right_op, preferred_element_type=f32)  41.7 us
  transfers between devices with their start and end apart: 207, of which 105 were waited for; matrix products, arithmetic and copies ran while one was open for 33% of the time, Pallas kernels for 6%

profile of v5, /device:TPU:0, one launch (start us, length us, event | category | flops | bytes accessed | tf_op | source)
XLA Modules:
  0.0 1293.7 jit_solution(6996235123354256971)
XLA Ops:
  52.7 17.8 %all-to-all-start = ((bf16[8,256,512]{2,1,0:T(8,128)(2,1)}), bf16[8,256,512]{2,1,0:T(8,128)(2,1)S(1)}, u32[]{:S(2)}, u32[]{:S(2)}) async-start(bf16[8,256,512]{2,1,0:T(8,128)(2,1)} %pad_maximum_fusion.13), calls=%async_computation | async-start | bytes 4194304 | tf_op jit(solution)/shard_map/all_to_all | solution.py:625
  82.1 15.7 %collective-permute-done.4 = bf16[1,1,1,48,640]{4,3,2,1,0:T(8,128)(2,1)S(1)} collective-permute-done((bf16[1,1,1,48,640]{4,3,2,1,0:T(8,128)(2,1)S(1)}, bf16[1,1,1,48,640]{4,3,2,1,0:T(8,128)(2,1)S(1)}, u32[]{:S(2)}, u32[]{:S(2)}) %collective-permute-start.4) | collective-permute-done | bytes 61472 | tf_op jit(solution)/shard_map/ppermute | solution.py:565
  133.8 6.3 all-to-all-done.1
  162.9 9.7 fusion.234.mixed
  172.5 8.5 shard_map.204
  203.5 37.2 %all-gather.10.cloned.1.call-done = bf16[8,256,320]{1,2,0:T(8,128)(2,1)} async-done(((bf16[4,256,320]{1,2,0:T(8,128)(2,1)}), bf16[8,256,320]{1,2,0:T(8,128)(2,1)}) %all-gather.10.cloned.1.call-update) | async-done | bytes 1310736 | tf_op jit(solution)/shard_map/all_gather | solution.py:622
  306.5 7.8 collective-permute-done.29
  319.5 20.8 %all-gather.12.cloned.1.call-done = bf16[8,256,768]{2,1,0:T(8,128)(2,1)} async-done(((bf16[4,256,768]{2,1,0:T(8,128)(2,1)}), bf16[8,256,768]{2,1,0:T(8,128)(2,1)}) %all-gather.12.cloned.1.call-update) | async-done | bytes 3145744 | tf_op jit(solution)/shard_map/all_gather | solution.py:622
  434.1 35.1 %all-gather.14.cloned.1.call-done = bf16[8,256,512]{2,1,0:T(8,128)(2,1)} async-done(((bf16[4,256,512]{2,1,0:T(8,128)(2,1)}), bf16[8,256,512]{2,1,0:T(8,128)(2,1)}) %all-gather.14.cloned.1.call-update) | async-done | bytes 2097168 | tf_op jit(solution)/shard_map/all_gather | solution.py:622
  478.0 10.6 fusion.228.mixed
  488.6 8.5 shard_map.206
  529.0 6.0 all-to-all-done.6
  551.5 10.9 collective-permute-done.55
  563.9 6.3 collective-permute-done.61
  592.4 19.7 %collective-permute-done.64 = bf16[1,1,1,48,640]{4,3,0,2,1:T(8,128)(2,1)S(1)} collective-permute-done((bf16[1,1,1,48,640]{4,3,0,2,1:T(8,128)(2,1)S(1)}, bf16[1,1,1,48,640]{4,3,0,2,1:T(8,128)(2,1)S(1)}, u32[]{:S(2)}, u32[]{:S(2)}) %collective-permute-start.64) | collective-permute-done | bytes 61472 | tf_op jit(solution)/shard_map/ppermute | solution.py:565
  632.5 7.6 collective-permute-done.93
  756.6 16.0 %shard_map.210 = (bf16[768,512]{1,0:T(8,128)(2,1)}, bf16[768,384]{1,0:T(8,128)(2,1)}, bf16[768,128]{1,0:T(8,128)(2,1)}, f32[8,192]{1,0:T(8,128)}, f32[8,512]{1,0:T(8,128)}, /*index=5*/f32[8,128]{1,0:T(8,128)}) custom-call(s32[1]{0:T(128)} %bitcast.77.core_ref, f32[768,1408]{1,0:T(8,128)} %fusion.228.mixed, f32[8,192]{1,0:T(8,128)} %get-tuple-element.389.taps, ...), custom_call_target="tpu_custom_call" | custom-call | flops 13271040000 | bytes 6291456 | tf_op jit(solution)/shard_map/pallas_call | solution.py:413
  951.9 6.7 collective-permute-done.150
  1015.1 16.0 %shard_map.216 = (bf16[768,512]{1,0:T(8,128)(2,1)}, bf16[768,384]{1,0:T(8,128)(2,1)}, bf16[768,128]{1,0:T(8,128)(2,1)}, f32[8,192]{1,0:T(8,128)}, f32[8,512]{1,0:T(8,128)}, /*index=5*/f32[8,128]{1,0:T(8,128)}) custom-call(s32[1]{0:T(128)} %bitcast.77.core_ref, f32[768,1408]{1,0:T(8,128)} %fusion.234.mixed, f32[8,192]{1,0:T(8,128)} %get-tuple-element.390.taps, ...), custom_call_target="tpu_custom_call" | custom-call | flops 13271040000 | bytes 6291456 | tf_op jit(solution)/shard_map/pallas_call | solution.py:413
  1050.2 6.6 convolution_convert_fusion.2
  1119.2 11.3 collective-permute-done.172
  1203.4 6.6 all-to-all-start.15
  1215.6 14.7 %collective-permute-done.164 = bf16[2,2,48,2048]{3,2,0,1:T(8,128)(2,1)S(1)} collective-permute-done((bf16[2,2,48,2048]{3,2,0,1:T(8,128)(2,1)S(1)}, bf16[2,2,48,2048]{3,2,0,1:T(8,128)(2,1)S(1)}, u32[]{:S(2)}, u32[]{:S(2)}) %collective-permute-start.164) | collective-permute-done | bytes 786464 | tf_op jit(solution)/shard_map/ppermute | solution.py:747
  1277.4 6.6 collective-permute-done.176
  (1486 shorter events, 956.3 us)
Async XLA Ops:
  8.0 145.0 %all-gather.8.cloned.1.call-start = ((), (), s32[]{:S(2)}) async-start(), calls=%async_computation.20 | async-start | bytes 3551232 | tf_op jit(solution)/shard_map/all_gather | solution.py:825
  52.7 70.1 %all-to-all-start = ((bf16[8,256,512]{2,1,0:T(8,128)(2,1)}), bf16[8,256,512]{2,1,0:T(8,128)(2,1)S(1)}, u32[]{:S(2)}, u32[]{:S(2)}) async-start(bf16[8,256,512]{2,1,0:T(8,128)(2,1)} %pad_maximum_fusion.13), calls=%async_computation | async-start | bytes 4194304 | tf_op jit(solution)/shard_map/all_to_all | solution.py:625
  145.5 36.5 %all-to-all-start.2 = ((bf16[4,256,768]{2,1,0:T(8,128)(2,1)}), bf16[4,256,768]{2,1,0:T(8,128)(2,1)}, u32[]{:S(2)}, u32[]{:S(2)}) async-start(bf16[4,256,768]{2,1,0:T(8,128)(2,1)} %maximum_add_fusion.2), calls=%async_computation.2 | async-start | bytes 3145728 | tf_op jit(solution)/shard_map/all_to_all | solution.py:619
  194.1 50.4 %all-to-all-start.3 = ((bf16[4,256,832]{1,2,0:T(8,128)(2,1)}), bf16[4,256,832]{1,2,0:T(8,128)(2,1)S(1)}, u32[]{:S(2)}, u32[]{:S(2)}) async-start(bf16[4,256,832]{1,2,0:T(8,128)(2,1)} %broadcast_add_fusion), calls=%async_computation.3 | async-start | bytes 3407872 | tf_op jit(solution)/shard_map/all_to_all | solution.py:619
  198.4 42.3 %all-gather.10.cloned.1.call-start = ((), (), s32[]{:S(2)}) async-start(), calls=%async_computation.21 | async-start | bytes 1966080 | tf_op jit(solution)/shard_map/all_gather | solution.py:622
  198.9 141.3 %all-gather.12.cloned.1.call-start = ((), (), s32[]{:S(2)}) async-start(), calls=%async_computation.22 | async-start | bytes 4718592 | tf_op jit(solution)/shard_map/all_gather | solution.py:622
  261.1 172.9 %all-gather.16.cloned.1.call-start = ((), (), s32[]{:S(2)}) async-start(), calls=%async_computation.24 | async-start | bytes 3551232 | tf_op jit(solution)/shard_map/all_gather | solution.py:825
  352.6 116.5 %all-gather.14.cloned.1.call-start = ((), (), s32[]{:S(2)}) async-start(), calls=%async_computation.23 | async-start | bytes 3145728 | tf_op jit(solution)/shard_map/all_gather | solution.py:622
  407.8 107.8 %all-gather.18.cloned.1.call-start = ((), (), s32[]{:S(2)}) async-start(), calls=%async_computation.25 | async-start | bytes 1966080 | tf_op jit(solution)/shard_map/all_gather | solution.py:622
  515.4 129.5 %all-gather.20.cloned.1.call-start = ((), (), s32[]{:S(2)}) async-start(), calls=%async_computation.26 | async-start | bytes 4718592 | tf_op jit(solution)/shard_map/all_gather | solution.py:622
  535.0 322.8 %reduce-scatter.5.cloned.1.call-start = ((), (), s32[]{:S(2)}) async-start(), calls=%async_computation.27 | async-start | bytes 4718592 | tf_op jit(solution)/shard_map/reduce_scatter | solution.py:628
  540.4 83.1 %collective-permute-start.89 = (bf16[1,2,1,48,640]{4,3,2,1,0:T(8,128)(2,1)S(1)}, bf16[1,2,1,48,640]{4,3,2,1,0:T(8,128)(2,1)S(1)}, u32[]{:S(2)}, u32[]{:S(2)}) collective-permute-start(bf16[1,2,1,48,640]{4,3,2,1,0:T(8,128)(2,1)S(1)} %maximum_select_fusion.82), channel_id=1, source_target_pairs={{0,2},{2,0},{1,3},{3,1},{4,6},{6,4},{5,7},{7,5},{8,10},{10,8},{9,1... | collective-permute-start | bytes 368648 | tf_op jit(solution)/shard_map/ppermute | solution.py:565
  543.8 86.8 %collective-permute-start.92 = (bf16[1,1,2,48,768]{4,3,2,1,0:T(8,128)(2,1)S(1)}, bf16[1,1,2,48,768]{4,3,2,1,0:T(8,128)(2,1)S(1)}, u32[]{:S(2)}, u32[]{:S(2)}) collective-permute-start(bf16[1,1,2,48,768]{4,3,2,1,0:T(8,128)(2,1)S(1)} %maximum_select_fusion.61), channel_id=1, source_target_pairs={{0,8},{8,0},{1,9},{9,1},{2,10},{10,2},{3,11},{11,3},{4,12},{12,4},... | collective-permute-start | bytes 442376 | tf_op jit(solution)/shard_map/ppermute | solution.py:565
  548.7 83.6 %collective-permute-start.87 = (bf16[2,2,1,48,640]{4,3,0,2,1:T(8,128)(2,1)S(1)}, bf16[2,2,1,48,640]{4,3,0,2,1:T(8,128)(2,1)S(1)}, u32[]{:S(2)}, u32[]{:S(2)}) collective-permute-start(bf16[2,2,1,48,640]{4,3,0,2,1:T(8,128)(2,1)S(1)} %maximum_select_fusion.44), channel_id=1, source_target_pairs={{0,2},{2,0},{1,3},{3,1},{4,6},{6,4},{5,7},{7,5},{8,10},{10,8},{9,1... | collective-permute-start | bytes 737288 | tf_op jit(solution)/shard_map/ppermute | solution.py:565
  744.8 186.9 %reduce-scatter.7.cloned.1.call-start = ((), (), s32[]{:S(2)}) async-start(), calls=%async_computation.28 | async-start | bytes 5111808 | tf_op jit(solution)/shard_map/reduce_scatter | solution.py:628
  824.0 221.8 %reduce-scatter.9.cloned.1.call-start = ((), (), s32[]{:S(2)}) async-start(), calls=%async_computation.29 | async-start | bytes 4718592 | tf_op jit(solution)/shard_map/reduce_scatter | solution.py:628
  990.7 66.1 %reduce-scatter.11.cloned.1.call-start = ((), (), s32[]{:S(2)}) async-start(), calls=%async_computation.30 | async-start | bytes 1966080 | tf_op jit(solution)/shard_map/reduce_scatter | solution.py:628
  1004.8 40.9 %all-to-all-start.14 = ((bf16[16,48,288]{2,1,0:T(8,128)(2,1)}), bf16[16,48,288]{2,1,0:T(8,128)(2,1)}, u32[]{:S(2)}, u32[]{:S(2)}) async-start(bf16[16,48,288]{2,1,0:T(8,128)(2,1)} %bitcast.1094), calls=%async_computation.18 | async-start | bytes 1179648 | tf_op jit(solution)/shard_map/all_to_all | solution.py:735
  1067.4 80.8 %collective-permute-start.177 = (bf16[256,288]{1,0:T(8,128)(2,1)}, bf16[256,288]{1,0:T(8,128)(2,1)}, u32[]{:S(2)}, u32[]{:S(2)}) collective-permute-start(bf16[256,288]{1,0:T(8,128)(2,1)} %shard_map.222), channel_id=1, source_target_pairs={{0,16},{16,0},{1,17},{17,1},{2,18},{18,2},{3,19},{19,3},{4,20},{20... | collective-permute-start | bytes 442376 | tf_op jit(solution)/shard_map/ppermute | solution.py:1018
  1070.9 62.8 %all-to-all-start.12 = ((bf16[4,256,832]{1,2,0:T(8,128)(2,1)}), bf16[4,256,832]{1,2,0:T(8,128)(2,1)}, u32[]{:S(2)}, u32[]{:S(2)}) async-start(bf16[4,256,832]{1,2,0:T(8,128)(2,1)} %reduce-scatter.7.cloned.1.call-done), calls=%async_computation.16 | async-start | bytes 3407872 | tf_op jit(solution)/shard_map/all_to_all | solution.py:619
  1098.4 48.3 %collective-permute-start.170 = (bf16[4,256,512]{1,2,0:T(8,128)(2,1)}, bf16[4,256,512]{1,2,0:T(8,128)(2,1)}, u32[]{:S(2)}, u32[]{:S(2)}) collective-permute-start(bf16[4,256,512]{1,2,0:T(8,128)(2,1)} %bitcast.1135), channel_id=1, source_target_pairs={{0,16},{16,0},{1,17},{17,1},{2,18},{18,2},{3,19},{19,3},{4,20},{20... | collective-permute-start | bytes 3145736 | tf_op jit(solution)/shard_map/ppermute | solution.py:633
  1131.3 48.8 %collective-permute-start.173 = (bf16[48,1152]{1,0:T(8,128)(2,1)}, bf16[48,1152]{1,0:T(8,128)(2,1)}, u32[]{:S(2)}, u32[]{:S(2)}) collective-permute-start(bf16[48,1152]{1,0:T(8,128)(2,1)} %fusion.177), channel_id=1, source_target_pairs={{0,4},{4,0},{1,5},{5,1},{2,6},{6,2},{3,7},{7,3},{8,12},{12,8},{9,1... | collective-permute-start | bytes 331784 | tf_op jit(solution)/shard_map/ppermute | solution.py:595
  1148.9 35.8 %all-to-all-start.9 = ((f32[32,1,256]{2,1,0:T(1,128)}), f32[32,1,256]{2,1,0:T(1,128)}, u32[]{:S(2)}, u32[]{:S(2)}) async-start(f32[32,1,256]{2,1,0:T(1,128)} %bitcast.404), calls=%async_computation.13 | async-start | bytes 65536 | tf_op jit(solution)/shard_map/all_to_all | solution.py:1095
  1154.2 41.7 %collective-permute-start.178 = (bf16[256,288]{1,0:T(8,128)(2,1)}, bf16[256,288]{1,0:T(8,128)(2,1)}, u32[]{:S(2)}, u32[]{:S(2)}) collective-permute-start(bf16[256,288]{1,0:T(8,128)(2,1)} %add_convert_fusion), channel_id=1, source_target_pairs={{0,1},{1,0},{2,3},{3,2},{4,5},{5,4},{6,7},{7,6},{8,9},{9,8},{10,11... | collective-permute-start | bytes 442376 | tf_op jit(solution)/shard_map/ppermute | solution.py:1024
  (363 other events, 3273.8 us)
Sparse Core Ops, SparseCore 0:
  15.2 57.0 all-gather.7
  352.7 55.9 all-gather.15
  410.9 58.2 all-gather.13
  470.6 38.3 all-gather.17
Sparse Core Ops, SparseCore 1:
  200.4 40.2 all-gather.9
  261.2 79.0 all-gather.11
  535.0 76.8 all-gather.19
  734.7 75.9 reduce-scatter.4
  824.1 81.7 reduce-scatter.6
  908.1 77.0 reduce-scatter.8
  999.2 37.5 reduce-scatter.10

commit v6 on v4

--- a/solution.py
+++ b/solution.py
@@ -72,6 +72,11 @@
 
 def after(x, point):
     return lax.optimization_barrier((x, point))[0]
+
+
+def following(x, *points):
+    zero = sum(jnp.minimum(jnp.abs(p.reshape(-1)[0].astype(f32)), 0.0) for p in points)
+    return x + zero.astype(x.dtype)
 
 
 def pick(x, dim, index):
@@ -842,10 +847,10 @@
         out_own = [None] * LAYERS
         ffn_own = [None] * LAYERS
         shares = [None] * LAYERS
-        mix_own[0] = spread_first(after(blocks[0][0], hidden_rows))
+        mix_own[0] = spread_first(blocks[0][0])
         out_cols = HD + width
         hidden_all = gather_rows(hidden_rows)
-        swapped = [[group_swap(x) for x in after(blocks[0][1:], hidden_all)]]
+        swapped = [[group_swap(following(x, mix_own[0])) for x in blocks[0][1:]]]
         for layer in range(1, LAYERS):
             both = group_swap(jnp.concatenate(blocks[layer][:2], axis=2))
             swapped.append([both[:, :, -out_cols:], group_swap(blocks[layer][2])])

time: 1250 us -> 1270 us (1.016)
  local copies, waits for them, and re-layouts: 222 us -> 237 us
  other arithmetic: 143 us -> 156 us
    all_to_all x8, waiting for transfers between devices: 27 us -> 13.3 us  [group_swap(): return lax.all_to_all(blocks, group_axes, 0, 0, tiled=True)]
    ppermute x3, waiting for transfers between devices: 20 us -> 33.5 us  [gather_lanes(): got = lax.ppermute(x, axis, SWAP)]
    unnamed x399 -> x416, local copies, waits for them, and re-layouts: 71.4 us -> 73.4 us
  transfers between devices with their start and end apart: 207 -> 207, of which waited for: 104 -> 104; matrix products, arithmetic and copies ran while one was open for 32% -> 34% of each run, Pallas kernels for 7% -> 7%
where the time goes in v6:
time: 1270 us; the launch traced here: 1250 us
  waiting for transfers between devices  372 us (29%)
  starting transfers between devices  299 us (24%)
  local copies, waits for them, and re-layouts  237 us (19%)
  other arithmetic  156 us (12%)
  Pallas kernels  86 us (7%)
  matrix products  81.9 us (6%)
  between operations  19.8 us (2%)
    ppermute x72, waiting for transfers between devices, gather_rows(): got = lax.ppermute(held, axis, SWAP)  125 us
    ppermute x72, waiting for transfers between devices, scatter_product(): got = lax.ppermute(pick(piece, dim, 1 - index).astype(bf16), axis, SWAP)  116 us
    ppermute x72, starting transfers between devices, gather_rows(): got = lax.ppermute(held, axis, SWAP)  91.6 us
    ppermute x72, starting transfers between devices, scatter_product(): got = lax.ppermute(pick(piece, dim, 1 - index).astype(bf16), axis, SWAP)  91.4 us
    unnamed x416, local copies, waits for them, and re-layouts  73.4 us
    pallas_call x8, Pallas kernels, call_whole(): pl.pallas_call(kernel, grid=(1,), in_specs=[pl.BlockSpec(memory_space=plt...  66.1 us
    dot_general x8, matrix products, matmul(): return jnp.dot(left_op, right_op, preferred_element_type=f32)  41.6 us
    dot_general x16, matrix products, matmul_nt(): lax.dot_general(left_op, right_op, (((1,), (1,)), ((), ())), preferred_el...  40.3 us
  transfers between devices with their start and end apart: 207, of which 104 were waited for; matrix products, arithmetic and copies ran while one was open for 34% of the time, Pallas kernels for 7%

profile of v6, /device:TPU:0, one launch (start us, length us, event | category | flops | bytes accessed | tf_op | source)
XLA Modules:
  0.0 1251.5 jit_solution(17871563378470729697)
XLA Ops:
  52.6 11.3 collective-permute-done.1
  69.9 22.1 %collective-permute-done.2 = bf16[2,2,1024]{2,1,0:T(2,128)(2,1)S(1)} collective-permute-done((bf16[2,2,1024]{2,1,0:T(2,128)(2,1)S(1)}, bf16[2,2,1024]{2,1,0:T(2,128)(2,1)S(1)}, u32[]{:S(2)}, u32[]{:S(2)}) %collective-permute-start.2) | collective-permute-done | bytes 8224 | tf_op jit(solution)/shard_map/ppermute | solution.py:638
  123.2 17.5 %collective-permute-done.11 = bf16[1,1,2,48,768]{4,3,2,1,0:T(8,128)(2,1)S(1)} collective-permute-done((bf16[1,1,2,48,768]{4,3,2,1,0:T(8,128)(2,1)S(1)}, bf16[1,1,2,48,768]{4,3,2,1,0:T(8,128)(2,1)S(1)}, u32[]{:S(2)}, u32[]{:S(2)}) %collective-permute-start.11) | collective-permute-done | bytes 147488 | tf_op jit(solution)/shard_map/ppermute | solution.py:565
  190.4 9.6 fusion.235.mixed
  200.0 8.6 shard_map.204
  281.2 7.8 collective-permute-done.29
  295.1 20.4 %all-gather.12.cloned.1.call-done = bf16[8,256,768]{2,1,0:T(8,128)(2,1)} async-done(((bf16[4,256,768]{2,1,0:T(8,128)(2,1)}), bf16[8,256,768]{2,1,0:T(8,128)(2,1)}) %all-gather.12.cloned.1.call-update) | async-done | bytes 3145744 | tf_op jit(solution)/shard_map/all_gather | solution.py:622
  337.7 6.8 collective-permute-done.35
  369.3 9.1 collective-permute-done.44
  406.8 21.4 %all-gather.16.cloned.1.call-done = bf16[2048,816]{0,1:T(8,128)(2,1)} async-done(((bf16[128,816]{0,1:T(8,128)(2,1)}), bf16[2048,816]{0,1:T(8,128)(2,1)}) %all-gather.16.cloned.1.call-update) | async-done | bytes 3342352 | tf_op jit(solution)/shard_map/all_gather | solution.py:825
  438.0 10.6 fusion.229.mixed
  448.6 8.5 shard_map.206
  509.7 10.7 collective-permute-done.55
  521.7 6.7 collective-permute-done.61
  562.4 11.5 collective-permute-done.71
  714.7 16.0 %shard_map.210 = (bf16[768,512]{1,0:T(8,128)(2,1)}, bf16[768,384]{1,0:T(8,128)(2,1)}, bf16[768,128]{1,0:T(8,128)(2,1)}, f32[8,192]{1,0:T(8,128)}, f32[8,512]{1,0:T(8,128)}, /*index=5*/f32[8,128]{1,0:T(8,128)}) custom-call(s32[1]{0:T(128)} %bitcast.65.core_ref, f32[768,1408]{1,0:T(8,128)} %fusion.229.mixed, f32[8,192]{1,0:T(8,128)} %get-tuple-element.376.taps, ...), custom_call_target="tpu_custom_call" | custom-call | flops 13271040000 | bytes 6291456 | tf_op jit(solution)/shard_map/pallas_call | solution.py:413
  840.0 7.0 collective-permute-done.130
  912.0 8.7 collective-permute-done.150
  968.4 16.0 %shard_map.216 = (bf16[768,512]{1,0:T(8,128)(2,1)}, bf16[768,384]{1,0:T(8,128)(2,1)}, bf16[768,128]{1,0:T(8,128)(2,1)}, f32[8,192]{1,0:T(8,128)}, f32[8,512]{1,0:T(8,128)}, /*index=5*/f32[8,128]{1,0:T(8,128)}) custom-call(s32[1]{0:T(128)} %bitcast.65.core_ref, f32[768,1408]{1,0:T(8,128)} %fusion.235.mixed, f32[8,192]{1,0:T(8,128)} %get-tuple-element.377.taps, ...), custom_call_target="tpu_custom_call" | custom-call | flops 13271040000 | bytes 6291456 | tf_op jit(solution)/shard_map/pallas_call | solution.py:413
  1003.5 6.6 convolution_convert_fusion.2
  1020.0 7.1 collective-permute-start.177
  1078.7 9.3 collective-permute-done.172
  1161.8 6.6 all-to-all-start.15
  1173.8 14.8 %collective-permute-done.164 = bf16[2,2,48,2048]{3,2,0,1:T(8,128)(2,1)S(1)} collective-permute-done((bf16[2,2,48,2048]{3,2,0,1:T(8,128)(2,1)S(1)}, bf16[2,2,48,2048]{3,2,0,1:T(8,128)(2,1)S(1)}, u32[]{:S(2)}, u32[]{:S(2)}) %collective-permute-start.164) | collective-permute-done | bytes 786464 | tf_op jit(solution)/shard_map/ppermute | solution.py:747
  (1480 shorter events, 957.1 us)
Async XLA Ops:
  7.2 173.2 %all-gather.8.cloned.1.call-start = ((), (), s32[]{:S(2)}) async-start(), calls=%async_computation.20 | async-start | bytes 3551232 | tf_op jit(solution)/shard_map/all_gather | solution.py:825
  7.2 43.2 %collective-permute-start = (bf16[2,2,256]{2,1,0:T(2,128)(2,1)}, bf16[2,2,256]{2,1,0:T(2,128)(2,1)S(1)}, u32[]{:S(2)}, u32[]{:S(2)}) collective-permute-start(bf16[2,2,256]{2,1,0:T(2,128)(2,1)} %param.15), channel_id=1, source_target_pairs={{0,4},{4,0},{1,5},{5,1},{2,6},{6,2},{3,7},{7,3},{8,12},{12,8},{9,1... | collective-permute-start | bytes 6152 | tf_op jit(solution)/shard_map/ppermute | solution.py:638
  19.3 91.8 %all-to-all-start = ((bf16[8,256,512]{2,1,0:T(8,128)(2,1)}), bf16[8,256,512]{2,1,0:T(8,128)(2,1)S(1)}, u32[]{:S(2)}, u32[]{:S(2)}) async-start(bf16[8,256,512]{2,1,0:T(8,128)(2,1)} %maximum_maximum_fusion), calls=%async_computation | async-start | bytes 4194304 | tf_op jit(solution)/shard_map/all_to_all | solution.py:625
  111.1 47.7 %all-to-all-start.2 = ((bf16[4,256,832]{1,2,0:T(8,128)(2,1)}), bf16[4,256,832]{1,2,0:T(8,128)(2,1)}, u32[]{:S(2)}, u32[]{:S(2)}) async-start(bf16[4,256,832]{1,2,0:T(8,128)(2,1)} %constant_dynamic-update-slice_fusion), calls=%async_computation.2 | async-start | bytes 3407872 | tf_op jit(solution)/shard_map/all_to_all | solution.py:619
  177.1 41.4 %all-gather.10.cloned.1.call-start = ((), (), s32[]{:S(2)}) async-start(), calls=%async_computation.21 | async-start | bytes 1966080 | tf_op jit(solution)/shard_map/all_gather | solution.py:622
  214.3 101.2 %all-gather.12.cloned.1.call-start = ((), (), s32[]{:S(2)}) async-start(), calls=%async_computation.22 | async-start | bytes 4718592 | tf_op jit(solution)/shard_map/all_gather | solution.py:622
  237.2 169.6 %all-gather.14.cloned.1.call-start = ((), (), s32[]{:S(2)}) async-start(), calls=%async_computation.23 | async-start | bytes 3145728 | tf_op jit(solution)/shard_map/all_gather | solution.py:622
  292.6 135.6 %all-gather.16.cloned.1.call-start = ((), (), s32[]{:S(2)}) async-start(), calls=%async_computation.24 | async-start | bytes 3551232 | tf_op jit(solution)/shard_map/all_gather | solution.py:825
  325.1 36.9 %collective-permute-start.84 = (bf16[48,2048]{1,0:T(8,128)(2,1)}, bf16[48,2048]{1,0:T(8,128)(2,1)}, u32[]{:S(2)}, u32[]{:S(2)}) collective-permute-start(bf16[48,2048]{1,0:T(8,128)(2,1)} %dynamic-slice_bitcast_fusion.2), channel_id=1, source_target_pairs={{0,16},{17,1},{2,18},{19,3},{4,20},{21,5},{6,22},{23,7},{8,24},{25... | collective-permute-start | bytes 589832 | tf_op jit(solution)/shard_map/ppermute | solution.py:726
  327.9 145.9 %all-gather.18.cloned.1.call-start = ((), (), s32[]{:S(2)}) async-start(), calls=%async_computation.25 | async-start | bytes 1966080 | tf_op jit(solution)/shard_map/all_gather | solution.py:622
  473.5 123.9 %all-gather.20.cloned.1.call-start = ((), (), s32[]{:S(2)}) async-start(), calls=%async_computation.26 | async-start | bytes 4718592 | tf_op jit(solution)/shard_map/all_gather | solution.py:622
  493.1 322.6 %reduce-scatter.5.cloned.1.call-start = ((), (), s32[]{:S(2)}) async-start(), calls=%async_computation.27 | async-start | bytes 4718592 | tf_op jit(solution)/shard_map/reduce_scatter | solution.py:628
  498.5 75.4 %collective-permute-start.89 = (bf16[1,2,1,48,640]{4,3,2,1,0:T(8,128)(2,1)S(1)}, bf16[1,2,1,48,640]{4,3,2,1,0:T(8,128)(2,1)S(1)}, u32[]{:S(2)}, u32[]{:S(2)}) collective-permute-start(bf16[1,2,1,48,640]{4,3,2,1,0:T(8,128)(2,1)S(1)} %maximum_select_fusion.82), channel_id=1, source_target_pairs={{0,2},{2,0},{1,3},{3,1},{4,6},{6,4},{5,7},{7,5},{8,10},{10,8},{9,1... | collective-permute-start | bytes 368648 | tf_op jit(solution)/shard_map/ppermute | solution.py:565
  501.9 81.4 %collective-permute-start.92 = (bf16[1,1,2,48,768]{4,3,2,1,0:T(8,128)(2,1)S(1)}, bf16[1,1,2,48,768]{4,3,2,1,0:T(8,128)(2,1)S(1)}, u32[]{:S(2)}, u32[]{:S(2)}) collective-permute-start(bf16[1,1,2,48,768]{4,3,2,1,0:T(8,128)(2,1)S(1)} %maximum_select_fusion.61), channel_id=1, source_target_pairs={{0,8},{8,0},{1,9},{9,1},{2,10},{10,2},{3,11},{11,3},{4,12},{12,4},... | collective-permute-start | bytes 442376 | tf_op jit(solution)/shard_map/ppermute | solution.py:565
  506.8 78.1 %collective-permute-start.87 = (bf16[2,2,1,48,640]{4,3,0,2,1:T(8,128)(2,1)S(1)}, bf16[2,2,1,48,640]{4,3,0,2,1:T(8,128)(2,1)S(1)}, u32[]{:S(2)}, u32[]{:S(2)}) collective-permute-start(bf16[2,2,1,48,640]{4,3,0,2,1:T(8,128)(2,1)S(1)} %maximum_select_fusion.44), channel_id=1, source_target_pairs={{0,2},{2,0},{1,3},{3,1},{4,6},{6,4},{5,7},{7,5},{8,10},{10,8},{9,1... | collective-permute-start | bytes 737288 | tf_op jit(solution)/shard_map/ppermute | solution.py:565
  699.8 194.1 %reduce-scatter.7.cloned.1.call-start = ((), (), s32[]{:S(2)}) async-start(), calls=%async_computation.28 | async-start | bytes 5111808 | tf_op jit(solution)/shard_map/reduce_scatter | solution.py:628
  782.9 216.1 %reduce-scatter.9.cloned.1.call-start = ((), (), s32[]{:S(2)}) async-start(), calls=%async_computation.29 | async-start | bytes 4718592 | tf_op jit(solution)/shard_map/reduce_scatter | solution.py:628
  947.2 62.9 %reduce-scatter.11.cloned.1.call-start = ((), (), s32[]{:S(2)}) async-start(), calls=%async_computation.30 | async-start | bytes 1966080 | tf_op jit(solution)/shard_map/reduce_scatter | solution.py:628
  961.2 37.8 %all-to-all-start.14 = ((bf16[16,48,288]{2,1,0:T(8,128)(2,1)}), bf16[16,48,288]{2,1,0:T(8,128)(2,1)}, u32[]{:S(2)}, u32[]{:S(2)}) async-start(bf16[16,48,288]{2,1,0:T(8,128)(2,1)} %bitcast.1085), calls=%async_computation.18 | async-start | bytes 1179648 | tf_op jit(solution)/shard_map/all_to_all | solution.py:735
  1020.0 85.5 %collective-permute-start.177 = (bf16[256,288]{1,0:T(8,128)(2,1)}, bf16[256,288]{1,0:T(8,128)(2,1)}, u32[]{:S(2)}, u32[]{:S(2)}) collective-permute-start(bf16[256,288]{1,0:T(8,128)(2,1)} %shard_map.222), channel_id=1, source_target_pairs={{0,16},{16,0},{1,17},{17,1},{2,18},{18,2},{3,19},{19,3},{4,20},{20... | collective-permute-start | bytes 442376 | tf_op jit(solution)/shard_map/ppermute | solution.py:1014
  1028.2 62.9 %all-to-all-start.12 = ((bf16[4,256,832]{1,2,0:T(8,128)(2,1)}), bf16[4,256,832]{1,2,0:T(8,128)(2,1)}, u32[]{:S(2)}, u32[]{:S(2)}) async-start(bf16[4,256,832]{1,2,0:T(8,128)(2,1)} %reduce-scatter.7.cloned.1.call-done), calls=%async_computation.16 | async-start | bytes 3407872 | tf_op jit(solution)/shard_map/all_to_all | solution.py:619
  1055.8 48.2 %collective-permute-start.170 = (bf16[4,256,512]{1,2,0:T(8,128)(2,1)}, bf16[4,256,512]{1,2,0:T(8,128)(2,1)}, u32[]{:S(2)}, u32[]{:S(2)}) collective-permute-start(bf16[4,256,512]{1,2,0:T(8,128)(2,1)} %bitcast.1125), channel_id=1, source_target_pairs={{0,16},{16,0},{1,17},{17,1},{2,18},{18,2},{3,19},{19,3},{4,20},{20... | collective-permute-start | bytes 3145736 | tf_op jit(solution)/shard_map/ppermute | solution.py:633
  1088.7 49.7 %collective-permute-start.173 = (bf16[48,1152]{1,0:T(8,128)(2,1)}, bf16[48,1152]{1,0:T(8,128)(2,1)}, u32[]{:S(2)}, u32[]{:S(2)}) collective-permute-start(bf16[48,1152]{1,0:T(8,128)(2,1)} %fusion.177), channel_id=1, source_target_pairs={{0,4},{4,0},{1,5},{5,1},{2,6},{6,2},{3,7},{7,3},{8,12},{12,8},{9,1... | collective-permute-start | bytes 331784 | tf_op jit(solution)/shard_map/ppermute | solution.py:595
  1112.6 41.6 %collective-permute-start.178 = (bf16[256,288]{1,0:T(8,128)(2,1)}, bf16[256,288]{1,0:T(8,128)(2,1)}, u32[]{:S(2)}, u32[]{:S(2)}) collective-permute-start(bf16[256,288]{1,0:T(8,128)(2,1)} %add_convert_fusion), channel_id=1, source_target_pairs={{0,1},{1,0},{2,3},{3,2},{4,5},{5,4},{6,7},{7,6},{8,9},{9,8},{10,11... | collective-permute-start | bytes 442376 | tf_op jit(solution)/shard_map/ppermute | solution.py:1020
  (367 other events, 3479.2 us)
Sparse Core Ops, SparseCore 0:
  14.4 80.7 all-gather.7
  180.5 38.0 all-gather.9
  237.4 78.0 all-gather.11
  317.4 59.8 all-gather.13
  379.9 48.2 all-gather.15
  429.6 37.4 all-gather.17
  493.2 77.8 all-gather.19
  686.3 83.2 reduce-scatter.4
  783.0 89.3 reduce-scatter.6
  874.5 76.9 reduce-scatter.8
  955.7 44.0 reduce-scatter.10
